TPU v7x, 512 devices: a whole 4x8x8 slice. The times are simulated.
512 devices in a mesh: cube: 4 (over y_hi), row: 16 (over z, core), col: 8 (over y_lo, x).
Axes of the slice: x: 4, y: 8 (y_hi: 4, y_lo: 2; y = y_hi * 2 + y_lo), z: 8, core: 2. Of those that a mesh axis runs over, the one named last changes fastest.
Arguments:
- leaf_front: float32 [16384, 2048], P(('cube', 'row'), 'col'), may hold values from -4 to 4
- leaf_panel: bfloat16 [16384, 1024], P(('cube', 'row'), 'col'), may hold values from -0.625 to 0.625
- leaf_inverse: bfloat16 [4, 1024, 1024], P('cube', 'row', 'col'), as said below
- leaf_fill: int32 [4, 16], replicated, may hold values 0 or 1
- mid_front: float32 [16384, 4096], P(('cube', 'row'), 'col'), may hold values from -4 to 4
- mid_panel: bfloat16 [16384, 1024], P(('cube', 'row'), 'col'), may hold values from -0.625 to 0.625
- mid_inverse: bfloat16 [2, 1024, 1024], P(None, 'row', 'col'), as said below
- mid_fill: int32 [2, 32], replicated, may hold values 0 or 1
- root_front: float32 [16384, 8192], P(('cube', 'row'), 'col'), may hold values from -4 to 4
- root_panel: bfloat16 [16384, 1024], P(('cube', 'row'), 'col'), may hold values from -0.625 to 0.625
- root_inverse: bfloat16 [1024, 1024], P('row', 'col'), as said below
- root_fill: int32 [64], replicated, may hold values 0 or 1
- leaf_map: int32 [4, 16], replicated, may hold values from 0 to 31, as said below
- mid_map: int32 [2, 32], replicated, may hold values from 0 to 63, as said below
Outputs:
- leaf_factor: bfloat16 [16384, 1024], P(('cube', 'row'), 'col')
- mid_factor: bfloat16 [16384, 1024], P(('cube', 'row'), 'col')
- root_factor: bfloat16 [16384, 1024], P(('cube', 'row'), 'col')
- root_update: float32 [16384, 8192], P(('cube', 'row'), 'col')
Inputs may be any that keep to these rules, and one draw needn't show every extreme that they name: The blocks of one leaf front go to distinct blocks of its parent; for every i with i % 16 < 8, leaf_map[x, i] % 16 equals i % 16. The blocks of one middle front go to distinct root blocks; for every i with i % 16 < 8, mid_map[x, i] % 16 equals i % 16. `leaf_inverse`: each matrix is lower triangular with its diagonal between 0.5 and 2. `mid_inverse`: lower triangular with its diagonal between 0.5 and 2. `root_inverse`: lower triangular with its diagonal between 0.5 and 2.
All inputs are finite; a program needn't handle non-finite values.
Results may differ from a plain program's by a relative error of at most 0.015.
Values may be sent and summed in bfloat16 or wider, within the bound.
No kernel may reach another device: no remote copies, remote signals or barrier semaphores. Data moves between devices by JAX's collectives and lax.ppermute only.
A program may use at most 64 MiB of HBM per device.

v0:
```python
import jax
import jax.numpy as jnp
from jax import lax
from jax.sharding import PartitionSpec as P

BLK = 256


def spread(value, axis, source):
    kept = jnp.where(lax.axis_index(axis) == source, value, 0).astype(value.dtype)
    return lax.psum(kept, axis)


def from_partner(value, axis, distance):
    mask = 2**distance
    pairs = [(source, source ^ mask) for source in range(lax.axis_size(axis))]
    return lax.ppermute(value, axis, pairs)


def factor_rows(panel, inverse, fill_rows):
    partial_value = lax.dot_general(
        panel,
        lax.all_gather(inverse, "row", axis=0, tiled=True),
        (((1,), (1,)), ((), ())),
        preferred_element_type=jnp.float32,
    )
    summed = lax.psum(partial_value.astype(jnp.bfloat16), "col").astype(jnp.float32)
    blocks = summed.reshape(fill_rows.shape[0], BLK, summed.shape[1])
    blocks = blocks * fill_rows.astype(jnp.float32)[:, None, None]
    return blocks.reshape(summed.shape).astype(jnp.bfloat16)


def column_owner_rows(factor, column_index):
    return spread(factor, "row", column_index)


def cube_collect(owned):
    return lax.all_gather(owned[None], "cube", axis=0, tiled=True)


def map_entries(table, front_number, period, offset):
    line = lax.dynamic_index_in_dim(table, front_number, 0, keepdims=False)
    return lax.dynamic_index_in_dim(line.reshape(-1, period), offset, 1, keepdims=False)


def lookup(line, blocks):
    hits = blocks[:, None] == jnp.arange(line.shape[0], dtype=jnp.int32)[None, :]
    return jnp.sum(jnp.where(hits, line[None, :], 0), axis=1)


def schur_term(factor, groups):
    product = jnp.einsum("rk,gnk->rgn", factor, groups, preferred_element_type=jnp.float32)
    height, count, width = product.shape
    product = product.reshape(height, count, width // BLK, BLK).transpose(0, 2, 1, 3)
    return product.reshape(height, count * width)


def row_folder(line, wanted, period, offset, slots, carry, piece):
    count = piece.shape[0] // BLK
    index = jnp.arange(count, dtype=jnp.int32)
    front_block = period * (index % slots) + offset + index // slots
    parents = lookup(line, front_block)
    select = (parents[:, None] == wanted[None, :]).astype(jnp.bfloat16)
    tiles = piece.reshape(count, BLK, piece.shape[1])
    moved = jnp.einsum("au,axk->uxk", select, tiles, preferred_element_type=jnp.float32)
    return moved.reshape(carry.shape)


def place_columns(tiles, column_parent, column_wanted):
    column_select = (column_parent[:, None] == column_wanted[None, :]).astype(jnp.bfloat16)
    height = tiles.shape[0]
    blocks = tiles.reshape(height, column_parent.shape[0], BLK)
    placed = jnp.einsum("hbx,bv->hvx", blocks, column_select, preferred_element_type=jnp.float32)
    return placed.reshape(height, column_wanted.shape[0] * BLK)


def local(
    leaf_front,
    leaf_panel,
    leaf_inverse,
    leaf_fill,
    mid_front,
    mid_panel,
    mid_inverse,
    mid_fill,
    root_front,
    root_panel,
    root_inverse,
    root_fill,
    leaf_map,
    mid_map,
):
    cube_index = lax.axis_index("cube")
    row_index = lax.axis_index("row")
    column_index = lax.axis_index("col")
    n_row = lax.axis_size("row")
    cube_bit = cube_index % 2
    pair_index = cube_index // 2
    slots = leaf_panel.shape[0] // BLK
    width = leaf_panel.shape[1]
    slot_range = jnp.arange(slots, dtype=jnp.int32)
    leaf_fill_rows = map_entries(leaf_fill, cube_index, n_row, row_index)
    leaf_rows = factor_rows(leaf_panel, leaf_inverse[0], leaf_fill_rows)
    leaf_columns = column_owner_rows(leaf_rows, column_index)
    leaf_schur = leaf_front - schur_term(leaf_rows, leaf_columns[None])
    leaf_update = leaf_schur.astype(jnp.bfloat16)
    mid_wanted_columns = n_row * jnp.arange(2 * slots, dtype=jnp.int32) + column_index
    leaf_line = lax.dynamic_index_in_dim(leaf_map, cube_index, 0, keepdims=False)
    leaf_wanted = jnp.concatenate(
        [2 * n_row * slot_range + row_index, 2 * n_row * slot_range + n_row + row_index]
    )
    leaf_init = jnp.zeros((2 * slots * BLK, leaf_update.shape[1]), jnp.float32)
    leaf_placed = row_folder(
        leaf_line,
        leaf_wanted,
        n_row,
        0,
        slots,
        leaf_init,
        lax.all_gather(leaf_update, "row", axis=0, tiled=True),
    )
    halves = leaf_placed.reshape(2, slots * BLK, leaf_update.shape[1])
    own_half = lax.dynamic_index_in_dim(halves, cube_bit, 0, keepdims=False)
    other_half = lax.dynamic_index_in_dim(halves, 1 - cube_bit, 0, keepdims=False)
    received = from_partner(other_half.astype(jnp.bfloat16), "cube", 0)
    own_columns = map_entries(leaf_map, cube_index, n_row, column_index)
    partner_columns = map_entries(leaf_map, cube_index + 1 - 2 * cube_bit, n_row, column_index)
    mid_assembled = place_columns(own_half.astype(jnp.bfloat16), own_columns, mid_wanted_columns)
    mid_assembled = mid_assembled + place_columns(received, partner_columns, mid_wanted_columns)
    mid_fill_rows = map_entries(mid_fill, pair_index, 2 * n_row, n_row * cube_bit + row_index)
    mid_weights = lax.dynamic_index_in_dim(mid_inverse, pair_index, 0, keepdims=False)
    mid_rows = factor_rows(mid_panel, mid_weights, mid_fill_rows)
    mid_own = column_owner_rows(mid_rows, column_index)
    mid_groups = lax.dynamic_slice_in_dim(cube_collect(mid_own), 2 * pair_index, 2, 0)
    mid_schur = mid_front + mid_assembled - schur_term(mid_rows, mid_groups)
    mid_update = mid_schur.astype(jnp.bfloat16)
    root_fill_rows = map_entries(root_fill[None], 0, 4 * n_row, n_row * cube_index + row_index)
    root_rows = factor_rows(root_panel, root_inverse, root_fill_rows)
    root_own = column_owner_rows(root_rows, column_index)
    root_groups = cube_collect(root_own)
    root_wanted_columns = n_row * jnp.arange(4 * slots, dtype=jnp.int32) + column_index
    mid_line = lax.dynamic_index_in_dim(mid_map, pair_index, 0, keepdims=False)
    root_wanted = jnp.concatenate(
        [4 * n_row * slot_range + n_row * owner + row_index for owner in range(4)]
    )
    root_init = jnp.zeros((4 * slots * BLK, mid_update.shape[1]), jnp.float32)
    root_placed = row_folder(
        mid_line,
        root_wanted,
        2 * n_row,
        n_row * cube_bit,
        slots,
        root_init,
        lax.all_gather(mid_update, "row", axis=0, tiled=True),
    )
    outgoing = root_placed.reshape(4, slots * BLK, mid_update.shape[1]).astype(jnp.bfloat16)
    arrived = lax.all_to_all(outgoing, "cube", split_axis=0, concat_axis=0, tiled=True)
    first_mid = (arrived[0].astype(jnp.float32) + arrived[1].astype(jnp.float32)).astype(
        jnp.bfloat16
    )
    second_mid = (arrived[2].astype(jnp.float32) + arrived[3].astype(jnp.float32)).astype(
        jnp.bfloat16
    )
    root_assembled = place_columns(
        first_mid, map_entries(mid_map, 0, n_row, column_index), root_wanted_columns
    )
    root_assembled = root_assembled + place_columns(
        second_mid, map_entries(mid_map, 1, n_row, column_index), root_wanted_columns
    )
    root_update = root_front + root_assembled - schur_term(root_rows, root_groups)
    leaf_factor = lax.dynamic_slice_in_dim(leaf_rows, column_index * width, width, 1)
    mid_factor = lax.dynamic_slice_in_dim(mid_rows, column_index * width, width, 1)
    root_factor = lax.dynamic_slice_in_dim(root_rows, column_index * width, width, 1)
    return (leaf_factor, mid_factor, root_factor, root_update)


def solution(mesh):
    in_specs = (
        P(("cube", "row"), "col"),
        P(("cube", "row"), "col"),
        P("cube", "row", "col"),
        P(),
        P(("cube", "row"), "col"),
        P(("cube", "row"), "col"),
        P(None, "row", "col"),
        P(),
        P(("cube", "row"), "col"),
        P(("cube", "row"), "col"),
        P("row", "col"),
        P(),
        P(),
        P(),
    )
    out_specs = (
        P(("cube", "row"), "col"),
        P(("cube", "row"), "col"),
        P(("cube", "row"), "col"),
        P(("cube", "row"), "col"),
    )
    return jax.shard_map(local, mesh=mesh, in_specs=in_specs, out_specs=out_specs, check_vma=False)
```

profile of v0, /device:TPU:1, one launch (start us, length us, event | category | flops | bytes accessed | tf_op | source)
XLA Modules:
  0.0 514.2 jit_solution(2238683496948807454)
XLA Ops:
  7.3 0.7 constant_dynamic-slice_fusion.7
  8.0 25.2 %all-gather.1 = bf16[1,1024,128]{2,1,0:T(8,128)(2,1)S(1)} all-gather(bf16[1,64,128]{2,1,0:T(8,128)(2,1)S(1)} %constant_dynamic-slice_fusion.7), channel_id=3, replica_groups=mesh['cube'=4,'row'=16,'col'=8] {'row'}, dimensions={1}, use_global_device_ids=true | all-gather | bytes 278528 | tf_op jit(solution)/shard_map/all_gather | solution.py:23
  33.2 15.4 %all_gather.23 = bf16[1024,128]{1,0:T(8,128)(2,1)S(1)} all-gather(bf16[64,128]{1,0:T(8,128)(2,1)} %param.24), channel_id=1, replica_groups=mesh['cube'=4,'row'=16,'col'=8] {'row'}, dimensions={0}, use_global_device_ids=true | all-gather | bytes 278528 | tf_op jit(solution)/shard_map/all_gather | solution.py:23
  48.6 16.7 %all-gather = bf16[1,1024,128]{2,1,0:T(8,128)(2,1)S(1)} all-gather(bf16[1,64,128]{2,1,0:T(8,128)(2,1)} %param.16), channel_id=2, replica_groups=mesh['cube'=4,'row'=16,'col'=8] {'row'}, dimensions={1}, use_global_device_ids=true | all-gather | bytes 278528 | tf_op jit(solution)/shard_map/all_gather | solution.py:23
  65.3 1.1 fusion.7
  66.4 1.9 convolution_convert_fusion
  68.3 1.1 convolution_convert_fusion.2
  72.1 1.3 dynamic_slice.67
  74.0 79.6 %all-reduce.7.cloned.1.call-done = (bf16[256,1024]{1,0:T(8,128)(2,1)}, bf16[256,1024]{1,0:T(8,128)(2,1)}, bf16[256,1024]{1,0:T(8,128)(2,1)}) async-done(((bf16[256,1024]{1,0:T(8,128)(2,1)}, bf16[256,1024]{1,0:T(8,128)(2,1)}, bf16[256,1024]{1,0:T(8,128)(2,1)}), (bf16[256,1024]{1,0:T(8,128)(2,1)}, bf16[256,1024]{1,0:T(8,128)(2,1)}, bf16[256,1024]{1,0:T(8,128)(2,1)})) %all-reduce.7.cloned.1.call-update) | async-done | bytes 1572880 | tf_op jit(solution)/shard_map/psum | solution.py:27
  153.6 2.0 broadcast_select_fusion
  155.6 2.7 select_bitcast_fusion
  158.4 123.6 %all-reduce.5.cloned.1.call-done = (bf16[1,256,1024]{2,1,0:T(8,128)(2,1)}, bf16[1,256,1024]{2,1,0:T(8,128)(2,1)}, bf16[256,1024]{1,0:T(8,128)(2,1)}) async-done(((bf16[1,256,1024]{2,1,0:T(8,128)(2,1)}, bf16[1,256,1024]{2,1,0:T(8,128)(2,1)}, bf16[256,1024]{1,0:T(8,128)(2,1)}), (bf16[1,256,1024]{2,1,0:T(8,128)(2,1)}, bf16[1,256,1024]{2,1,0:T(8,128)(2,1)}, ...) | async-done | bytes 1572880 | tf_op jit(solution)/shard_map/psum | solution.py:11
  282.0 2.0 fusion.9
  284.7 0.6 fusion.34
  285.4 1.3 compare_convert_fusion
  286.8 41.6 %all-gather.7.cloned.1.call-done = bf16[4096,256]{1,0:T(8,128)(2,1)} async-done(((bf16[256,256]{1,0:T(8,128)(2,1)}), bf16[4096,256]{1,0:T(8,128)(2,1)}) %all-gather.7.cloned.1.call-update) | async-done | bytes 2097168 | tf_op jit(solution)/shard_map/all_gather | solution.py:120
  328.4 2.9 fusion.2
  331.8 4.2 collective-permute-start
  336.0 44.5 %all-gather.9.cloned.1.call-done = bf16[4,256,1024]{2,1,0:T(8,128)(2,1)} async-done(((bf16[1,256,1024]{2,1,0:T(8,128)(2,1)}), bf16[4,256,1024]{2,1,0:T(8,128)(2,1)}) %all-gather.9.cloned.1.call-update) | async-done | bytes 2097168 | tf_op jit(solution)/shard_map/all_gather | solution.py:38
  380.4 1.3 constant_dynamic-slice_fusion.1
  382.2 1.2 fusion.8
  384.0 46.1 %all-gather.11.cloned.1.call-done = bf16[4096,512]{1,0:T(8,128)(2,1)} async-done(((bf16[256,512]{1,0:T(8,128)(2,1)}), bf16[4096,512]{1,0:T(8,128)(2,1)}) %all-gather.11.cloned.1.call-update) | async-done | bytes 4194320 | tf_op jit(solution)/shard_map/all_gather | solution.py:154
  430.1 4.7 fusion.4
  434.9 1.2 copy.41
  436.0 6.5 %all-to-all-start = ((bf16[4,256,512]{2,1,0:T(8,128)(2,1)}), bf16[4,256,512]{2,1,0:T(8,128)(2,1)S(1)}, u32[]{:S(2)}, u32[]{:S(2)}) async-start(bf16[4,256,512]{2,1,0:T(8,128)(2,1)} %copy.41), calls=%async_computation | async-start | bytes 2097152 | tf_op jit(solution)/shard_map/all_to_all | solution.py:157
  442.9 0.7 constant_dynamic-slice_fusion.6
  443.5 0.6 constant_dynamic-slice_fusion.8
  444.2 0.6 constant_dynamic-slice_fusion.5
  444.8 41.9 %all-to-all-done = bf16[4,256,512]{2,1,0:T(8,128)(2,1)S(1)} async-done(((bf16[4,256,512]{2,1,0:T(8,128)(2,1)}), bf16[4,256,512]{2,1,0:T(8,128)(2,1)S(1)}, u32[]{:S(2)}, u32[]{:S(2)}) %all-to-all-start) | async-done | bytes 1048608 | tf_op jit(solution)/shard_map/all_to_all | solution.py:157
  488.5 0.6 convolution_add_fusion
  489.4 14.7 %all-gather.13.cloned.1.call-done = bf16[4,256,1024]{2,1,0:T(8,128)(2,1)} async-done(((bf16[1,256,1024]{2,1,0:T(8,128)(2,1)}), bf16[4,256,1024]{2,1,0:T(8,128)(2,1)}) %all-gather.13.cloned.1.call-update) | async-done | bytes 2097168 | tf_op jit(solution)/shard_map/all_gather | solution.py:38
  504.0 3.3 convolution_subtract_fusion
  (61 shorter events, 5.9 us)
Async XLA Ops:
  7.2 58.1 %copy-start = (bf16[256,128]{1,0:T(8,128)(2,1)S(1)}, bf16[256,128]{1,0:T(8,128)(2,1)}, u32[]{:S(2)}) copy-start(bf16[256,128]{1,0:T(8,128)(2,1)} %param.19) | copy-start | bytes 196612
  7.2 61.2 %copy-start.4 = (bf16[256,128]{1,0:T(8,128)(2,1)S(1)}, bf16[256,128]{1,0:T(8,128)(2,1)}, u32[]{:S(2)}) copy-start(bf16[256,128]{1,0:T(8,128)(2,1)} %param.15) | copy-start | bytes 196612
  7.2 146.4 %all-reduce.7.cloned.1.call-start = ((), (), s32[]{:S(2)}) async-start(), calls=%async_computation.6 | async-start | bytes 3145728 | tf_op jit(solution)/shard_map/psum | solution.py:27
  65.3 4.3 copy-start.7
  65.3 5.5 %copy-start.8 = (s32[64]{0:T(128)S(1)}, s32[64]{0:T(128)}, u32[]{:S(2)}) copy-start(s32[64]{0:T(128)} %param.25) | copy-start | bytes 772
  69.5 212.5 %all-reduce.5.cloned.1.call-start = ((), (), s32[]{:S(2)}) async-start(), calls=%async_computation.5 | async-start | bytes 3145728 | tf_op jit(solution)/shard_map/psum | solution.py:11
  155.6 126.4 %copy-start.3 = (f32[256,256]{1,0:T(8,128)S(1)}, f32[256,256]{1,0:T(8,128)}, u32[]{:S(2)}) copy-start(f32[256,256]{1,0:T(8,128)} %param.14) | copy-start | bytes 786436
  158.3 126.4 %copy-start.6 = (s32[4,16]{1,0:T(4,128)S(1)}, s32[4,16]{1,0:T(4,128)}, u32[]{:S(2)}) copy-start(s32[4,16]{1,0:T(4,128)} %param.26) | copy-start | bytes 772
  158.3 170.0 %all-gather.7.cloned.1.call-start = ((), (), s32[]{:S(2)}) async-start(), calls=%async_computation.1 | async-start | bytes 2228224 | tf_op jit(solution)/shard_map/all_gather | solution.py:120
  284.1 96.4 %all-gather.9.cloned.1.call-start = ((), (), s32[]{:S(2)}) async-start(), calls=%async_computation.2 | async-start | bytes 2621440 | tf_op jit(solution)/shard_map/all_gather | solution.py:38
  284.6 145.5 %all-gather.11.cloned.1.call-start = ((), (), s32[]{:S(2)}) async-start(), calls=%async_computation.3 | async-start | bytes 4456448 | tf_op jit(solution)/shard_map/all_gather | solution.py:154
  331.8 50.4 %copy-start.2 = (f32[256,512]{1,0:T(8,128)S(1)}, f32[256,512]{1,0:T(8,128)}, u32[]{:S(2)}) copy-start(f32[256,512]{1,0:T(8,128)} %param.18) | copy-start | bytes 1572868
  331.8 50.0 %collective-permute-start = (bf16[256,256]{1,0:T(8,128)(2,1)S(1)}, bf16[256,256]{1,0:T(8,128)(2,1)S(1)}, u32[]{:S(2)}, u32[]{:S(2)}) collective-permute-start(bf16[256,256]{1,0:T(8,128)(2,1)S(1)} %bitcast.75), channel_id=1, source_target_pairs={{0,128},{128,0},{256,384},{384,256},{1,129},{129,1},{257,385},{385... | collective-permute-start | bytes 393224 | tf_op jit(solution)/shard_map/ppermute | solution.py:17
  382.1 1.5 copy-start.5
  383.5 120.6 %all-gather.13.cloned.1.call-start = ((), (), s32[]{:S(2)}) async-start(), calls=%async_computation.4 | async-start | bytes 2621440 | tf_op jit(solution)/shard_map/all_gather | solution.py:38
  436.0 50.7 %all-to-all-start = ((bf16[4,256,512]{2,1,0:T(8,128)(2,1)}), bf16[4,256,512]{2,1,0:T(8,128)(2,1)S(1)}, u32[]{:S(2)}, u32[]{:S(2)}) async-start(bf16[4,256,512]{2,1,0:T(8,128)(2,1)} %copy.41), calls=%async_computation | async-start | bytes 2097152 | tf_op jit(solution)/shard_map/all_to_all | solution.py:157
  488.5 15.5 %copy-start.1 = (f32[256,1024]{1,0:T(8,128)S(1)}, f32[256,1024]{1,0:T(8,128)}, u32[]{:S(2)}) copy-start(f32[256,1024]{1,0:T(8,128)} %param.22) | copy-start | bytes 3145732
Sparse Core Ops, SparseCore 0:
  69.6 83.9 all-reduce.6
  158.5 123.4 all-reduce.4
  284.9 43.4 all-gather.6
  330.5 49.8 all-gather.8
  383.6 46.5 all-gather.10
  432.3 71.6 all-gather.12
where the time goes:
time: 515 us; the launch traced here: 514 us
  waiting for transfers between devices  393 us (76%)
  blocking collectives  57.3 us (11%)
  matrix products  19.5 us (4%)
  between operations  16.4 us (3%)
  starting transfers between devices  10.9 us (2%)
  local copies, waits for them, and re-layouts  9.87 us (2%)
  other arithmetic  7.45 us (1%)
    psum x1, waiting for transfers between devices, spread(): return lax.psum(kept, axis)  124 us
    psum x1, waiting for transfers between devices, factor_rows(): lax.psum(partial_value.astype(jnp.bfloat16), 'col').astype(jnp.float32)  79.6 us
    all_gather x2, waiting for transfers between devices, cube_collect(): return lax.all_gather(owned[None], 'cube', axis=0, tiled=True)  59.1 us
    all_gather x3, blocking collectives, factor_rows(): lax.all_gather(inverse, 'row', axis=0, tiled=True)  57.3 us
    all_gather x1, waiting for transfers between devices, local(): lax.all_gather(mid_update, 'row', axis=0, tiled=True)  46.1 us
    all_to_all x1, waiting for transfers between devices, local(): lax.all_to_all(outgoing, 'cube', split_axis=0, concat_axis=0, tiled=True)  41.9 us
    all_gather x1, waiting for transfers between devices, local(): lax.all_gather(leaf_update, 'row', axis=0, tiled=True)  41.6 us
  transfers between devices with their start and end apart: 8, of which 7 were waited for; matrix products, arithmetic and copies ran while one was open for 4% of the time, Pallas kernels for 0%

commit v1 on v0

v1 whole, which is shorter than its diff:
```python
import jax
import jax.numpy as jnp
from jax import lax
from jax.experimental import pallas as pl
from jax.experimental.pallas import tpu as pltpu
from jax.sharding import Mesh, PartitionSpec as P

CUBE = ("pair", "half")
ROW = ("z", "core")
COL = ("ylo", "x")
VMEM = pl.BlockSpec(memory_space=pltpu.VMEM)
SMEM = pl.BlockSpec(memory_space=pltpu.SMEM)
BF = jnp.bfloat16
F32 = jnp.float32


def params():
    return pltpu.CompilerParams(vmem_limit_bytes=40 * 1024 * 1024)


def shape(dims, dtype=BF):
    return jax.ShapeDtypeStruct(dims, dtype)


def dot_t(left, right):
    return lax.dot_general(left, right, (((1,), (1,)), ((), ())), preferred_element_type=F32)


def weights_kernel(where, leaf, mid, root, out):
    pair = where[0] // 2
    for to in range(8):
        out[to, 0] = leaf[0]
        out[to, 1] = mid[pair]
        out[to, 2] = root[...]


def partial_kernel(where, leaf, mid, root, own, other, out):
    first = where[1] % 2 == 0
    for front, panel in enumerate((leaf, mid, root)):
        for group in range(0, 8, 2):
            rows = []
            for at in (group, group + 1):
                mine, theirs = own[at, front], other[at, front]
                rows.append(jnp.where(first, mine, theirs))
                rows.append(jnp.where(first, theirs, mine))
            product = dot_t(panel[...], jnp.concatenate(rows, 0)).astype(BF)
            out[group, front] = product[:, :128]
            out[group + 1, front] = product[:, 128:]


def factor_kernel(where, leaf_fill, mid_fill, root_fill, parts, leaf, mid, root, spread, low, high):
    cube, row = where[0], where[1]
    fills = (
        leaf_fill[cube, row],
        mid_fill[cube // 2, 16 * (cube % 2) + row],
        root_fill[16 * cube + row],
    )
    for front, target in enumerate((leaf, mid, root)):
        total = parts[0, front].astype(F32)
        for at in range(1, 8):
            total = total + parts[at, front].astype(F32)
        value = (total * fills[front].astype(F32)).astype(BF)
        target[...] = value
        for to in range(8):
            spread[to, front] = value
        low[front] = value[:128]
        high[front] = value[128:]


def update_kernel(where, factors, own, other, leaf_front, mid_front, out, rows, columns):
    first = where[1] % 2 == 0
    for front in range(2):
        for at in range(8):
            rows[front, :, 128 * at : 128 * at + 128] = factors[at, front]
    for kind in range(3):
        for at in range(8):
            half, group = at // 4, 2 * (at % 4)
            mine, theirs = own[at, kind], other[at, kind]
            span = slice(128 * half, 128 * half + 128)
            columns[kind, span, 128 * group : 128 * group + 128] = jnp.where(first, mine, theirs)
            columns[kind, span, 128 * group + 128 : 128 * group + 256] = jnp.where(
                first, theirs, mine
            )
    for kind in range(3):
        product = dot_t(rows[min(kind, 1)], columns[kind])
        if kind == 0:
            matrix = leaf_front[...]
        else:
            matrix = mid_front[:, 256 * (kind - 1) : 256 * kind]
        value = matrix - product
        for side in range(2):
            piece = value[:, 128 * side : 128 * side + 128].reshape(32, 8, 128)
            out[:, side, kind] = piece.astype(BF)


def place_kernel(where, leaf_map, mid_map, pieces, out, total):
    column = where[2]
    total[...] = jnp.zeros_like(total)
    for front in range(4):
        pair = front // 2
        slot = mid_map[pair, leaf_map[front, column]] // 16
        for block in range(16):
            target = mid_map[pair, leaf_map[front, block]]
            total[4 * target + slot] += pieces[16 * front + block, 0].astype(F32)
    for pair in range(2):
        slots = [mid_map[pair, 16 * at + column] // 16 for at in range(2)]
        for block in range(32):
            target = mid_map[pair, block]
            for at in range(2):
                total[4 * target + slots[at]] += pieces[32 * pair + block, 1 + at].astype(F32)
    out[...] = total[...].reshape(64, 4, 8, 128).astype(BF)


def root_kernel(factors, blocks, arrived, front, out, rows, columns):
    @pl.when(pl.program_id(0) == 0)
    def _():
        for at in range(8):
            rows[:, 128 * at : 128 * at + 128] = factors[at, 0]

    for half in range(2):
        for at in range(8):
            columns[128 * half : 128 * half + 128, 128 * at : 128 * at + 128] = blocks[
                8 * half + at
            ]
    value = front[...] - dot_t(rows[...], columns[...])
    for side in range(2):
        added = arrived[:, side, 0].astype(F32).reshape(256, 128)
        span = slice(128 * side, 128 * side + 128)
        out[:, span] = value[:, span] + added


def swap(value, axis):
    return lax.ppermute(value, axis, [(0, 1), (1, 0)])


def transpose(low, high):
    to_low = [(8 * r + c, 8 * c + r) for r in range(8) for c in range(8)]
    to_high = [(8 * r + c, 8 * (c + 8) + r) for r in range(8) for c in range(8)]
    return lax.ppermute(low, ROW + COL, to_low), lax.ppermute(high, ROW + COL, to_high)


def local(
    leaf_front,
    leaf_panel,
    leaf_inverse,
    leaf_fill,
    mid_front,
    mid_panel,
    mid_inverse,
    mid_fill,
    root_front,
    root_panel,
    root_inverse,
    root_fill,
    leaf_map,
    mid_map,
):
    row = lax.axis_index(ROW)
    where = jnp.stack([lax.axis_index(CUBE), row, lax.axis_index(COL)]).astype(jnp.int32)

    weights = pl.pallas_call(
        weights_kernel,
        out_shape=shape((8, 3, 64, 128)),
        in_specs=[SMEM, VMEM, VMEM, VMEM],
        out_specs=VMEM,
        compiler_params=params(),
    )(where, leaf_inverse, mid_inverse, root_inverse)
    own = lax.all_to_all(weights, "z", 0, 0, tiled=True)
    other = swap(own, "core")
    partials = pl.pallas_call(
        partial_kernel,
        out_shape=shape((8, 3, 256, 128)),
        in_specs=[SMEM] + [VMEM] * 5,
        out_specs=VMEM,
        compiler_params=params(),
    )(where, leaf_panel, mid_panel, root_panel, own, other)
    partials = lax.all_to_all(partials, COL, 0, 0, tiled=True)
    piece = shape((256, 128))
    leaf_factor, mid_factor, root_factor, spread, low, high = pl.pallas_call(
        factor_kernel,
        out_shape=(piece, piece, piece, shape((8, 3, 256, 128)), shape((3, 128, 128)), shape((3, 128, 128))),
        in_specs=[SMEM] * 4 + [VMEM],
        out_specs=(VMEM,) * 6,
        compiler_params=params(),
    )(where, leaf_fill, mid_fill, root_fill, partials)

    low, high = transpose(low, high)
    factors = lax.all_to_all(spread, COL, 0, 0, tiled=True)
    turned = jnp.where(row < 8, low, high)
    root_blocks = lax.all_gather(turned[2], CUBE + ROW, axis=0, tiled=False)
    half = lax.axis_index("half")
    partner = swap(turned[1], "half")
    first = jnp.where(half == 0, turned[1], partner)
    second = jnp.where(half == 0, partner, turned[1])
    sent = jnp.stack([turned[0], first, second])
    own = lax.all_to_all(jnp.broadcast_to(sent[None], (8, 3, 128, 128)), "z", 0, 0, tiled=True)
    other = swap(own, "core")
    updates = pl.pallas_call(
        update_kernel,
        out_shape=shape((32, 2, 3, 8, 128)),
        in_specs=[SMEM] + [VMEM] * 5,
        out_specs=VMEM,
        scratch_shapes=[pltpu.VMEM((2, 256, 1024), BF), pltpu.VMEM((3, 256, 1024), BF)],
        compiler_params=params(),
    )(where, factors, own, other, leaf_front, mid_front)
    pieces = lax.all_to_all(updates.reshape(64, 3, 8, 128), CUBE + ROW, 0, 0, tiled=True)
    placed = pl.pallas_call(
        place_kernel,
        out_shape=shape((64, 4, 8, 128)),
        in_specs=[SMEM] * 3 + [VMEM],
        out_specs=VMEM,
        scratch_shapes=[pltpu.VMEM((256, 8, 128), F32)],
        compiler_params=params(),
    )(where, leaf_map, mid_map, pieces)
    arrived = lax.all_to_all(placed, CUBE + ROW, 0, 0, tiled=True)
    root_update = pl.pallas_call(
        root_kernel,
        grid=(4,),
        out_shape=shape((256, 1024), F32),
        in_specs=[
            pl.BlockSpec((8, 1, 256, 128), lambda s: (0, 2, 0, 0)),
            pl.BlockSpec((16, 128, 128), lambda s: (s, 0, 0)),
            pl.BlockSpec((32, 2, 1, 8, 128), lambda s: (0, 0, s, 0, 0)),
            pl.BlockSpec((256, 256), lambda s: (0, s)),
        ],
        out_specs=pl.BlockSpec((256, 256), lambda s: (0, s)),
        scratch_shapes=[pltpu.VMEM((256, 1024), BF), pltpu.VMEM((256, 1024), BF)],
        compiler_params=params(),
    )(factors, root_blocks, arrived.reshape(32, 2, 4, 8, 128), root_front)
    return leaf_factor, mid_factor, root_factor, root_update


def solution(mesh):
    fine = Mesh(
        mesh.devices.reshape(2, 2, 8, 2, 2, 4), ("pair", "half", "z", "core", "ylo", "x")
    )
    block = P(CUBE + ROW, COL)
    in_specs = (
        block,
        block,
        P(CUBE, ROW, COL),
        P(),
        block,
        block,
        P(None, ROW, COL),
        P(),
        block,
        block,
        P(ROW, COL),
        P(),
        P(),
        P(),
    )
    return jax.shard_map(
        local, mesh=fine, in_specs=in_specs, out_specs=(block,) * 4, check_vma=False
    )
```

time: 515 us -> 231 us (0.45)
  waiting for transfers between devices: 393 us -> 57.9 us
  blocking collectives: 57.3 us -> 107 us
  starting transfers between devices: 10.9 us -> 31.6 us
  matrix products: 19.5 us -> 0 us
  Pallas kernels: 0 us -> 9.53 us
  other arithmetic: 7.45 us -> 0.11 us
    psum x2 -> x0, waiting for transfers between devices: 203 us -> none  [the longest x1 124 us: spread(): return lax.psum(kept, axis)]
    all_to_all x0 -> x4, blocking collectives: none -> 107 us  [the longest x1 31.5 us: local(): lax.all_to_all(updates.reshape(64, 3, 8, 128), CUBE + ROW, 0, 0, tiled=True)]
    all_gather x4 -> x1, waiting for transfers between devices: 147 us -> 41.6 us  [local(): root_blocks = lax.all_gather(turned[2], CUBE + ROW, axis=0, tiled=False)]
    all_gather x3 -> x0, blocking collectives: 57.3 us -> none  [factor_rows(): lax.all_gather(inverse, 'row', axis=0, tiled=True)]
    all_to_all x1 -> x2, waiting for transfers between devices: 41.9 us -> 5.08 us  [the longest x1 5.08 us: local(): factors = lax.all_to_all(spread, COL, 0, 0, tiled=True)]
    dot_general x10 -> x0, matrix products: 19.5 us -> none  [the longest x2 7.6 us: row_folder(): jnp.einsum('au,axk->uxk', select, tiles, preferred_element_type=jnp.float32)]
    ppermute x1 -> x5, starting transfers between devices: 4.16 us -> 21 us  [the longest x3 15.8 us: swap(): return lax.ppermute(value, axis, [(0, 1), (1, 0)])]
    ppermute x1 -> x5, waiting for transfers between devices: 0.01 us -> 10.5 us  [the longest x3 4.9 us: swap(): return lax.ppermute(value, axis, [(0, 1), (1, 0)])]
  transfers between devices with their start and end apart: 8 -> 8, of which waited for: 7 -> 7; matrix products, arithmetic and copies ran while one was open for 4% -> 0% of each run, Pallas kernels for 0% -> 2%
where the time goes in v1:
time: 231 us; the launch traced here: 230 us
  blocking collectives  107 us (46%)
  waiting for transfers between devices  57.9 us (25%)
  starting transfers between devices  31.6 us (14%)
  between operations  14.2 us (6%)
  Pallas kernels  9.53 us (4%)
  local copies, waits for them, and re-layouts  9.29 us (4%)
    all_gather x1, waiting for transfers between devices, local(): root_blocks = lax.all_gather(turned[2], CUBE + ROW, axis=0, tiled=False)  41.6 us
    all_to_all x1, blocking collectives, local(): lax.all_to_all(updates.reshape(64, 3, 8, 128), CUBE + ROW, 0, 0, tiled=True)  31.5 us
    all_to_all x1, blocking collectives, local(): lax.all_to_all(jnp.broadcast_to(sent[None], (8, 3, 128, 128)), 'z', 0, 0,...  26.2 us
    all_to_all x1, blocking collectives, local(): partials = lax.all_to_all(partials, COL, 0, 0, tiled=True)  25 us
    all_to_all x1, blocking collectives, local(): own = lax.all_to_all(weights, 'z', 0, 0, tiled=True)  24.2 us
    ppermute x3, starting transfers between devices, swap(): return lax.ppermute(value, axis, [(0, 1), (1, 0)])  15.8 us
    unnamed x32, local copies, waits for them, and re-layouts  8.52 us
    all_to_all x1, starting transfers between devices, local(): arrived = lax.all_to_all(placed, CUBE + ROW, 0, 0, tiled=True)  6.54 us
  transfers between devices with their start and end apart: 8, of which 7 were waited for; matrix products, arithmetic and copies ran while one was open for 0% of the time, Pallas kernels for 2%

profile of v1, /device:TPU:1, one launch (start us, length us, event | category | flops | bytes accessed | tf_op | source)
XLA Modules:
  0.0 229.6 jit_solution(659307171207741231)
XLA Ops:
  7.3 0.8 copy-done.8
  8.0 0.7 copy-done.9
  8.7 0.7 copy-done.10
  10.0 24.2 %all_to_all.30.own = bf16[8,3,64,128]{3,2,1,0:T(8,128)(2,1)S(1)} all-to-all(bf16[8,3,64,128]{3,2,1,0:T(8,128)(2,1)S(1)} %shard_map.165), channel_id=1, replica_groups=mesh['pair'=2,'half'=2,'z'=8,'core'=2,'ylo'=2,'x'=4] {'z'}, dimensions={0} | all-to-all | bytes 786432 | tf_op jit(solution)/shard_map/all_to_all | solution.py:168
  34.2 4.0 %collective-permute-start = (bf16[8,3,64,128]{3,2,1,0:T(8,128)(2,1)S(1)}, bf16[8,3,64,128]{3,2,1,0:T(8,128)(2,1)S(1)}, u32[]{:S(2)}, u32[]{:S(2)}) collective-permute-start(bf16[8,3,64,128]{3,2,1,0:T(8,128)(2,1)S(1)} %all_to_all.30.own), channel_id=1, source_target_pairs={{0,8},{8,0},{1,9},{9,1},{2,10},{10,2},{3,11},{11,3},{4,12},{12,4},... | collective-permute-start | bytes 1179656 | tf_op jit(solution)/shard_map/ppermute | solution.py:133
  38.3 1.3 collective-permute-done.other
  39.6 0.8 copy-done.5
  40.4 0.8 copy-done.6
  41.3 0.8 copy-done.7
  42.1 1.1 shard_map.166
  43.3 25.0 %all_to_all.31.parts = bf16[8,3,256,128]{3,2,1,0:T(8,128)(2,1)S(1)} all-to-all(bf16[8,3,256,128]{3,2,1,0:T(8,128)(2,1)S(1)} %shard_map.166), channel_id=1, replica_groups=mesh['pair'=2,'half'=2,'z'=8,'core'=2,'ylo'=2,'x'=4] {'ylo','x'}, dimensions={0} | all-to-all | bytes 3145728 | tf_op jit(solution)/shard_map/all_to_all | solution.py:177
  68.3 1.5 shard_map.167
  69.8 1.1 copy-done.1
  70.9 3.9 %collective-permute-start.1 = (bf16[3,128,128]{2,1,0:T(8,128)(2,1)S(1)}, bf16[3,128,128]{2,1,0:T(8,128)(2,1)S(1)}, u32[]{:S(2)}, u32[]{:S(2)}) collective-permute-start(bf16[3,128,128]{2,1,0:T(8,128)(2,1)S(1)} %get-tuple-element.14), channel_id=1, source_target_pairs={{0,0},{1,8},{2,16},{3,24},{4,32},{5,40},{6,48},{7,56},{8,1},{9,9},... | collective-permute-start | bytes 294920 | tf_op jit(solution)/shard_map/ppermute | solution.py:139
  74.8 1.3 collective-permute-start.2
  76.1 1.7 collective-permute-done.1
  77.8 3.9 %collective-permute-done.2 = bf16[3,128,128]{2,1,0:T(8,128)(2,1)S(1)} collective-permute-done((bf16[3,128,128]{2,1,0:T(8,128)(2,1)S(1)}, bf16[3,128,128]{2,1,0:T(8,128)(2,1)S(1)}, u32[]{:S(2)}, u32[]{:S(2)}) %collective-permute-start.2) | collective-permute-done | bytes 98336 | tf_op jit(solution)/shard_map/ppermute | solution.py:139
  82.4 4.2 %collective-permute-start.3 = (bf16[128,128]{1,0:T(8,128)(2,1)S(1)}, bf16[128,128]{1,0:T(8,128)(2,1)S(1)}, u32[]{:S(2)}, u32[]{:S(2)}) collective-permute-start(bf16[128,128]{1,0:T(8,128)(2,1)S(1)} %get-tuple-element.19), channel_id=1, source_target_pairs={{0,128},{128,0},{1,129},{129,1},{2,130},{130,2},{3,131},{131,3},{4... | collective-permute-start | bytes 98312 | tf_op jit(solution)/shard_map/ppermute | solution.py:133
  86.6 1.7 collective-permute-done.3
  88.5 26.2 %all_to_all.32.own = bf16[8,3,128,128]{3,2,1,0:T(8,128)(2,1)S(1)} all-to-all(bf16[8,3,128,128]{3,2,1,0:T(8,128)(2,1)S(1)} %broadcast_in_dim.2), channel_id=1, replica_groups=mesh['pair'=2,'half'=2,'z'=8,'core'=2,'ylo'=2,'x'=4] {'z'}, dimensions={0} | all-to-all | bytes 1572864 | tf_op jit(solution)/shard_map/all_to_all | solution.py:196
  114.7 4.1 %all-to-all-start.2 = ((bf16[8,3,256,128]{3,2,1,0:T(8,128)(2,1)}), bf16[8,3,256,128]{3,2,1,0:T(8,128)(2,1)S(1)}, u32[]{:S(2)}, u32[]{:S(2)}) async-start(bf16[8,3,256,128]{3,2,1,0:T(8,128)(2,1)} %copy-done.1), calls=%async_computation.2 | async-start | bytes 3145728 | tf_op jit(solution)/shard_map/all_to_all | solution.py:188
  119.5 7.6 %collective-permute-start.4 = (bf16[8,3,128,128]{3,2,1,0:T(8,128)(2,1)S(1)}, bf16[8,3,128,128]{3,2,1,0:T(8,128)(2,1)S(1)}, u32[]{:S(2)}, u32[]{:S(2)}) collective-permute-start(bf16[8,3,128,128]{3,2,1,0:T(8,128)(2,1)S(1)} %all_to_all.32.own), channel_id=1, source_target_pairs={{0,8},{8,0},{1,9},{9,1},{2,10},{10,2},{3,11},{11,3},{4,12},{12,4},... | collective-permute-start | bytes 2359304 | tf_op jit(solution)/shard_map/ppermute | solution.py:133
  127.1 1.9 collective-permute-done.4.other
  129.0 5.1 %all-to-all-done.2.factors = bf16[8,3,256,128]{3,2,1,0:T(8,128)(2,1)S(1)} async-done(((bf16[8,3,256,128]{3,2,1,0:T(8,128)(2,1)}), bf16[8,3,256,128]{3,2,1,0:T(8,128)(2,1)S(1)}, u32[]{:S(2)}, u32[]{:S(2)}) %all-to-all-start.2) | async-done | bytes 1572896 | tf_op jit(solution)/shard_map/all_to_all | solution.py:188
  134.0 1.0 copy-done.3
  135.1 1.3 shard_map.168
  136.4 31.5 %all_to_all.33.pieces = bf16[64,3,8,128]{3,2,1,0:T(8,128)(2,1)S(1)} all-to-all(bf16[64,3,8,128]{3,2,1,0:T(8,128)(2,1)S(1)} %bitcast.16), channel_id=1, replica_groups=mesh['pair'=2,'half'=2,'z'=8,'core'=2,'ylo'=2,'x'=4] {'pair','half','z',..., dimensions={0} | all-to-all | bytes 786432 | tf_op jit(solution)/shard_map/all_to_all | solution.py:206
  167.9 2.2 shard_map.169
  170.1 6.5 %all-to-all-start.5 = ((bf16[64,4,8,128]{3,2,1,0:T(8,128)(2,1)}), bf16[64,4,8,128]{3,2,1,0:T(8,128)(2,1)S(1)}, u32[]{:S(2)}, u32[]{:S(2)}) async-start(bf16[64,4,8,128]{3,2,1,0:T(8,128)(2,1)} %shard_map.169), calls=%async_computation.5 | async-start | bytes 1048576 | tf_op jit(solution)/shard_map/all_to_all | solution.py:215
  176.6 41.6 %all-gather.2.cloned.1.call-done.blocks = bf16[64,128,128]{2,1,0:T(8,128)(2,1)} async-done(((bf16[1,128,128]{2,1,0:T(8,128)(2,1)}), bf16[64,128,128]{2,1,0:T(8,128)(2,1)}) %all-gather.2.cloned.1.call-update) | async-done | bytes 2097168 | tf_op jit(solution)/shard_map/all_gather | solution.py:190
  218.3 1.6 copy-done
  219.9 2.9 %shard_map.170 = f32[256,1024]{1,0:T(8,128)} custom-call(bf16[8,3,256,128]{3,2,1,0:T(8,128)(2,1)S(1)} %all-to-all-done.2.factors, bf16[64,128,128]{2,1,0:T(8,128)(2,1)S(1)} %copy-done, bf16[32,2,4,8,128]{4,3,2,1,0:T(8,128)(2,1)S(1)} %bitcast.15, f32[256,1024]{1,0:T(8,128)S(1)} %copy-done.2), custom_call_target="tpu_custom_call" | custom-call | tf_op jit(solution)/shard_map/pallas_call | solution.py:216
  (33 shorter events, 2.2 us)
Async XLA Ops:
  7.3 0.8 copy-start.8
  8.0 0.7 copy-start.9
  8.7 0.7 copy-start.10
  34.2 5.4 %collective-permute-start = (bf16[8,3,64,128]{3,2,1,0:T(8,128)(2,1)S(1)}, bf16[8,3,64,128]{3,2,1,0:T(8,128)(2,1)S(1)}, u32[]{:S(2)}, u32[]{:S(2)}) collective-permute-start(bf16[8,3,64,128]{3,2,1,0:T(8,128)(2,1)S(1)} %all_to_all.30.own), channel_id=1, source_target_pairs={{0,8},{8,0},{1,9},{9,1},{2,10},{10,2},{3,11},{11,3},{4,12},{12,4},... | collective-permute-start | bytes 1179656 | tf_op jit(solution)/shard_map/ppermute | solution.py:133
  39.6 0.8 copy-start.5
  40.4 0.8 copy-start.6
  41.3 0.8 copy-start.7
  43.2 25.0 %copy-start.11 = (s32[4,16]{1,0:T(4,128)S(1)}, s32[4,16]{1,0:T(4,128)}, u32[]{:S(2)}) copy-start(s32[4,16]{1,0:T(4,128)} %leaf_fill.1) | copy-start | bytes 772
  43.3 25.0 %copy-start.13 = (s32[2,32]{1,0:T(2,128)S(1)}, s32[2,32]{1,0:T(2,128)}, u32[]{:S(2)}) copy-start(s32[2,32]{1,0:T(2,128)} %mid_fill.1) | copy-start | bytes 772
  43.3 25.0 %copy-start.15 = (s32[64]{0:T(128)S(1)}, s32[64]{0:T(128)}, u32[]{:S(2)}) copy-start(s32[64]{0:T(128)} %root_fill.1) | copy-start | bytes 772
  69.8 1.1 copy-start.1
  70.9 6.9 %collective-permute-start.1 = (bf16[3,128,128]{2,1,0:T(8,128)(2,1)S(1)}, bf16[3,128,128]{2,1,0:T(8,128)(2,1)S(1)}, u32[]{:S(2)}, u32[]{:S(2)}) collective-permute-start(bf16[3,128,128]{2,1,0:T(8,128)(2,1)S(1)} %get-tuple-element.14), channel_id=1, source_target_pairs={{0,0},{1,8},{2,16},{3,24},{4,32},{5,40},{6,48},{7,56},{8,1},{9,9},... | collective-permute-start | bytes 294920 | tf_op jit(solution)/shard_map/ppermute | solution.py:139
  74.8 6.9 %collective-permute-start.2 = (bf16[3,128,128]{2,1,0:T(8,128)(2,1)S(1)}, bf16[3,128,128]{2,1,0:T(8,128)(2,1)S(1)}, u32[]{:S(2)}, u32[]{:S(2)}) collective-permute-start(bf16[3,128,128]{2,1,0:T(8,128)(2,1)S(1)} %get-tuple-element.15), channel_id=1, source_target_pairs={{0,64},{1,72},{2,80},{3,88},{4,96},{5,104},{6,112},{7,120},{8,65},... | collective-permute-start | bytes 294920 | tf_op jit(solution)/shard_map/ppermute | solution.py:139
  82.4 5.9 %collective-permute-start.3 = (bf16[128,128]{1,0:T(8,128)(2,1)S(1)}, bf16[128,128]{1,0:T(8,128)(2,1)S(1)}, u32[]{:S(2)}, u32[]{:S(2)}) collective-permute-start(bf16[128,128]{1,0:T(8,128)(2,1)S(1)} %get-tuple-element.19), channel_id=1, source_target_pairs={{0,128},{128,0},{1,129},{129,1},{2,130},{130,2},{3,131},{131,3},{4... | collective-permute-start | bytes 98312 | tf_op jit(solution)/shard_map/ppermute | solution.py:133
  114.7 19.4 %copy-start.4 = (f32[256,256]{1,0:T(8,128)S(1)}, f32[256,256]{1,0:T(8,128)}, u32[]{:S(2)}) copy-start(f32[256,256]{1,0:T(8,128)} %leaf_front.1) | copy-start | bytes 786436
  114.7 19.4 %all-to-all-start.2 = ((bf16[8,3,256,128]{3,2,1,0:T(8,128)(2,1)}), bf16[8,3,256,128]{3,2,1,0:T(8,128)(2,1)S(1)}, u32[]{:S(2)}, u32[]{:S(2)}) async-start(bf16[8,3,256,128]{3,2,1,0:T(8,128)(2,1)} %copy-done.1), calls=%async_computation.2 | async-start | bytes 3145728 | tf_op jit(solution)/shard_map/all_to_all | solution.py:188
  118.7 99.5 %all-gather.2.cloned.1.call-start = ((), (), s32[]{:S(2)}) async-start(), calls=%async_computation.6 | async-start | bytes 2129920 | tf_op jit(solution)/shard_map/all_gather | solution.py:190
  118.8 49.1 %copy-start.12 = (s32[4,16]{1,0:T(4,128)S(1)}, s32[4,16]{1,0:T(4,128)}, u32[]{:S(2)}) copy-start(s32[4,16]{1,0:T(4,128)} %leaf_map.1) | copy-start | bytes 772
  118.8 49.1 %copy-start.14 = (s32[2,32]{1,0:T(2,128)S(1)}, s32[2,32]{1,0:T(2,128)}, u32[]{:S(2)}) copy-start(s32[2,32]{1,0:T(2,128)} %mid_map.1) | copy-start | bytes 772
  119.5 9.5 %collective-permute-start.4 = (bf16[8,3,128,128]{3,2,1,0:T(8,128)(2,1)S(1)}, bf16[8,3,128,128]{3,2,1,0:T(8,128)(2,1)S(1)}, u32[]{:S(2)}, u32[]{:S(2)}) collective-permute-start(bf16[8,3,128,128]{3,2,1,0:T(8,128)(2,1)S(1)} %all_to_all.32.own), channel_id=1, source_target_pairs={{0,8},{8,0},{1,9},{9,1},{2,10},{10,2},{3,11},{11,3},{4,12},{12,4},... | collective-permute-start | bytes 2359304 | tf_op jit(solution)/shard_map/ppermute | solution.py:133
  134.0 1.0 copy-start.3
  136.4 81.8 %copy-start.2 = (f32[256,1024]{1,0:T(8,128)S(1)}, f32[256,1024]{1,0:T(8,128)}, u32[]{:S(2)}) copy-start(f32[256,1024]{1,0:T(8,128)} %front.1) | copy-start | bytes 3145732
  170.1 48.2 %all-to-all-start.5 = ((bf16[64,4,8,128]{3,2,1,0:T(8,128)(2,1)}), bf16[64,4,8,128]{3,2,1,0:T(8,128)(2,1)S(1)}, u32[]{:S(2)}, u32[]{:S(2)}) async-start(bf16[64,4,8,128]{3,2,1,0:T(8,128)(2,1)} %shard_map.169), calls=%async_computation.5 | async-start | bytes 1048576 | tf_op jit(solution)/shard_map/all_to_all | solution.py:215
  218.3 1.6 copy-start
Sparse Core Ops, SparseCore 0:
  122.9 95.2 all-gather.1

commit v2 on v1

--- a/solution.py
+++ b/solution.py
@@ -14,8 +14,11 @@
 F32 = jnp.float32
 
 
-def params():
-    return pltpu.CompilerParams(vmem_limit_bytes=40 * 1024 * 1024)
+ANY = pl.BlockSpec(memory_space=pl.ANY)
+
+
+def params(mebibytes=40):
+    return pltpu.CompilerParams(vmem_limit_bytes=mebibytes * 1024 * 1024)
 
 
 def shape(dims, dtype=BF):
@@ -26,29 +29,32 @@
     return lax.dot_general(left, right, (((1,), (1,)), ((), ())), preferred_element_type=F32)
 
 
-def weights_kernel(where, leaf, mid, root, out):
+def weights_kernel(where, leaf, mid, root, leaf_panel, mid_panel, root_panel, out, panels):
     pair = where[0] // 2
+    panels[0] = leaf_panel[...]
+    panels[1] = mid_panel[...]
+    panels[2] = root_panel[...]
     for to in range(8):
         out[to, 0] = leaf[0]
         out[to, 1] = mid[pair]
         out[to, 2] = root[...]
 
 
-def partial_kernel(where, leaf, mid, root, own, other, out):
+def partial_kernel(where, panels, own, other, out):
     first = where[1] % 2 == 0
-    for front, panel in enumerate((leaf, mid, root)):
+    for front in range(3):
         for group in range(0, 8, 2):
             rows = []
             for at in (group, group + 1):
                 mine, theirs = own[at, front], other[at, front]
                 rows.append(jnp.where(first, mine, theirs))
                 rows.append(jnp.where(first, theirs, mine))
-            product = dot_t(panel[...], jnp.concatenate(rows, 0)).astype(BF)
+            product = dot_t(panels[front], jnp.concatenate(rows, 0)).astype(BF)
             out[group, front] = product[:, :128]
             out[group + 1, front] = product[:, 128:]
 
 
-def factor_kernel(where, leaf_fill, mid_fill, root_fill, parts, leaf, mid, root, spread, low, high):
+def factor_kernel(where, leaf_fill, mid_fill, root_fill, parts, leaf, mid, root, spread, low, high, low_two, high_two):
     cube, row = where[0], where[1]
     fills = (
         leaf_fill[cube, row],
@@ -65,6 +71,23 @@
             spread[to, front] = value
         low[front] = value[:128]
         high[front] = value[128:]
+        if front > 0:
+            low_two[front - 1] = value[:128]
+            high_two[front - 1] = value[128:]
+
+
+def turn_kernel(where, low, high, low_two, high_two, after, sent, root):
+    cube, row = where[0], where[1]
+    own = [jnp.where(row < 8, low[front], high[front]) for front in range(3)]
+    partner = [jnp.where(row < 8, low_two[front], high_two[front]) for front in range(2)]
+    even = cube % 2 == 0
+    first, second = jnp.where(even, own[1], partner[0]), jnp.where(even, partner[0], own[1])
+    for to in range(8):
+        sent[to, 0] = own[0]
+        sent[to, 1] = first
+        sent[to, 2] = second
+    root[0] = jnp.where(even, own[2], partner[1])
+    root[1] = jnp.where(even, partner[1], own[2])
 
 
 def update_kernel(where, factors, own, other, leaf_front, mid_front, out, rows, columns):
@@ -111,7 +134,7 @@
     out[...] = total[...].reshape(64, 4, 8, 128).astype(BF)
 
 
-def root_kernel(factors, blocks, arrived, front, out, rows, columns):
+def root_kernel(factors, blocks, front, out, rows, columns):
     @pl.when(pl.program_id(0) == 0)
     def _():
         for at in range(8):
@@ -120,23 +143,39 @@
     for half in range(2):
         for at in range(8):
             columns[128 * half : 128 * half + 128, 128 * at : 128 * at + 128] = blocks[
-                8 * half + at
+                8 * half + at, 0
             ]
-    value = front[...] - dot_t(rows[...], columns[...])
+    out[...] = front[...] - dot_t(rows[...], columns[...])
+
+
+def add_kernel(base, arrived, out):
     for side in range(2):
         added = arrived[:, side, 0].astype(F32).reshape(256, 128)
         span = slice(128 * side, 128 * side + 128)
-        out[:, span] = value[:, span] + added
+        out[:, span] = base[:, span] + added
 
 
 def swap(value, axis):
     return lax.ppermute(value, axis, [(0, 1), (1, 0)])
 
 
-def transpose(low, high):
-    to_low = [(8 * r + c, 8 * c + r) for r in range(8) for c in range(8)]
-    to_high = [(8 * r + c, 8 * (c + 8) + r) for r in range(8) for c in range(8)]
-    return lax.ppermute(low, ROW + COL, to_low), lax.ppermute(high, ROW + COL, to_high)
+def transpose(low, high, low_two, high_two):
+    low_pairs, high_pairs, low_cross, high_cross = [], [], [], []
+    for r in range(8):
+        for c in range(8):
+            low_pairs.append((8 * r + c, 8 * c + r))
+            high_pairs.append((8 * r + c, 8 * (c + 8) + r))
+            for half in range(2):
+                source = 128 * half + 8 * r + c
+                low_cross.append((source, 128 * (1 - half) + 8 * c + r))
+                high_cross.append((source, 128 * (1 - half) + 8 * (c + 8) + r))
+    plane = ROW + COL
+    return (
+        lax.ppermute(low, plane, low_pairs),
+        lax.ppermute(high, plane, high_pairs),
+        lax.ppermute(low_two, ("half",) + plane, low_cross),
+        lax.ppermute(high_two, ("half",) + plane, high_cross),
+    )
 
 
 def local(
@@ -158,42 +197,50 @@
     row = lax.axis_index(ROW)
     where = jnp.stack([lax.axis_index(CUBE), row, lax.axis_index(COL)]).astype(jnp.int32)
 
-    weights = pl.pallas_call(
+    weights, panels = pl.pallas_call(
         weights_kernel,
-        out_shape=shape((8, 3, 64, 128)),
-        in_specs=[SMEM, VMEM, VMEM, VMEM],
-        out_specs=VMEM,
-        compiler_params=params(),
-    )(where, leaf_inverse, mid_inverse, root_inverse)
+        out_shape=(shape((8, 3, 64, 128)), shape((3, 256, 128))),
+        in_specs=[SMEM] + [VMEM] * 6,
+        out_specs=(VMEM, VMEM),
+        compiler_params=params(60),
+    )(where, leaf_inverse, mid_inverse, root_inverse, leaf_panel, mid_panel, root_panel)
     own = lax.all_to_all(weights, "z", 0, 0, tiled=True)
     other = swap(own, "core")
     partials = pl.pallas_call(
         partial_kernel,
         out_shape=shape((8, 3, 256, 128)),
-        in_specs=[SMEM] + [VMEM] * 5,
+        in_specs=[SMEM] + [VMEM] * 3,
         out_specs=VMEM,
         compiler_params=params(),
-    )(where, leaf_panel, mid_panel, root_panel, own, other)
+    )(where, panels, own, other)
     partials = lax.all_to_all(partials, COL, 0, 0, tiled=True)
-    piece = shape((256, 128))
-    leaf_factor, mid_factor, root_factor, spread, low, high = pl.pallas_call(
+    piece, three, two = shape((256, 128)), shape((3, 128, 128)), shape((2, 128, 128))
+    leaf_factor, mid_factor, root_factor, spread, *pieces = pl.pallas_call(
         factor_kernel,
-        out_shape=(piece, piece, piece, shape((8, 3, 256, 128)), shape((3, 128, 128)), shape((3, 128, 128))),
+        out_shape=(piece, piece, piece, shape((8, 3, 256, 128)), three, three, two, two),
         in_specs=[SMEM] * 4 + [VMEM],
-        out_specs=(VMEM,) * 6,
+        out_specs=(VMEM,) * 8,
         compiler_params=params(),
     )(where, leaf_fill, mid_fill, root_fill, partials)
 
-    low, high = transpose(low, high)
+    pieces = transpose(*pieces)
     factors = lax.all_to_all(spread, COL, 0, 0, tiled=True)
-    turned = jnp.where(row < 8, low, high)
-    root_blocks = lax.all_gather(turned[2], CUBE + ROW, axis=0, tiled=False)
-    half = lax.axis_index("half")
-    partner = swap(turned[1], "half")
-    first = jnp.where(half == 0, turned[1], partner)
-    second = jnp.where(half == 0, partner, turned[1])
-    sent = jnp.stack([turned[0], first, second])
-    own = lax.all_to_all(jnp.broadcast_to(sent[None], (8, 3, 128, 128)), "z", 0, 0, tiled=True)
+    sent, root_pair = pl.pallas_call(
+        turn_kernel,
+        out_shape=(shape((8, 3, 128, 128)), two),
+        in_specs=[SMEM] + [VMEM] * 4 + [ANY],
+        out_specs=(VMEM, VMEM),
+        compiler_params=params(),
+    )(where, *pieces, factors)
+    root_other = swap(root_pair, "pair")
+    own = lax.all_to_all(sent, "z", 0, 0, tiled=True)
+    pair = lax.axis_index("pair")
+    root_four = jnp.where(
+        pair == 0,
+        jnp.concatenate([root_pair, root_other]),
+        jnp.concatenate([root_other, root_pair]),
+    )
+    root_blocks = lax.all_gather(root_four, ROW, axis=0, tiled=False)
     other = swap(own, "core")
     updates = pl.pallas_call(
         update_kernel,
@@ -213,20 +260,29 @@
         compiler_params=params(),
     )(where, leaf_map, mid_map, pieces)
     arrived = lax.all_to_all(placed, CUBE + ROW, 0, 0, tiled=True)
-    root_update = pl.pallas_call(
+    spot = pl.BlockSpec((256, 256), lambda s: (0, s))
+    base = pl.pallas_call(
         root_kernel,
         grid=(4,),
         out_shape=shape((256, 1024), F32),
         in_specs=[
             pl.BlockSpec((8, 1, 256, 128), lambda s: (0, 2, 0, 0)),
-            pl.BlockSpec((16, 128, 128), lambda s: (s, 0, 0)),
-            pl.BlockSpec((32, 2, 1, 8, 128), lambda s: (0, 0, s, 0, 0)),
-            pl.BlockSpec((256, 256), lambda s: (0, s)),
+            pl.BlockSpec((16, 1, 128, 128), lambda s: (0, s, 0, 0)),
+            spot,
         ],
-        out_specs=pl.BlockSpec((256, 256), lambda s: (0, s)),
+        out_specs=spot,
         scratch_shapes=[pltpu.VMEM((256, 1024), BF), pltpu.VMEM((256, 1024), BF)],
-        compiler_params=params(),
-    )(factors, root_blocks, arrived.reshape(32, 2, 4, 8, 128), root_front)
+        compiler_params=params(60),
+        cost_estimate=pl.CostEstimate(flops=2**29, bytes_accessed=2**22, transcendentals=0),
+    )(factors, root_blocks, root_front)
+    root_update = pl.pallas_call(
+        add_kernel,
+        grid=(4,),
+        out_shape=shape((256, 1024), F32),
+        in_specs=[spot, pl.BlockSpec((32, 2, 1, 8, 128), lambda s: (0, 0, s, 0, 0))],
+        out_specs=spot,
+        compiler_params=params(),
+    )(base, arrived.reshape(32, 2, 4, 8, 128))
     return leaf_factor, mid_factor, root_factor, root_update
 
 

time: 231 us -> 215 us (0.931)
  waiting for transfers between devices: 57.9 us -> 31.1 us
  starting transfers between devices: 31.6 us -> 39.5 us
  local copies, waits for them, and re-layouts: 9.29 us -> 2.77 us
  Pallas kernels: 9.53 us -> 15.6 us
  blocking collectives: 107 us -> 110 us
    all_gather x1, waiting for transfers between devices: 41.6 us -> 0.02 us  [local(): root_blocks = lax.all_gather(root_four, ROW, axis=0, tiled=False)]
    all_to_all x1, waiting for transfers between devices: 0.01 us -> 14.5 us  [local(): arrived = lax.all_to_all(placed, CUBE + ROW, 0, 0, tiled=True)]
    all_to_all x1, blocking collectives: 26.2 us -> 37.7 us  [local(): own = lax.all_to_all(sent, 'z', 0, 0, tiled=True)]
    all_to_all x1, blocking collectives: 31.5 us -> 22.6 us  [local(): lax.all_to_all(updates.reshape(64, 3, 8, 128), CUBE + ROW, 0, 0, tiled=True)]
    ppermute x2 -> x4, starting transfers between devices: 5.18 us -> 12.2 us  [the longest x1 5.54 us: transpose(): lax.ppermute(low, plane, low_pairs)]
    unnamed x32 -> x24, local copies, waits for them, and re-layouts: 8.52 us -> 2.77 us
    ppermute x2 -> x4, waiting for transfers between devices: 5.63 us -> 11 us  [the longest x1 5.19 us: transpose(): lax.ppermute(low, plane, low_pairs)]
    all_to_all x1, waiting for transfers between devices: 5.08 us -> 0.01 us  [local(): factors = lax.all_to_all(spread, COL, 0, 0, tiled=True)]
  transfers between devices with their start and end apart: 8 -> 10, of which waited for: 7 -> 7; matrix products, arithmetic and copies ran while one was open for 0% -> 0% of each run, Pallas kernels for 2% -> 4%
where the time goes in v2:
time: 215 us; the launch traced here: 214 us
  blocking collectives  110 us (51%)
  starting transfers between devices  39.5 us (18%)
  waiting for transfers between devices  31.1 us (14%)
  Pallas kernels  15.6 us (7%)
  between operations  14.2 us (7%)
  local copies, waits for them, and re-layouts  2.77 us (1%)
    all_to_all x1, blocking collectives, local(): own = lax.all_to_all(sent, 'z', 0, 0, tiled=True)  37.7 us
    all_to_all x1, blocking collectives, local(): partials = lax.all_to_all(partials, COL, 0, 0, tiled=True)  25 us
    all_to_all x1, blocking collectives, local(): own = lax.all_to_all(weights, 'z', 0, 0, tiled=True)  24.4 us
    all_to_all x1, blocking collectives, local(): lax.all_to_all(updates.reshape(64, 3, 8, 128), CUBE + ROW, 0, 0, tiled=True)  22.6 us
    ppermute x3, starting transfers between devices, swap(): return lax.ppermute(value, axis, [(0, 1), (1, 0)])  17.2 us
    all_to_all x1, waiting for transfers between devices, local(): arrived = lax.all_to_all(placed, CUBE + ROW, 0, 0, tiled=True)  14.5 us
    all_to_all x1, starting transfers between devices, local(): arrived = lax.all_to_all(placed, CUBE + ROW, 0, 0, tiled=True)  6.26 us
    ppermute x3, waiting for transfers between devices, swap(): return lax.ppermute(value, axis, [(0, 1), (1, 0)])  5.62 us
  transfers between devices with their start and end apart: 10, of which 7 were waited for; matrix products, arithmetic and copies ran while one was open for 0% of the time, Pallas kernels for 4%

profile of v2, /device:TPU:1, one launch (start us, length us, event | category | flops | bytes accessed | tf_op | source)
XLA Modules:
  0.0 214.1 jit_solution(8461177441221479591)
XLA Ops:
  7.7 1.8 shard_map.165
  9.5 24.4 %all_to_all.30.own = bf16[8,3,64,128]{3,2,1,0:T(8,128)(2,1)S(1)} all-to-all(bf16[8,3,64,128]{3,2,1,0:T(8,128)(2,1)} %get-tuple-element.17), channel_id=1, replica_groups=mesh['pair'=2,'half'=2,'z'=8,'core'=2,'ylo'=2,'x'=4] {'z'}, dimensions={0} | all-to-all | bytes 786432 | tf_op jit(solution)/shard_map/all_to_all | solution.py:207
  33.9 4.0 %collective-permute-start = (bf16[8,3,64,128]{3,2,1,0:T(8,128)(2,1)S(1)}, bf16[8,3,64,128]{3,2,1,0:T(8,128)(2,1)S(1)}, u32[]{:S(2)}, u32[]{:S(2)}) collective-permute-start(bf16[8,3,64,128]{3,2,1,0:T(8,128)(2,1)S(1)} %all_to_all.30.own), channel_id=1, source_target_pairs={{0,8},{8,0},{1,9},{9,1},{2,10},{10,2},{3,11},{11,3},{4,12},{12,4},... | collective-permute-start | bytes 1179656 | tf_op jit(solution)/shard_map/ppermute | solution.py:159
  37.9 1.3 collective-permute-done.other
  39.3 0.9 copy-done.4
  40.2 0.6 copy-done.5
  40.8 1.1 shard_map.166
  41.9 25.0 %all_to_all.31.parts = bf16[8,3,256,128]{3,2,1,0:T(8,128)(2,1)S(1)} all-to-all(bf16[8,3,256,128]{3,2,1,0:T(8,128)(2,1)S(1)} %shard_map.166), channel_id=1, replica_groups=mesh['pair'=2,'half'=2,'z'=8,'core'=2,'ylo'=2,'x'=4] {'ylo','x'}, dimensions={0} | all-to-all | bytes 3145728 | tf_op jit(solution)/shard_map/all_to_all | solution.py:216
  67.0 2.1 shard_map.167
  69.0 3.7 %all-to-all-start.2 = ((bf16[8,3,256,128]{3,2,1,0:T(8,128)(2,1)}), bf16[8,3,256,128]{3,2,1,0:T(8,128)(2,1)S(1)}, u32[]{:S(2)}, u32[]{:S(2)}) async-start(bf16[8,3,256,128]{3,2,1,0:T(8,128)(2,1)} %get-tuple-element.21), calls=%async_computation.2 | async-start | bytes 3145728 | tf_op jit(solution)/shard_map/all_to_all | solution.py:227
  72.8 5.5 %collective-permute-start.1 = (bf16[3,128,128]{2,1,0:T(8,128)(2,1)S(1)}, bf16[3,128,128]{2,1,0:T(8,128)(2,1)S(1)}, u32[]{:S(2)}, u32[]{:S(2)}) collective-permute-start(bf16[3,128,128]{2,1,0:T(8,128)(2,1)S(1)} %get-tuple-element.22), channel_id=1, source_target_pairs={{0,0},{1,8},{2,16},{3,24},{4,32},{5,40},{6,48},{7,56},{8,1},{9,9},... | collective-permute-start | bytes 294920 | tf_op jit(solution)/shard_map/ppermute | solution.py:174
  78.3 1.3 collective-permute-start.2
  79.6 3.9 %collective-permute-start.3 = (bf16[2,128,128]{2,1,0:T(8,128)(2,1)S(1)}, bf16[2,128,128]{2,1,0:T(8,128)(2,1)S(1)}, u32[]{:S(2)}, u32[]{:S(2)}) collective-permute-start(bf16[2,128,128]{2,1,0:T(8,128)(2,1)S(1)} %get-tuple-element.24), channel_id=1, source_target_pairs={{0,128},{128,0},{1,136},{129,8},{2,144},{130,16},{3,152},{131,24},... | collective-permute-start | bytes 196616 | tf_op jit(solution)/shard_map/ppermute | solution.py:176
  83.6 1.4 collective-permute-start.4
  85.1 4.4 %collective-permute-done.3.low_two = bf16[2,128,128]{2,1,0:T(8,128)(2,1)S(1)} collective-permute-done((bf16[2,128,128]{2,1,0:T(8,128)(2,1)S(1)}, bf16[2,128,128]{2,1,0:T(8,128)(2,1)S(1)}, u32[]{:S(2)}, u32[]{:S(2)}) %collective-permute-start.3) | collective-permute-done | bytes 65568 | tf_op jit(solution)/shard_map/ppermute | solution.py:176
  89.4 1.4 collective-permute-done.4.high_two
  90.8 5.2 %collective-permute-done.1.low = bf16[3,128,128]{2,1,0:T(8,128)(2,1)S(1)} collective-permute-done((bf16[3,128,128]{2,1,0:T(8,128)(2,1)S(1)}, bf16[3,128,128]{2,1,0:T(8,128)(2,1)S(1)}, u32[]{:S(2)}, u32[]{:S(2)}) %collective-permute-start.1) | collective-permute-done | bytes 98336 | tf_op jit(solution)/shard_map/ppermute | solution.py:174
  96.0 0.7 shard_map.168
  96.7 6.6 %collective-permute-start.5 = (bf16[2,128,128]{2,1,0:T(8,128)(2,1)S(1)}, bf16[2,128,128]{2,1,0:T(8,128)(2,1)S(1)}, u32[]{:S(2)}, u32[]{:S(2)}) collective-permute-start(bf16[2,128,128]{2,1,0:T(8,128)(2,1)S(1)} %get-tuple-element.26), channel_id=1, source_target_pairs={{0,256},{256,0},{1,257},{257,1},{2,258},{258,2},{3,259},{259,3},{4... | collective-permute-start | bytes 196616 | tf_op jit(solution)/shard_map/ppermute | solution.py:159
  103.3 2.4 %collective-permute-done.5 = bf16[2,128,128]{2,1,0:T(8,128)(2,1)S(1)} collective-permute-done((bf16[2,128,128]{2,1,0:T(8,128)(2,1)S(1)}, bf16[2,128,128]{2,1,0:T(8,128)(2,1)S(1)}, u32[]{:S(2)}, u32[]{:S(2)}) %collective-permute-start.5) | collective-permute-done | bytes 65568 | tf_op jit(solution)/shard_map/ppermute | solution.py:159
  105.7 0.7 maximum_select_fusion
  106.4 37.7 %all_to_all.32.own = bf16[8,3,128,128]{3,2,1,0:T(8,128)(2,1)S(1)} all-to-all(bf16[8,3,128,128]{3,2,1,0:T(8,128)(2,1)S(1)} %get-tuple-element.27), channel_id=1, replica_groups=mesh['pair'=2,'half'=2,'z'=8,'core'=2,'ylo'=2,'x'=4] {'z'}, dimensions={0} | all-to-all | bytes 1572864 | tf_op jit(solution)/shard_map/all_to_all | solution.py:236
  144.1 6.7 %collective-permute-start.6 = (bf16[8,3,128,128]{3,2,1,0:T(8,128)(2,1)S(1)}, bf16[8,3,128,128]{3,2,1,0:T(8,128)(2,1)S(1)}, u32[]{:S(2)}, u32[]{:S(2)}) collective-permute-start(bf16[8,3,128,128]{3,2,1,0:T(8,128)(2,1)S(1)} %all_to_all.32.own), channel_id=1, source_target_pairs={{0,8},{8,0},{1,9},{9,1},{2,10},{10,2},{3,11},{11,3},{4,12},{12,4},... | collective-permute-start | bytes 2359304 | tf_op jit(solution)/shard_map/ppermute | solution.py:159
  150.8 1.9 collective-permute-done.6.other
  152.7 1.4 shard_map.170
  154.0 22.6 %all_to_all.33.pieces = bf16[64,3,8,128]{3,2,1,0:T(8,128)(2,1)S(1)} all-to-all(bf16[64,3,8,128]{3,2,1,0:T(8,128)(2,1)S(1)} %bitcast.8), channel_id=1, replica_groups=mesh['pair'=2,'half'=2,'z'=8,'core'=2,'ylo'=2,'x'=4] {'pair','half','z',..., dimensions={0} | all-to-all | bytes 786432 | tf_op jit(solution)/shard_map/all_to_all | solution.py:253
  176.7 2.2 %shard_map.171 = bf16[64,4,8,128]{3,2,1,0:T(8,128)(2,1)} custom-call(s32[3]{0:T(128)S(1)} %copy-done.6, s32[4,16]{1,0:T(4,128)S(1)} %copy-done.8, s32[2,32]{1,0:T(2,128)S(1)} %copy-done.10, bf16[64,3,8,128]{3,2,1,0:T(8,128)(2,1)S(1)} %all_to_all.33.pieces), custom_call_target="tpu_custom_call" | custom-call | tf_op jit(solution)/shard_map/pallas_call | solution.py:254
  178.8 6.3 %all-to-all-start.5 = ((bf16[64,4,8,128]{3,2,1,0:T(8,128)(2,1)}), bf16[64,4,8,128]{3,2,1,0:T(8,128)(2,1)S(1)}, u32[]{:S(2)}, u32[]{:S(2)}) async-start(bf16[64,4,8,128]{3,2,1,0:T(8,128)(2,1)} %shard_map.171), calls=%async_computation.5 | async-start | bytes 1048576 | tf_op jit(solution)/shard_map/all_to_all | solution.py:262
  185.1 4.8 %shard_map.169.base = f32[256,1024]{1,0:T(8,128)} custom-call(bf16[8,3,256,128]{3,2,1,0:T(8,128)(2,1)} %copy-done, bf16[16,4,128,128]{3,2,1,0:T(8,128)(2,1)} %all-gather.2.cloned.1.call-done.blocks, f32[256,1024]{1,0:T(8,128)} %front.1), custom_call_target="tpu_custom_call" | custom-call | flops 536870912 | bytes 4194304 | tf_op jit(solution)/shard_map/pallas_call | solution.py:264
  189.9 14.5 %all-to-all-done.5 = bf16[64,4,8,128]{3,2,1,0:T(8,128)(2,1)S(1)} async-done(((bf16[64,4,8,128]{3,2,1,0:T(8,128)(2,1)}), bf16[64,4,8,128]{3,2,1,0:T(8,128)(2,1)S(1)}, u32[]{:S(2)}, u32[]{:S(2)}) %all-to-all-start.5) | async-done | bytes 524320 | tf_op jit(solution)/shard_map/all_to_all | solution.py:262
  204.4 1.2 copy-done.1
  205.6 1.7 shard_map.172
  (27 shorter events, 0.7 us)
Async XLA Ops:
  33.9 5.4 %collective-permute-start = (bf16[8,3,64,128]{3,2,1,0:T(8,128)(2,1)S(1)}, bf16[8,3,64,128]{3,2,1,0:T(8,128)(2,1)S(1)}, u32[]{:S(2)}, u32[]{:S(2)}) collective-permute-start(bf16[8,3,64,128]{3,2,1,0:T(8,128)(2,1)S(1)} %all_to_all.30.own), channel_id=1, source_target_pairs={{0,8},{8,0},{1,9},{9,1},{2,10},{10,2},{3,11},{11,3},{4,12},{12,4},... | collective-permute-start | bytes 1179656 | tf_op jit(solution)/shard_map/ppermute | solution.py:159
  39.3 0.9 copy-start.4
  40.2 0.6 copy-start.5
  41.9 25.1 %copy-start.7 = (s32[4,16]{1,0:T(4,128)S(1)}, s32[4,16]{1,0:T(4,128)}, u32[]{:S(2)}) copy-start(s32[4,16]{1,0:T(4,128)} %leaf_fill.1) | copy-start | bytes 772
  41.9 25.0 %copy-start.9 = (s32[2,32]{1,0:T(2,128)S(1)}, s32[2,32]{1,0:T(2,128)}, u32[]{:S(2)}) copy-start(s32[2,32]{1,0:T(2,128)} %mid_fill.1) | copy-start | bytes 772
  41.9 25.0 %copy-start.11 = (s32[64]{0:T(128)S(1)}, s32[64]{0:T(128)}, u32[]{:S(2)}) copy-start(s32[64]{0:T(128)} %root_fill.1) | copy-start | bytes 772
  69.0 27.0 %copy-start.6 = (s32[3]{0:T(128)S(1)}, s32[3]{0:T(128)}, u32[]{:S(2)}) copy-start(s32[3]{0:T(128)} %pad_add_fusion.where) | copy-start | bytes 40
  69.0 27.0 %all-to-all-start.2 = ((bf16[8,3,256,128]{3,2,1,0:T(8,128)(2,1)}), bf16[8,3,256,128]{3,2,1,0:T(8,128)(2,1)S(1)}, u32[]{:S(2)}, u32[]{:S(2)}) async-start(bf16[8,3,256,128]{3,2,1,0:T(8,128)(2,1)} %get-tuple-element.21), calls=%async_computation.2 | async-start | bytes 3145728 | tf_op jit(solution)/shard_map/all_to_all | solution.py:227
  72.7 112.4 %all-gather.2.cloned.1.call-start = ((), (), s32[]{:S(2)}) async-start(), calls=%async_computation.6 | async-start | bytes 2228224 | tf_op jit(solution)/shard_map/all_gather | solution.py:243
  72.8 23.2 %collective-permute-start.1 = (bf16[3,128,128]{2,1,0:T(8,128)(2,1)S(1)}, bf16[3,128,128]{2,1,0:T(8,128)(2,1)S(1)}, u32[]{:S(2)}, u32[]{:S(2)}) collective-permute-start(bf16[3,128,128]{2,1,0:T(8,128)(2,1)S(1)} %get-tuple-element.22), channel_id=1, source_target_pairs={{0,0},{1,8},{2,16},{3,24},{4,32},{5,40},{6,48},{7,56},{8,1},{9,9},... | collective-permute-start | bytes 294920 | tf_op jit(solution)/shard_map/ppermute | solution.py:174
  78.3 17.7 %collective-permute-start.2 = (bf16[3,128,128]{2,1,0:T(8,128)(2,1)S(1)}, bf16[3,128,128]{2,1,0:T(8,128)(2,1)S(1)}, u32[]{:S(2)}, u32[]{:S(2)}) collective-permute-start(bf16[3,128,128]{2,1,0:T(8,128)(2,1)S(1)} %get-tuple-element.23), channel_id=1, source_target_pairs={{0,64},{1,72},{2,80},{3,88},{4,96},{5,104},{6,112},{7,120},{8,65},... | collective-permute-start | bytes 294920 | tf_op jit(solution)/shard_map/ppermute | solution.py:175
  79.6 9.8 %collective-permute-start.3 = (bf16[2,128,128]{2,1,0:T(8,128)(2,1)S(1)}, bf16[2,128,128]{2,1,0:T(8,128)(2,1)S(1)}, u32[]{:S(2)}, u32[]{:S(2)}) collective-permute-start(bf16[2,128,128]{2,1,0:T(8,128)(2,1)S(1)} %get-tuple-element.24), channel_id=1, source_target_pairs={{0,128},{128,0},{1,136},{129,8},{2,144},{130,16},{3,152},{131,24},... | collective-permute-start | bytes 196616 | tf_op jit(solution)/shard_map/ppermute | solution.py:176
  83.6 69.0 %copy-start.2 = (f32[256,512]{1,0:T(8,128)S(1)}, f32[256,512]{1,0:T(8,128)}, u32[]{:S(2)}) copy-start(f32[256,512]{1,0:T(8,128)} %mid_front.1) | copy-start | bytes 1572868
  83.6 69.0 %copy-start.3 = (f32[256,256]{1,0:T(8,128)S(1)}, f32[256,256]{1,0:T(8,128)}, u32[]{:S(2)}) copy-start(f32[256,256]{1,0:T(8,128)} %leaf_front.1) | copy-start | bytes 786436
  83.6 7.2 %collective-permute-start.4 = (bf16[2,128,128]{2,1,0:T(8,128)(2,1)S(1)}, bf16[2,128,128]{2,1,0:T(8,128)(2,1)S(1)}, u32[]{:S(2)}, u32[]{:S(2)}) collective-permute-start(bf16[2,128,128]{2,1,0:T(8,128)(2,1)S(1)} %get-tuple-element.25), channel_id=1, source_target_pairs={{0,192},{128,64},{1,200},{129,72},{2,208},{130,80},{3,216},{131,88... | collective-permute-start | bytes 196616 | tf_op jit(solution)/shard_map/ppermute | solution.py:177
  96.0 56.6 %copy-start = (bf16[8,3,256,128]{3,2,1,0:T(8,128)(2,1)}, bf16[8,3,256,128]{3,2,1,0:T(8,128)(2,1)S(1)}, u32[]{:S(2)}) copy-start(bf16[8,3,256,128]{3,2,1,0:T(8,128)(2,1)S(1)} %all-to-all-done.2.after.factors) | copy-start | bytes 4718596
  96.7 9.0 %collective-permute-start.5 = (bf16[2,128,128]{2,1,0:T(8,128)(2,1)S(1)}, bf16[2,128,128]{2,1,0:T(8,128)(2,1)S(1)}, u32[]{:S(2)}, u32[]{:S(2)}) collective-permute-start(bf16[2,128,128]{2,1,0:T(8,128)(2,1)S(1)} %get-tuple-element.26), channel_id=1, source_target_pairs={{0,256},{256,0},{1,257},{257,1},{2,258},{258,2},{3,259},{259,3},{4... | collective-permute-start | bytes 196616 | tf_op jit(solution)/shard_map/ppermute | solution.py:159
  144.1 32.6 %copy-start.8 = (s32[4,16]{1,0:T(4,128)S(1)}, s32[4,16]{1,0:T(4,128)}, u32[]{:S(2)}) copy-start(s32[4,16]{1,0:T(4,128)} %leaf_map.1) | copy-start | bytes 772
  144.1 32.6 %copy-start.10 = (s32[2,32]{1,0:T(2,128)S(1)}, s32[2,32]{1,0:T(2,128)}, u32[]{:S(2)}) copy-start(s32[2,32]{1,0:T(2,128)} %mid_map.1) | copy-start | bytes 772
  144.1 8.6 %collective-permute-start.6 = (bf16[8,3,128,128]{3,2,1,0:T(8,128)(2,1)S(1)}, bf16[8,3,128,128]{3,2,1,0:T(8,128)(2,1)S(1)}, u32[]{:S(2)}, u32[]{:S(2)}) collective-permute-start(bf16[8,3,128,128]{3,2,1,0:T(8,128)(2,1)S(1)} %all_to_all.32.own), channel_id=1, source_target_pairs={{0,8},{8,0},{1,9},{9,1},{2,10},{10,2},{3,11},{11,3},{4,12},{12,4},... | collective-permute-start | bytes 2359304 | tf_op jit(solution)/shard_map/ppermute | solution.py:159
  178.8 25.6 %all-to-all-start.5 = ((bf16[64,4,8,128]{3,2,1,0:T(8,128)(2,1)}), bf16[64,4,8,128]{3,2,1,0:T(8,128)(2,1)S(1)}, u32[]{:S(2)}, u32[]{:S(2)}) async-start(bf16[64,4,8,128]{3,2,1,0:T(8,128)(2,1)} %shard_map.171), calls=%async_computation.5 | async-start | bytes 1048576 | tf_op jit(solution)/shard_map/all_to_all | solution.py:262
  204.4 1.2 copy-start.1
Sparse Core Ops, SparseCore 0:
  106.5 54.0 all-gather.1

commit v3 on v2

v3 whole, which is shorter than its diff:
```python
import jax
import jax.numpy as jnp
from jax import lax
from jax.experimental import pallas as pl
from jax.experimental.pallas import tpu as pltpu
from jax.sharding import Mesh, PartitionSpec as P

CUBE = ("pair", "half")
ROW = ("z", "core")
COL = ("ylo", "x")
VMEM = pl.BlockSpec(memory_space=pltpu.VMEM)
SMEM = pl.BlockSpec(memory_space=pltpu.SMEM)
BF = jnp.bfloat16
F32 = jnp.float32


def shape(dims, dtype=BF):
    return jax.ShapeDtypeStruct(dims, dtype)


def call(kernel, outs, ins, mebibytes=40, scratch=()):
    tables = sum(1 for value in ins if value.dtype == jnp.int32)
    many = isinstance(outs, tuple)
    return pl.pallas_call(
        kernel,
        out_shape=outs,
        in_specs=[SMEM] * tables + [VMEM] * (len(ins) - tables),
        out_specs=(VMEM,) * len(outs) if many else VMEM,
        scratch_shapes=list(scratch),
        compiler_params=pltpu.CompilerParams(vmem_limit_bytes=mebibytes * 1024 * 1024),
    )(*ins)


def dot_t(left, right):
    return lax.dot_general(left, right, (((1,), (1,)), ((), ())), preferred_element_type=F32)


def inputs_kernel(where, leaf, mid, root, leaf_panel, mid_panel, root_panel, weights, panels):
    weights[0] = leaf[0]
    weights[1] = mid[where[0] // 2]
    weights[2] = root[...]
    panels[0] = leaf_panel[...]
    panels[1] = mid_panel[...]
    panels[2] = root_panel[...]


def fronts_kernel(where, leaf, mid, keep, give):
    first = where[1] % 2 == 0
    for kind in range(3):
        if kind == 0:
            low, high = leaf[:, :128], leaf[:, 128:]
        else:
            at = 256 * (kind - 1)
            low, high = mid[:, at : at + 128], mid[:, at + 128 : at + 256]
        keep[kind] = jnp.where(first, low, high)
        give[kind] = jnp.where(first, high, low)


def factor_kernel(
    where, leaf_fill, mid_fill, root_fill, panels, own, other,
    leaf, mid, root, stack, low, high, rows, weights,
):
    cube, row = where[0], where[1]
    first = row % 2 == 0
    fills = (
        leaf_fill[cube, row],
        mid_fill[cube // 2, 16 * (cube % 2) + row],
        root_fill[16 * cube + row],
    )
    for front, target in enumerate((leaf, mid, root)):
        for at in range(8):
            span = slice(128 * at, 128 * at + 128)
            rows[front, :, span] = panels[at, front]
            mine, theirs = own[at, front], other[at, front]
            weights[front, :64, span] = jnp.where(first, mine, theirs)
            weights[front, 64:, span] = jnp.where(first, theirs, mine)
        total = dot_t(rows[front], weights[front])
        value = (total * fills[front].astype(F32)).astype(BF)
        target[...] = value
        stack[front] = value
        low[front] = value[:128]
        high[front] = value[128:]


def turn_kernel(where, low, high, kept, cross):
    first = where[1] % 2 == 0
    for front in range(3):
        kept[front] = jnp.where(first, low[front], high[front])
    for front in range(2):
        cross[front] = jnp.where(first, low[front + 1], high[front + 1])


def columns_kernel(where, kept, partner, sent, root):
    even = where[0] % 2 == 0
    for to in range(8):
        sent[to, 0] = kept[0]
        sent[to, 1] = jnp.where(even, kept[1], partner[0])
        sent[to, 2] = jnp.where(even, partner[0], kept[1])
    root[0] = jnp.where(even, kept[2], partner[1])
    root[1] = jnp.where(even, partner[1], kept[2])


def update_kernel(
    where, own, other, blocks, own_front, other_front, out, rows, columns
):
    first, column = where[1] % 2 == 0, where[2]
    for at in range(8):
        group = (at + 8 - column) % 8
        span = slice(128 * at, 128 * at + 128)
        for front in range(2):
            mine, theirs = own[group, front], other[group, front]
            rows[front, :256, span] = jnp.where(first, mine, theirs)
            rows[front, 256:, span] = jnp.where(first, theirs, mine)
        for kind in range(3):
            columns[kind, :, span] = blocks[at, kind]
    for kind in range(3):
        product = dot_t(rows[min(kind, 1)], columns[kind])
        mine, theirs = own_front[kind], other_front[kind]
        for block in range(2):
            matrix = jnp.where(first, theirs, mine) if block else jnp.where(first, mine, theirs)
            value = matrix - product[256 * block : 256 * block + 256]
            out[:, block, kind] = value.reshape(32, 8, 128).astype(BF)


def place_kernel(where, leaf_map, mid_map, pieces, out, total):
    column = where[2]
    total[...] = jnp.zeros_like(total)
    for front in range(4):
        pair = front // 2
        slot = mid_map[pair, leaf_map[front, column]] // 16
        for block in range(16):
            target = mid_map[pair, leaf_map[front, block]]
            piece = pieces[8 * front + block // 2, block % 2, 0]
            total[4 * target + slot] += piece.astype(F32)
    for pair in range(2):
        slots = [mid_map[pair, 16 * at + column] // 16 for at in range(2)]
        for block in range(32):
            target = mid_map[pair, block]
            for at in range(2):
                piece = pieces[16 * pair + block // 2, block % 2, 1 + at]
                total[4 * target + slots[at]] += piece.astype(F32)
    out[...] = total[...].reshape(64, 4, 8, 128).astype(BF)


def root_kernel(where, factors, blocks, front, out, rows, columns):
    column = where[2]

    @pl.when(pl.program_id(0) == 0)
    def _():
        for at in range(8):
            rows[:, 128 * at : 128 * at + 128] = factors[(at + 8 - column) % 8, 0]

    for at in range(8):
        span = slice(128 * at, 128 * at + 128)
        columns[:128, span] = blocks[2 * at, 0]
        columns[128:, span] = blocks[2 * at + 1, 0]
    out[...] = front[...] - dot_t(rows[...], columns[...])


def add_kernel(base, arrived, out):
    for side in range(2):
        added = arrived[:, side, 0].astype(F32).reshape(256, 128)
        span = slice(128 * side, 128 * side + 128)
        out[:, span] = base[:, span] + added


def swap(value, axis):
    return lax.ppermute(value, axis, [(0, 1), (1, 0)])


def transpose(low, high):
    pairs = [[], []]
    for r in range(8):
        for c in range(8):
            for half in range(2):
                pairs[half].append((8 * r + c, 8 * (2 * ((c + r) % 8) + half) + r))
    plane = ROW + COL
    return lax.ppermute(low, plane, pairs[0]), lax.ppermute(high, plane, pairs[1])


def turn_weights(value):
    pairs = [(8 * q + c, 8 * (2 * c + q % 2) + q // 2) for q in range(16) for c in range(8)]
    return lax.ppermute(value, ROW + COL, pairs)


def exchange(value, axes):
    return lax.all_to_all(value, axes, 0, 0, tiled=True)


def local(
    leaf_front,
    leaf_panel,
    leaf_inverse,
    leaf_fill,
    mid_front,
    mid_panel,
    mid_inverse,
    mid_fill,
    root_front,
    root_panel,
    root_inverse,
    root_fill,
    leaf_map,
    mid_map,
):
    where = jnp.stack([lax.axis_index(CUBE), lax.axis_index(ROW), lax.axis_index(COL)])
    where = where.astype(jnp.int32)
    piece, one = shape((256, 128)), shape((128, 128))
    two, three = shape((2, 128, 128)), shape((3, 128, 128))

    weights, panels = call(
        inputs_kernel,
        (shape((3, 64, 128)), shape((3, 256, 128))),
        (where, leaf_inverse, mid_inverse, root_inverse, leaf_panel, mid_panel, root_panel),
        60,
    )
    panels = lax.all_gather(panels, COL, axis=0, tiled=False)
    weights = turn_weights(weights)
    own = exchange(jnp.broadcast_to(weights[None], (8, 3, 64, 128)), "z")
    other = swap(own, "core")
    half_front = shape((3, 256, 128), F32)
    own_front, give_front = call(
        fronts_kernel, (half_front, half_front), (where, leaf_front, mid_front)
    )
    other_front = swap(give_front, "core")
    leaf_factor, mid_factor, root_factor, stack, low, high = call(
        factor_kernel,
        (piece, piece, piece, shape((3, 256, 128)), three, three),
        (where, leaf_fill, mid_fill, root_fill, panels, own, other),
        scratch=(pltpu.VMEM((3, 256, 1024), BF), pltpu.VMEM((3, 128, 1024), BF)),
    )

    factors = lax.all_gather(stack, COL, axis=0, tiled=False)
    low, high = transpose(low, high)
    kept, cross = call(turn_kernel, (three, two), (where, low, high))
    partner = swap(cross, "half")
    sent, root_pair = call(
        columns_kernel, (shape((8, 3, 128, 128)), two), (where, kept, partner)
    )
    blocks = exchange(sent, "z")
    factors, blocks = lax.optimization_barrier((factors, blocks))
    root_other = swap(root_pair, "pair")
    root_four = jnp.where(
        lax.axis_index("pair") == 0,
        jnp.concatenate([root_pair, root_other]),
        jnp.concatenate([root_other, root_pair]),
    )
    root_blocks = lax.all_gather(root_four, ROW, axis=0, tiled=False)
    other_factors = swap(factors, "core")
    updates = call(
        update_kernel,
        shape((32, 2, 3, 8, 128)),
        (where, factors, other_factors, blocks, own_front, other_front),
        scratch=(pltpu.VMEM((2, 512, 1024), BF), pltpu.VMEM((3, 128, 1024), BF)),
    )
    pieces = exchange(updates, CUBE + ("z",))
    placed = call(
        place_kernel,
        shape((64, 4, 8, 128)),
        (where, leaf_map, mid_map, pieces),
        scratch=(pltpu.VMEM((256, 8, 128), F32),),
    )
    arrived = exchange(placed, CUBE + ROW)
    spot = pl.BlockSpec((256, 256), lambda s: (0, s))
    limit = pltpu.CompilerParams(vmem_limit_bytes=40 * 1024 * 1024)
    base = pl.pallas_call(
        root_kernel,
        grid=(4,),
        out_shape=shape((256, 1024), F32),
        in_specs=[
            SMEM,
            pl.BlockSpec((8, 1, 256, 128), lambda s: (0, 2, 0, 0)),
            pl.BlockSpec((16, 1, 128, 128), lambda s: (0, s, 0, 0)),
            spot,
        ],
        out_specs=spot,
        scratch_shapes=[pltpu.VMEM((256, 1024), BF), pltpu.VMEM((256, 1024), BF)],
        compiler_params=limit,
        cost_estimate=pl.CostEstimate(flops=2**29, bytes_accessed=2**22, transcendentals=0),
    )(where, factors, root_blocks, root_front)
    root_update = pl.pallas_call(
        add_kernel,
        grid=(4,),
        out_shape=shape((256, 1024), F32),
        in_specs=[spot, pl.BlockSpec((32, 2, 1, 8, 128), lambda s: (0, 0, s, 0, 0))],
        out_specs=spot,
        compiler_params=limit,
    )(base, arrived.reshape(32, 2, 4, 8, 128))
    return leaf_factor, mid_factor, root_factor, root_update


def solution(mesh):
    fine = Mesh(
        mesh.devices.reshape(2, 2, 8, 2, 2, 4), ("pair", "half", "z", "core", "ylo", "x")
    )
    block = P(CUBE + ROW, COL)
    in_specs = (
        block,
        block,
        P(CUBE, ROW, COL),
        P(),
        block,
        block,
        P(None, ROW, COL),
        P(),
        block,
        block,
        P(ROW, COL),
        P(),
        P(),
        P(),
    )
    return jax.shard_map(
        local, mesh=fine, in_specs=in_specs, out_specs=(block,) * 4, check_vma=False
    )
```

time: 215 us -> 190 us (0.88)
  blocking collectives: 110 us -> 51.2 us
  starting transfers between devices: 39.5 us -> 55.5 us
  waiting for transfers between devices: 31.1 us -> 46.9 us
  local copies, waits for them, and re-layouts: 2.77 us -> 5.77 us
    all_to_all x4 -> x2, blocking collectives: 110 us -> 51.2 us  [exchange(): return lax.all_to_all(value, axes, 0, 0, tiled=True)]
    all_to_all x2, waiting for transfers between devices: 14.5 us -> 24.4 us  [exchange(): return lax.all_to_all(value, axes, 0, 0, tiled=True)]
    ppermute x4 -> x3, waiting for transfers between devices: 11 us -> 3.01 us  [the longest x1 3.01 us: transpose(): lax.ppermute(high, plane, pairs[1])]
    all_to_all x2, starting transfers between devices: 9.97 us -> 16.8 us  [exchange(): return lax.all_to_all(value, axes, 0, 0, tiled=True)]
    all_gather x0 -> x2, waiting for transfers between devices: none -> 6.7 us  [the longest x1 6.69 us: local(): panels = lax.all_gather(panels, COL, axis=0, tiled=False)]
    ppermute x4 -> x3, starting transfers between devices: 12.2 us -> 17.4 us  [the longest x1 8.27 us: transpose(): lax.ppermute(high, plane, pairs[1])]
    ppermute x3 -> x5, waiting for transfers between devices: 5.62 us -> 10.5 us  [swap(): return lax.ppermute(value, axis, [(0, 1), (1, 0)])]
    ppermute x3 -> x5, starting transfers between devices: 17.2 us -> 21.2 us  [swap(): return lax.ppermute(value, axis, [(0, 1), (1, 0)])]
  transfers between devices with their start and end apart: 10 -> 13, of which waited for: 7 -> 9; matrix products, arithmetic and copies ran while one was open for 0% -> 0% of each run, Pallas kernels for 4% -> 5%
where the time goes in v3:
time: 190 us; the launch traced here: 189 us
  starting transfers between devices  55.5 us (29%)
  blocking collectives  51.2 us (27%)
  waiting for transfers between devices  46.9 us (25%)
  Pallas kernels  14.5 us (8%)
  between operations  13.9 us (7%)
  local copies, waits for them, and re-layouts  5.77 us (3%)
    all_to_all x2, blocking collectives, exchange(): return lax.all_to_all(value, axes, 0, 0, tiled=True)  51.2 us
    all_to_all x2, waiting for transfers between devices, exchange(): return lax.all_to_all(value, axes, 0, 0, tiled=True)  24.4 us
    ppermute x5, starting transfers between devices, swap(): return lax.ppermute(value, axis, [(0, 1), (1, 0)])  21.2 us
    all_to_all x2, starting transfers between devices, exchange(): return lax.all_to_all(value, axes, 0, 0, tiled=True)  16.8 us
    ppermute x5, waiting for transfers between devices, swap(): return lax.ppermute(value, axis, [(0, 1), (1, 0)])  10.5 us
    pallas_call x7, Pallas kernels, call(): pl.pallas_call(kernel, out_shape=outs, in_specs=[SMEM] * tables + [VMEM]...  10.3 us
    ppermute x1, starting transfers between devices, transpose(): lax.ppermute(high, plane, pairs[1])  8.27 us
    ppermute x1, starting transfers between devices, transpose(): lax.ppermute(low, plane, pairs[0])  7.68 us
  transfers between devices with their start and end apart: 13, of which 9 were waited for; matrix products, arithmetic and copies ran while one was open for 0% of the time, Pallas kernels for 5%

profile of v3, /device:TPU:1, one launch (start us, length us, event | category | flops | bytes accessed | tf_op | source)
XLA Modules:
  0.0 189.2 jit_solution(14402886630222596809)
XLA Ops:
  7.9 1.7 shard_map.165
  9.7 1.5 collective-permute-start
  11.2 31.2 %all_to_all.20.own = bf16[8,3,64,128]{3,2,1,0:T(8,128)(2,1)S(1)} all-to-all(bf16[8,3,64,128]{3,2,1,0:T(8,128)(2,1)S(1)} %broadcast_in_dim.2), channel_id=1, replica_groups=mesh['pair'=2,'half'=2,'z'=8,'core'=2,'ylo'=2,'x'=4] {'z'}, dimensions={0} | all-to-all | bytes 786432 | tf_op jit(solution)/shard_map/all_to_all | solution.py:187
  42.4 6.3 %collective-permute-start.1 = (bf16[8,3,64,128]{3,2,1,0:T(8,128)(2,1)S(1)}, bf16[8,3,64,128]{3,2,1,0:T(8,128)(2,1)S(1)}, u32[]{:S(2)}, u32[]{:S(2)}) collective-permute-start(bf16[8,3,64,128]{3,2,1,0:T(8,128)(2,1)S(1)} %all_to_all.20.own), channel_id=1, source_target_pairs={{0,8},{8,0},{1,9},{9,1},{2,10},{10,2},{3,11},{11,3},{4,12},{12,4},... | collective-permute-start | bytes 1179656 | tf_op jit(solution)/shard_map/ppermute | solution.py:168
  48.7 1.3 collective-permute-done.1.other
  50.0 6.7 %all-gather.8.cloned.1.call-done = bf16[24,256,128]{2,1,0:T(8,128)(2,1)} async-done(((bf16[3,256,128]{2,1,0:T(8,128)(2,1)}), bf16[24,256,128]{2,1,0:T(8,128)(2,1)}) %all-gather.8.cloned.1.call-update) | async-done | bytes 1572880 | tf_op jit(solution)/shard_map/all_gather | solution.py:217
  56.7 1.4 copy-done.3
  58.1 2.0 %shard_map.166 = (bf16[256,128]{1,0:T(8,128)(2,1)}, bf16[256,128]{1,0:T(8,128)(2,1)}, bf16[256,128]{1,0:T(8,128)(2,1)}, bf16[3,256,128]{2,1,0:T(8,128)(2,1)}, bf...) custom-call(s32[3]{0:T(128)S(1)} %copy-done.7, s32[4,16]{1,0:T(4,128)S(1)} %copy-done.8, ...), custom_call_target="tpu_custom_call" | custom-call | tf_op jit(solution)/shard_map/pallas_call | solution.py:24
  60.2 7.7 %collective-permute-start.2 = (bf16[3,128,128]{2,1,0:T(8,128)(2,1)S(1)}, bf16[3,128,128]{2,1,0:T(8,128)(2,1)S(1)}, u32[]{:S(2)}, u32[]{:S(2)}) collective-permute-start(bf16[3,128,128]{2,1,0:T(8,128)(2,1)S(1)} %get-tuple-element.26), channel_id=1, source_target_pairs={{0,0},{1,16},{2,32},{3,48},{4,64},{5,80},{6,96},{7,112},{8,17},{9,... | collective-permute-start | bytes 294920 | tf_op jit(solution)/shard_map/ppermute | solution.py:178
  67.9 8.3 %collective-permute-start.3 = (bf16[3,128,128]{2,1,0:T(8,128)(2,1)S(1)}, bf16[3,128,128]{2,1,0:T(8,128)(2,1)S(1)}, u32[]{:S(2)}, u32[]{:S(2)}) collective-permute-start(bf16[3,128,128]{2,1,0:T(8,128)(2,1)S(1)} %get-tuple-element.27), channel_id=1, source_target_pairs={{0,8},{1,24},{2,40},{3,56},{4,72},{5,88},{6,104},{7,120},{8,25},{9... | collective-permute-start | bytes 294920 | tf_op jit(solution)/shard_map/ppermute | solution.py:178
  76.2 3.0 %collective-permute-done.3.high = bf16[3,128,128]{2,1,0:T(8,128)(2,1)S(1)} collective-permute-done((bf16[3,128,128]{2,1,0:T(8,128)(2,1)S(1)}, bf16[3,128,128]{2,1,0:T(8,128)(2,1)S(1)}, u32[]{:S(2)}, u32[]{:S(2)}) %collective-permute-start.3) | collective-permute-done | bytes 98336 | tf_op jit(solution)/shard_map/ppermute | solution.py:178
  79.8 4.1 %collective-permute-start.4 = (bf16[2,128,128]{2,1,0:T(8,128)(2,1)S(1)}, bf16[2,128,128]{2,1,0:T(8,128)(2,1)S(1)}, u32[]{:S(2)}, u32[]{:S(2)}) collective-permute-start(bf16[2,128,128]{2,1,0:T(8,128)(2,1)S(1)} %get-tuple-element.29), channel_id=1, source_target_pairs={{0,128},{128,0},{1,129},{129,1},{2,130},{130,2},{3,131},{131,3},{4... | collective-permute-start | bytes 196616 | tf_op jit(solution)/shard_map/ppermute | solution.py:168
  83.9 3.6 %collective-permute-done.4.partner = bf16[2,128,128]{2,1,0:T(8,128)(2,1)S(1)} collective-permute-done((bf16[2,128,128]{2,1,0:T(8,128)(2,1)S(1)}, bf16[2,128,128]{2,1,0:T(8,128)(2,1)S(1)}, u32[]{:S(2)}, u32[]{:S(2)}) %collective-permute-start.4) | collective-permute-done | bytes 65568 | tf_op jit(solution)/shard_map/ppermute | solution.py:168
  87.5 1.5 shard_map.168
  89.0 7.1 %all-to-all-start.1 = ((bf16[8,3,128,128]{3,2,1,0:T(8,128)(2,1)}), bf16[8,3,128,128]{3,2,1,0:T(8,128)(2,1)S(1)}, u32[]{:S(2)}, u32[]{:S(2)}) async-start(bf16[8,3,128,128]{3,2,1,0:T(8,128)(2,1)} %get-tuple-element.30), calls=%async_computation.1 | async-start | bytes 1572864 | tf_op jit(solution)/shard_map/all_to_all | solution.py:187
  96.2 6.5 %collective-permute-start.5 = (bf16[2,128,128]{2,1,0:T(8,128)(2,1)S(1)}, bf16[2,128,128]{2,1,0:T(8,128)(2,1)S(1)}, u32[]{:S(2)}, u32[]{:S(2)}) collective-permute-start(bf16[2,128,128]{2,1,0:T(8,128)(2,1)S(1)} %get-tuple-element.32), channel_id=1, source_target_pairs={{0,256},{256,0},{1,257},{257,1},{2,258},{258,2},{3,259},{259,3},{4... | collective-permute-start | bytes 196616 | tf_op jit(solution)/shard_map/ppermute | solution.py:168
  102.7 3.9 %collective-permute-done.5 = bf16[2,128,128]{2,1,0:T(8,128)(2,1)S(1)} collective-permute-done((bf16[2,128,128]{2,1,0:T(8,128)(2,1)S(1)}, bf16[2,128,128]{2,1,0:T(8,128)(2,1)S(1)}, u32[]{:S(2)}, u32[]{:S(2)}) %collective-permute-start.5) | collective-permute-done | bytes 65568 | tf_op jit(solution)/shard_map/ppermute | solution.py:168
  107.2 12.4 %all-to-all-done.1.blocks = bf16[8,3,128,128]{3,2,1,0:T(8,128)(2,1)S(1)} async-done(((bf16[8,3,128,128]{3,2,1,0:T(8,128)(2,1)}), bf16[8,3,128,128]{3,2,1,0:T(8,128)(2,1)S(1)}, u32[]{:S(2)}, u32[]{:S(2)}) %all-to-all-start.1) | async-done | bytes 786464 | tf_op jit(solution)/shard_map/all_to_all | solution.py:187
  119.7 2.4 %collective-permute-start.6 = (bf16[8,3,256,128]{3,2,1,0:T(8,128)(2,1)}, bf16[8,3,256,128]{3,2,1,0:T(8,128)(2,1)S(1)}, u32[]{:S(2)}, u32[]{:S(2)}) collective-permute-start(bf16[8,3,256,128]{3,2,1,0:T(8,128)(2,1)} %bitcast.8), channel_id=1, source_target_pairs={{0,8},{8,0},{1,9},{9,1},{2,10},{10,2},{3,11},{11,3},{4,12},{12,4},... | collective-permute-start | bytes 4718600 | tf_op jit(solution)/shard_map/ppermute | solution.py:168
  122.7 1.9 %collective-permute-start.7 = (f32[3,256,128]{2,1,0:T(8,128)S(1)}, f32[3,256,128]{2,1,0:T(8,128)S(1)}, u32[]{:S(2)}, u32[]{:S(2)}) collective-permute-start(f32[3,256,128]{2,1,0:T(8,128)S(1)} %get-tuple-element.35), channel_id=1, source_target_pairs={{0,8},{8,0},{1,9},{9,1},{2,10},{10,2},{3,11},{11,3},{4,12},{12,4},... | collective-permute-start | bytes 1179656 | tf_op jit(solution)/shard_map/ppermute | solution.py:168
  124.7 1.7 collective-permute-done.7.other_front
  126.3 1.4 copy-done
  127.8 1.7 shard_map.171
  129.5 20.0 %all_to_all.21.pieces = bf16[32,2,3,8,128]{4,3,2,1,0:T(8,128)(2,1)S(1)} all-to-all(bf16[32,2,3,8,128]{4,3,2,1,0:T(8,128)(2,1)S(1)} %shard_map.171), channel_id=1, replica_groups=mesh['pair'=2,'half'=2,'z'=8,'core'=2,'ylo'=2,'x'=4] {'pair','half','z'}, dimensions={0} | all-to-all | bytes 786432 | tf_op jit(solution)/shard_map/all_to_all | solution.py:187
  149.5 2.2 %shard_map.172 = bf16[64,4,8,128]{3,2,1,0:T(8,128)(2,1)} custom-call(s32[3]{0:T(128)S(1)} %copy-done.7, s32[4,16]{1,0:T(4,128)S(1)} %copy-done.9, s32[2,32]{1,0:T(2,128)S(1)} %copy-done.11, bf16[32,2,3,8,128]{4,3,2,1,0:T(8,128)(2,1)S(1)} %all_to_all.21.pieces), custom_call_target="tpu_custom_call" | custom-call | tf_op jit(solution)/shard_map/pallas_call | solution.py:24
  151.7 9.8 %all-to-all-start.3 = ((bf16[64,4,8,128]{3,2,1,0:T(8,128)(2,1)}), bf16[64,4,8,128]{3,2,1,0:T(8,128)(2,1)S(1)}, u32[]{:S(2)}, u32[]{:S(2)}) async-start(bf16[64,4,8,128]{3,2,1,0:T(8,128)(2,1)} %shard_map.172), calls=%async_computation.3 | async-start | bytes 1048576 | tf_op jit(solution)/shard_map/all_to_all | solution.py:187
  161.4 2.2 %all-gather.6.cloned.1.call-done.blocks = bf16[16,4,128,128]{3,2,1,0:T(8,128)(2,1)} async-done(((bf16[1,4,128,128]{3,2,1,0:T(8,128)(2,1)}), bf16[16,4,128,128]{3,2,1,0:T(8,128)(2,1)}) %all-gather.6.cloned.1.call-update) | async-done | bytes 2097168 | tf_op jit(solution)/shard_map/all_gather | solution.py:248
  163.7 1.6 copy-done.2
  165.3 1.2 copy-done.4
  166.5 2.5 %shard_map.169.base = f32[256,1024]{1,0:T(8,128)S(1)} custom-call(s32[3]{0:T(128)S(1)} %copy-done.7, bf16[8,3,256,128]{3,2,1,0:T(8,128)(2,1)S(1)} %bitcast.10, bf16[16,4,128,128]{3,2,1,0:T(8,128)(2,1)S(1)} %copy-done.2, f32[256,1024]{1,0:T(8,128)S(1)} %copy-done.4), custom_call_target="tpu_custom_call" | custom-call | flops 536870912 | bytes 4194304 | tf_op jit(solution)/shard_map/pallas_call | solution.py:266
  169.0 12.0 %all-to-all-done.3 = bf16[64,4,8,128]{3,2,1,0:T(8,128)(2,1)S(1)} async-done(((bf16[64,4,8,128]{3,2,1,0:T(8,128)(2,1)}), bf16[64,4,8,128]{3,2,1,0:T(8,128)(2,1)S(1)}, u32[]{:S(2)}, u32[]{:S(2)}) %all-to-all-start.3) | async-done | bytes 524320 | tf_op jit(solution)/shard_map/all_to_all | solution.py:187
  181.0 1.7 shard_map.173
  (37 shorter events, 2.8 us)
Async XLA Ops:
  7.2 49.6 %copy-start.8 = (s32[4,16]{1,0:T(4,128)S(1)}, s32[4,16]{1,0:T(4,128)}, u32[]{:S(2)}) copy-start(s32[4,16]{1,0:T(4,128)} %leaf_fill.1) | copy-start | bytes 772
  7.2 49.6 %copy-start.10 = (s32[2,32]{1,0:T(2,128)S(1)}, s32[2,32]{1,0:T(2,128)}, u32[]{:S(2)}) copy-start(s32[2,32]{1,0:T(2,128)} %mid_fill.1) | copy-start | bytes 772
  7.2 49.5 %copy-start.12 = (s32[64]{0:T(128)S(1)}, s32[64]{0:T(128)}, u32[]{:S(2)}) copy-start(s32[64]{0:T(128)} %root_fill.1) | copy-start | bytes 772
  7.2 49.5 %all-gather.8.cloned.1.call-start = ((), (), s32[]{:S(2)}) async-start(), calls=%async_computation.5 | async-start | bytes 1769472 | tf_op jit(solution)/shard_map/all_gather | solution.py:217
  7.9 48.8 %copy-start.7 = (s32[3]{0:T(128)S(1)}, s32[3]{0:T(128)}, u32[]{:S(2)}) copy-start(s32[3]{0:T(128)} %pad_add_fusion.where) | copy-start | bytes 40
  9.6 110.1 %all-gather.10.cloned.1.call-start = ((), (), s32[]{:S(2)}) async-start(), calls=%async_computation.6 | async-start | bytes 1769472 | tf_op jit(solution)/shard_map/all_gather | solution.py:233
  9.7 1.5 collective-permute-start
  42.4 7.6 %collective-permute-start.1 = (bf16[8,3,64,128]{3,2,1,0:T(8,128)(2,1)S(1)}, bf16[8,3,64,128]{3,2,1,0:T(8,128)(2,1)S(1)}, u32[]{:S(2)}, u32[]{:S(2)}) collective-permute-start(bf16[8,3,64,128]{3,2,1,0:T(8,128)(2,1)S(1)} %all_to_all.20.own), channel_id=1, source_target_pairs={{0,8},{8,0},{1,9},{9,1},{2,10},{10,2},{3,11},{11,3},{4,12},{12,4},... | collective-permute-start | bytes 1179656 | tf_op jit(solution)/shard_map/ppermute | solution.py:168
  56.7 1.4 copy-start.3
  60.2 61.9 %copy-start.5 = (f32[256,512]{1,0:T(8,128)S(1)}, f32[256,512]{1,0:T(8,128)}, u32[]{:S(2)}) copy-start(f32[256,512]{1,0:T(8,128)} %mid.3) | copy-start | bytes 1572868
  60.2 61.9 %copy-start.6 = (f32[256,256]{1,0:T(8,128)S(1)}, f32[256,256]{1,0:T(8,128)}, u32[]{:S(2)}) copy-start(f32[256,256]{1,0:T(8,128)} %leaf.3) | copy-start | bytes 786436
  60.2 16.0 %collective-permute-start.2 = (bf16[3,128,128]{2,1,0:T(8,128)(2,1)S(1)}, bf16[3,128,128]{2,1,0:T(8,128)(2,1)S(1)}, u32[]{:S(2)}, u32[]{:S(2)}) collective-permute-start(bf16[3,128,128]{2,1,0:T(8,128)(2,1)S(1)} %get-tuple-element.26), channel_id=1, source_target_pairs={{0,0},{1,16},{2,32},{3,48},{4,64},{5,80},{6,96},{7,112},{8,17},{9,... | collective-permute-start | bytes 294920 | tf_op jit(solution)/shard_map/ppermute | solution.py:178
  67.9 11.3 %collective-permute-start.3 = (bf16[3,128,128]{2,1,0:T(8,128)(2,1)S(1)}, bf16[3,128,128]{2,1,0:T(8,128)(2,1)S(1)}, u32[]{:S(2)}, u32[]{:S(2)}) collective-permute-start(bf16[3,128,128]{2,1,0:T(8,128)(2,1)S(1)} %get-tuple-element.27), channel_id=1, source_target_pairs={{0,8},{1,24},{2,40},{3,56},{4,72},{5,88},{6,104},{7,120},{8,25},{9... | collective-permute-start | bytes 294920 | tf_op jit(solution)/shard_map/ppermute | solution.py:178
  79.8 7.7 %collective-permute-start.4 = (bf16[2,128,128]{2,1,0:T(8,128)(2,1)S(1)}, bf16[2,128,128]{2,1,0:T(8,128)(2,1)S(1)}, u32[]{:S(2)}, u32[]{:S(2)}) collective-permute-start(bf16[2,128,128]{2,1,0:T(8,128)(2,1)S(1)} %get-tuple-element.29), channel_id=1, source_target_pairs={{0,128},{128,0},{1,129},{129,1},{2,130},{130,2},{3,131},{131,3},{4... | collective-permute-start | bytes 196616 | tf_op jit(solution)/shard_map/ppermute | solution.py:168
  89.0 30.7 %all-to-all-start.1 = ((bf16[8,3,128,128]{3,2,1,0:T(8,128)(2,1)}), bf16[8,3,128,128]{3,2,1,0:T(8,128)(2,1)S(1)}, u32[]{:S(2)}, u32[]{:S(2)}) async-start(bf16[8,3,128,128]{3,2,1,0:T(8,128)(2,1)} %get-tuple-element.30), calls=%async_computation.1 | async-start | bytes 1572864 | tf_op jit(solution)/shard_map/all_to_all | solution.py:187
  96.1 67.5 %all-gather.6.cloned.1.call-start = ((), (), s32[]{:S(2)}) async-start(), calls=%async_computation.4 | async-start | bytes 2228224 | tf_op jit(solution)/shard_map/all_gather | solution.py:248
  96.2 10.4 %collective-permute-start.5 = (bf16[2,128,128]{2,1,0:T(8,128)(2,1)S(1)}, bf16[2,128,128]{2,1,0:T(8,128)(2,1)S(1)}, u32[]{:S(2)}, u32[]{:S(2)}) collective-permute-start(bf16[2,128,128]{2,1,0:T(8,128)(2,1)S(1)} %get-tuple-element.32), channel_id=1, source_target_pairs={{0,256},{256,0},{1,257},{257,1},{2,258},{258,2},{3,259},{259,3},{4... | collective-permute-start | bytes 196616 | tf_op jit(solution)/shard_map/ppermute | solution.py:168
  119.7 6.7 %collective-permute-start.6 = (bf16[8,3,256,128]{3,2,1,0:T(8,128)(2,1)}, bf16[8,3,256,128]{3,2,1,0:T(8,128)(2,1)S(1)}, u32[]{:S(2)}, u32[]{:S(2)}) collective-permute-start(bf16[8,3,256,128]{3,2,1,0:T(8,128)(2,1)} %bitcast.8), channel_id=1, source_target_pairs={{0,8},{8,0},{1,9},{9,1},{2,10},{10,2},{3,11},{11,3},{4,12},{12,4},... | collective-permute-start | bytes 4718600 | tf_op jit(solution)/shard_map/ppermute | solution.py:168
  122.7 3.6 %collective-permute-start.7 = (f32[3,256,128]{2,1,0:T(8,128)S(1)}, f32[3,256,128]{2,1,0:T(8,128)S(1)}, u32[]{:S(2)}, u32[]{:S(2)}) collective-permute-start(f32[3,256,128]{2,1,0:T(8,128)S(1)} %get-tuple-element.35), channel_id=1, source_target_pairs={{0,8},{8,0},{1,9},{9,1},{2,10},{10,2},{3,11},{11,3},{4,12},{12,4},... | collective-permute-start | bytes 1179656 | tf_op jit(solution)/shard_map/ppermute | solution.py:168
  126.3 1.4 copy-start
  127.8 21.7 %copy-start.9 = (s32[4,16]{1,0:T(4,128)S(1)}, s32[4,16]{1,0:T(4,128)}, u32[]{:S(2)}) copy-start(s32[4,16]{1,0:T(4,128)} %leaf_map.1) | copy-start | bytes 772
  127.8 21.7 %copy-start.11 = (s32[2,32]{1,0:T(2,128)S(1)}, s32[2,32]{1,0:T(2,128)}, u32[]{:S(2)}) copy-start(s32[2,32]{1,0:T(2,128)} %mid_map.1) | copy-start | bytes 772
  129.5 34.1 %copy-start.1 = (bf16[24,256,128]{2,1,0:T(8,128)(2,1)S(1)}, bf16[24,256,128]{2,1,0:T(8,128)(2,1)}, u32[]{:S(2)}) copy-start(bf16[24,256,128]{2,1,0:T(8,128)(2,1)} %all-gather.10.cloned.1.call-done) | copy-start | bytes 4718596
  151.7 29.3 %all-to-all-start.3 = ((bf16[64,4,8,128]{3,2,1,0:T(8,128)(2,1)}), bf16[64,4,8,128]{3,2,1,0:T(8,128)(2,1)S(1)}, u32[]{:S(2)}, u32[]{:S(2)}) async-start(bf16[64,4,8,128]{3,2,1,0:T(8,128)(2,1)} %shard_map.172), calls=%async_computation.3 | async-start | bytes 1048576 | tf_op jit(solution)/shard_map/all_to_all | solution.py:187
  163.7 1.6 copy-start.2
  165.3 1.2 copy-start.4
Sparse Core Ops, SparseCore 0:
  10.7 45.9 all-gather.7
  60.3 46.8 all-gather.9
  109.4 54.2 all-gather.5

commit v4 on v3

v4 whole, which is shorter than its diff:
```python
import jax
import jax.numpy as jnp
from jax import lax
from jax.experimental import pallas as pl
from jax.experimental.pallas import tpu as pltpu
from jax.sharding import Mesh, PartitionSpec as P

CUBE = ("pair", "half")
ROW = ("z", "core")
COL = ("ylo", "x")
VMEM = pl.BlockSpec(memory_space=pltpu.VMEM)
SMEM = pl.BlockSpec(memory_space=pltpu.SMEM)
BF = jnp.bfloat16
F32 = jnp.float32


def shape(dims, dtype=BF):
    return jax.ShapeDtypeStruct(dims, dtype)


def call(kernel, outs, ins, mebibytes=40, scratch=()):
    tables = sum(1 for value in ins if value.dtype == jnp.int32)
    many = isinstance(outs, tuple)
    return pl.pallas_call(
        kernel,
        out_shape=outs,
        in_specs=[SMEM] * tables + [VMEM] * (len(ins) - tables),
        out_specs=(VMEM,) * len(outs) if many else VMEM,
        scratch_shapes=list(scratch),
        compiler_params=pltpu.CompilerParams(vmem_limit_bytes=mebibytes * 1024 * 1024),
    )(*ins)


def dot_t(left, right):
    return lax.dot_general(left, right, (((1,), (1,)), ((), ())), preferred_element_type=F32)


def inputs_kernel(
    where, leaf, mid, root, leaf_panel, mid_panel, root_panel, weights, panels, low, high
):
    for to in range(8):
        weights[to, 0] = leaf[0]
        weights[to, 1] = mid[where[0] // 2]
        weights[to, 2] = root[...]
    for front, panel in enumerate((leaf_panel, mid_panel, root_panel)):
        panels[front] = panel[...]
        low[front] = panel[:128]
        high[front] = panel[128:]


def fronts_kernel(where, leaf, mid, keep, give):
    first = where[1] % 2 == 0
    for kind in range(3):
        if kind == 0:
            low, high = leaf[:, :128], leaf[:, 128:]
        else:
            at = 256 * (kind - 1)
            low, high = mid[:, at : at + 128], mid[:, at + 128 : at + 256]
        keep[kind] = jnp.where(first, low, high)
        give[kind] = jnp.where(first, high, low)


def whole_kernel(
    where, weights, panels, low, high, whole, root, kept, cross, last, spread
):
    first = where[1] % 2 == 0
    for front in range(2):
        for at in range(8):
            whole[front, :, 128 * at : 128 * at + 128] = weights[at, front]
    for at in range(8):
        root[at] = weights[at, 2]
        spread[at] = panels[...]
    for front in range(3):
        kept[front] = jnp.where(first, low[front], high[front])
    for front in range(2):
        cross[front] = jnp.where(first, low[front + 1], high[front + 1])
    last[...] = kept[2]


def columns_kernel(
    where, kept, partner, across, corner, weights, panels, sent, joined, give
):
    cube = where[0]
    even = cube % 2 == 0
    for to in range(8):
        sent[to, 0] = kept[0]
        sent[to, 1] = jnp.where(even, kept[1], partner[0])
        sent[to, 2] = jnp.where(even, partner[0], kept[1])
    joined[:8] = weights[...]
    for slot in range(4):
        same_half, same_pair = cube % 2 == slot % 2, cube // 2 == slot // 2
        piece = jnp.where(
            same_pair,
            jnp.where(same_half, kept[2], partner[1]),
            jnp.where(same_half, across[...], corner[...]),
        )
        for half in range(2):
            joined[8 + 2 * slot + half] = piece[64 * half : 64 * half + 64]
    give[...] = panels[:, :2]


def update_kernel(
    where, leaf_fill, mid_fill, weights, own, other, blocks, own_front, other_front,
    out, leaf_factor, mid_factor, panel, factor,
):
    cube, row, column = where[0], where[1], where[2]
    first = row % 2 == 0
    upper = row - row % 2
    mine_at = pl.ds(pl.multiple_of(128 * column, 128), 128)
    for front, target in enumerate((leaf_factor, mid_factor)):
        if front == 0:
            fills = [leaf_fill[cube, upper], leaf_fill[cube, upper + 1], leaf_fill[cube, column]]
        else:
            pair, base = cube // 2, 16 * (cube % 2) + upper
            fills = [mid_fill[pair, base], mid_fill[pair, base + 1]]
            fills += [mid_fill[pair, column], mid_fill[pair, 16 + column]]
        height = 640 + 128 * front
        for at in range(8):
            span = slice(128 * at, 128 * at + 128)
            mine, theirs = own[at, front], other[at, front]
            panel[:256, span] = jnp.where(first, mine, theirs)
            panel[256:512, span] = jnp.where(first, theirs, mine)
            for kind in range(1 + front):
                piece = blocks[(at + column) % 8, kind + front]
                panel[512 + 128 * kind : 640 + 128 * kind, span] = piece
        for at in range(0, 16, 4):
            rows = weights[at : at + 4, front].reshape(256, 1024)
            part = dot_t(panel[:height], rows)
            span = slice(64 * at, 64 * at + 256)
            for index, fill in enumerate(fills):
                low = 256 * index if index < 2 else 128 * index + 256
                high = low + 256 if index < 2 else low + 128
                value = part[low:high] * fill.astype(F32)
                factor[low:high, span] = value.astype(BF)
        target[...] = jnp.where(first, factor[:256, mine_at], factor[256:512, mine_at])
        for kind in range(1 + front):
            at = kind + front
            product = dot_t(factor[:512], factor[512 + 128 * kind : 640 + 128 * kind])
            mine, theirs = own_front[at], other_front[at]
            for block in range(2):
                matrix = jnp.where(first, theirs, mine) if block else jnp.where(first, mine, theirs)
                value = matrix - product[256 * block : 256 * block + 256]
                out[:, block, at] = value.reshape(32, 8, 128).astype(BF)


def place_kernel(where, leaf_map, mid_map, pieces, out, total):
    column = where[2]
    total[...] = jnp.zeros_like(total)
    for front in range(4):
        pair = front // 2
        slot = mid_map[pair, leaf_map[front, column]] // 16
        for block in range(16):
            target = mid_map[pair, leaf_map[front, block]]
            piece = pieces[8 * front + block // 2, block % 2, 0]
            total[4 * target + slot] += piece.astype(F32)
    for pair in range(2):
        slots = [mid_map[pair, 16 * at + column] // 16 for at in range(2)]
        for block in range(32):
            target = mid_map[pair, block]
            for at in range(2):
                piece = pieces[16 * pair + block // 2, block % 2, 1 + at]
                total[4 * target + slots[at]] += piece.astype(F32)
    out[...] = total[...].reshape(64, 4, 8, 128).astype(BF)


def root_kernel(
    where, fill, panels, joined, front, out, root_factor, weights, panel, rows, columns
):
    cube, row, column = where[0], where[1], where[2]
    slot = pl.program_id(0)

    @pl.when(slot == 0)
    def _():
        for at in range(8):
            span = slice(128 * at, 128 * at + 128)
            panel[:, span] = panels[at, 0]
            for owner in range(16):
                weights[64 * owner : 64 * owner + 64, span] = joined[owner, at]
        for at in range(0, 1024, 256):
            part = dot_t(panel[...], weights[at : at + 256])
            rows[:, at : at + 256] = (part * fill[16 * cube + row].astype(F32)).astype(BF)
        root_factor[...] = rows[:, pl.ds(pl.multiple_of(128 * column, 128), 128)]

    for half in range(2):
        for at in range(8):
            owner = 2 * ((at + column) % 8) + half
            piece = joined[owner, pl.ds(8 + 2 * slot, 2)].reshape(128, 128)
            panel[128 * half : 128 * half + 128, 128 * at : 128 * at + 128] = piece
    for at in range(0, 1024, 256):
        part = dot_t(panel[...], weights[at : at + 256])
        columns[:, at : at + 256] = (part * fill[16 * slot + column].astype(F32)).astype(BF)
    out[...] = front[...] - dot_t(rows[...], columns[...])


def add_kernel(base, arrived, out):
    for side in range(2):
        added = arrived[:, side, 0].astype(F32).reshape(256, 128)
        span = slice(128 * side, 128 * side + 128)
        out[:, span] = base[:, span] + added


def swap(value, axis):
    return lax.ppermute(value, axis, [(0, 1), (1, 0)])


def transpose(low, high):
    pairs = [[], []]
    for r in range(8):
        for c in range(8):
            for half in range(2):
                pairs[half].append((8 * r + c, 8 * (2 * ((c + r) % 8) + half) + r))
    plane = ROW + COL
    return lax.ppermute(low, plane, pairs[0]), lax.ppermute(high, plane, pairs[1])


def exchange(value, axes):
    return lax.all_to_all(value, axes, 0, 0, tiled=True)


def local(
    leaf_front,
    leaf_panel,
    leaf_inverse,
    leaf_fill,
    mid_front,
    mid_panel,
    mid_inverse,
    mid_fill,
    root_front,
    root_panel,
    root_inverse,
    root_fill,
    leaf_map,
    mid_map,
):
    where = jnp.stack([lax.axis_index(CUBE), lax.axis_index(ROW), lax.axis_index(COL)])
    where = where.astype(jnp.int32)
    piece = shape((256, 128))
    two, three = shape((2, 128, 128)), shape((3, 128, 128))
    panel_three, panel_all = shape((3, 256, 128)), shape((8, 3, 256, 128))

    weights, panels, low, high = call(
        inputs_kernel,
        (shape((8, 3, 64, 128)), panel_three, three, three),
        (where, leaf_inverse, mid_inverse, root_inverse, leaf_panel, mid_panel, root_panel),
        60,
    )
    low, high = transpose(low, high)
    weights = exchange(weights, COL)
    whole, root_weights, kept, cross, last, spread = call(
        whole_kernel,
        (shape((2, 64, 1024)), shape((8, 64, 128)), three, two, shape((128, 128)), panel_all),
        (where, weights, panels, low, high),
    )
    weights = lax.all_gather(whole, ROW, axis=0, tiled=False)
    partner = swap(cross, "half")
    across = swap(last, "pair")
    corner = lax.ppermute(last, CUBE, [(0, 3), (1, 2), (2, 1), (3, 0)])
    panels = exchange(spread, COL)
    sent, joined, give = call(
        columns_kernel,
        (shape((8, 3, 128, 128)), shape((16, 64, 128)), shape((8, 2, 256, 128))),
        (where, kept, partner, across, corner, root_weights, panels),
    )
    joined = lax.all_gather(joined, ROW, axis=0, tiled=False)
    other_panels = swap(give, "core")
    half_front = shape((3, 256, 128), F32)
    own_front, give_front = call(
        fronts_kernel, (half_front, half_front), (where, leaf_front, mid_front)
    )
    other_front = swap(give_front, "core")
    blocks = exchange(sent, "z")
    blocks, other_panels, other_front = lax.optimization_barrier(
        (blocks, other_panels, other_front)
    )
    updates, leaf_factor, mid_factor = call(
        update_kernel,
        (shape((32, 2, 3, 8, 128)), piece, piece),
        (where, leaf_fill, mid_fill, weights, panels, other_panels, blocks, own_front, other_front),
        scratch=(pltpu.VMEM((768, 1024), BF), pltpu.VMEM((768, 1024), BF)),
    )
    pieces = exchange(updates, CUBE + ("z",))
    placed = call(
        place_kernel,
        shape((64, 4, 8, 128)),
        (where, leaf_map, mid_map, pieces),
        scratch=(pltpu.VMEM((256, 8, 128), F32),),
    )
    arrived = exchange(placed, CUBE + ROW)
    spot = pl.BlockSpec((256, 256), lambda s: (0, s))
    limit = pltpu.CompilerParams(vmem_limit_bytes=40 * 1024 * 1024)
    base, root_factor = pl.pallas_call(
        root_kernel,
        grid=(4,),
        out_shape=(shape((256, 1024), F32), piece),
        in_specs=[
            SMEM,
            SMEM,
            pl.BlockSpec((8, 1, 256, 128), lambda s: (0, 2, 0, 0)),
            pl.BlockSpec((16, 16, 64, 128), lambda s: (0, 0, 0, 0)),
            spot,
        ],
        out_specs=(spot, pl.BlockSpec((256, 128), lambda s: (0, 0))),
        scratch_shapes=[
            pltpu.VMEM((1024, 1024), BF),
            pltpu.VMEM((256, 1024), BF),
            pltpu.VMEM((256, 1024), BF),
            pltpu.VMEM((256, 1024), BF),
        ],
        compiler_params=limit,
        cost_estimate=pl.CostEstimate(flops=2**32, bytes_accessed=2**23, transcendentals=0),
    )(where, root_fill, panels, joined, root_front)
    root_update = pl.pallas_call(
        add_kernel,
        grid=(4,),
        out_shape=shape((256, 1024), F32),
        in_specs=[spot, pl.BlockSpec((32, 2, 1, 8, 128), lambda s: (0, 0, s, 0, 0))],
        out_specs=spot,
        compiler_params=limit,
    )(base, arrived.reshape(32, 2, 4, 8, 128))
    return leaf_factor, mid_factor, root_factor, root_update


def solution(mesh):
    fine = Mesh(
        mesh.devices.reshape(2, 2, 8, 2, 2, 4), ("pair", "half", "z", "core", "ylo", "x")
    )
    block = P(CUBE + ROW, COL)
    in_specs = (
        block,
        block,
        P(CUBE, ROW, COL),
        P(),
        block,
        block,
        P(None, ROW, COL),
        P(),
        block,
        block,
        P(ROW, COL),
        P(),
        P(),
        P(),
    )
    return jax.shard_map(
        local, mesh=fine, in_specs=in_specs, out_specs=(block,) * 4, check_vma=False
    )
```

time: 190 us -> 172 us (0.905)
  blocking collectives: 51.2 us -> 21.9 us
  waiting for transfers between devices: 46.9 us -> 38.1 us
  local copies, waits for them, and re-layouts: 5.77 us -> 13.7 us
  Pallas kernels: 14.5 us -> 21.6 us
  starting transfers between devices: 55.5 us -> 60.7 us
    all_to_all x2 -> x1, blocking collectives: 51.2 us -> 21.9 us  [exchange(): return lax.all_to_all(value, axes, 0, 0, tiled=True)]
    all_to_all x2 -> x4, starting transfers between devices: 16.8 us -> 28.3 us  [exchange(): return lax.all_to_all(value, axes, 0, 0, tiled=True)]
    unnamed x26 -> x36, local copies, waits for them, and re-layouts: 5.7 us -> 13.7 us
    ppermute x5 -> x4, starting transfers between devices: 21.2 us -> 13.3 us  [swap(): return lax.ppermute(value, axis, [(0, 1), (1, 0)])]
    all_gather x3 -> x2, waiting for transfers between devices: 8.91 us -> 2.42 us  [the longest x1 2.42 us: local(): joined = lax.all_gather(joined, ROW, axis=0, tiled=False)]
    all_to_all x2 -> x4, waiting for transfers between devices: 24.4 us -> 18.8 us  [exchange(): return lax.all_to_all(value, axes, 0, 0, tiled=True)]
    ppermute x5 -> x4, waiting for transfers between devices: 10.5 us -> 14.9 us  [swap(): return lax.ppermute(value, axis, [(0, 1), (1, 0)])]
    pallas_call x1, Pallas kernels: 2.47 us -> 6.64 us  [local(): pl.pallas_call(root_kernel, grid=(4,), out_shape=(shape((256, 1024), F32)...]
  transfers between devices with their start and end apart: 13 -> 13, of which waited for: 9 -> 6; matrix products, arithmetic and copies ran while one was open for 0% -> 0% of each run, Pallas kernels for 5% -> 9%
where the time goes in v4:
time: 172 us; the launch traced here: 171 us
  starting transfers between devices  60.7 us (35%)
  waiting for transfers between devices  38.1 us (22%)
  blocking collectives  21.9 us (13%)
  Pallas kernels  21.6 us (13%)
  between operations  14.2 us (8%)
  local copies, waits for them, and re-layouts  13.7 us (8%)
    all_to_all x4, starting transfers between devices, exchange(): return lax.all_to_all(value, axes, 0, 0, tiled=True)  28.3 us
    all_to_all x1, blocking collectives, exchange(): return lax.all_to_all(value, axes, 0, 0, tiled=True)  21.9 us
    all_to_all x4, waiting for transfers between devices, exchange(): return lax.all_to_all(value, axes, 0, 0, tiled=True)  18.8 us
    ppermute x4, waiting for transfers between devices, swap(): return lax.ppermute(value, axis, [(0, 1), (1, 0)])  14.9 us
    unnamed x36, local copies, waits for them, and re-layouts  13.7 us
    pallas_call x6, Pallas kernels, call(): pl.pallas_call(kernel, out_shape=outs, in_specs=[SMEM] * tables + [VMEM]...  13.3 us
    ppermute x4, starting transfers between devices, swap(): return lax.ppermute(value, axis, [(0, 1), (1, 0)])  13.3 us
    ppermute x1, starting transfers between devices, transpose(): lax.ppermute(high, plane, pairs[1])  10.3 us
  transfers between devices with their start and end apart: 13, of which 6 were waited for; matrix products, arithmetic and copies ran while one was open for 0% of the time, Pallas kernels for 9%

profile of v4, /device:TPU:1, one launch (start us, length us, event | category | flops | bytes accessed | tf_op | source)
XLA Modules:
  0.0 170.8 jit_solution(14578149581739717602)
XLA Ops:
  7.8 1.9 %shard_map.165 = (bf16[8,3,64,128]{3,2,1,0:T(8,128)(2,1)}, bf16[3,256,128]{2,1,0:T(8,128)(2,1)}, bf16[3,128,128]{2,1,0:T(8,128)(2,1)}, bf16[3,128,128]{2,1,0:T(8,128)(2,1)}) custom-call(s32[3]{0:T(128)} %pad_add_fusion.where, bf16[1,64,128]{2,1,0:T(8,128)(2,1)} %leaf.2, bf16[2,64,128]{2,1,0:T(8,128)(2,1)} %mid.2, bf16[64,128]{1,0:T(8,128)(2,1)} %root.1, ...), custom_call_target="tpu_custom_call" | custom-call | tf_op jit(solution)/shard_map/pallas_call | solution.py:24
  9.7 5.9 %all-to-all-start = ((bf16[8,3,64,128]{3,2,1,0:T(8,128)(2,1)}), bf16[8,3,64,128]{3,2,1,0:T(8,128)(2,1)S(1)}, u32[]{:S(2)}, u32[]{:S(2)}) async-start(bf16[8,3,64,128]{3,2,1,0:T(8,128)(2,1)} %get-tuple-element.27), calls=%async_computation | async-start | bytes 786432 | tf_op jit(solution)/shard_map/all_to_all | solution.py:217
  15.6 6.2 %collective-permute-start = (bf16[3,128,128]{2,1,0:T(8,128)(2,1)}, bf16[3,128,128]{2,1,0:T(8,128)(2,1)S(1)}, u32[]{:S(2)}, u32[]{:S(2)}) collective-permute-start(bf16[3,128,128]{2,1,0:T(8,128)(2,1)} %get-tuple-element.29), channel_id=1, source_target_pairs={{0,0},{1,16},{2,32},{3,48},{4,64},{5,80},{6,96},{7,112},{8,17},{9,... | collective-permute-start | bytes 294920 | tf_op jit(solution)/shard_map/ppermute | solution.py:213
  21.9 10.3 %collective-permute-start.1 = (bf16[3,128,128]{2,1,0:T(8,128)(2,1)}, bf16[3,128,128]{2,1,0:T(8,128)(2,1)S(1)}, u32[]{:S(2)}, u32[]{:S(2)}) collective-permute-start(bf16[3,128,128]{2,1,0:T(8,128)(2,1)} %get-tuple-element.30), channel_id=1, source_target_pairs={{0,8},{1,24},{2,40},{3,56},{4,72},{5,88},{6,104},{7,120},{8,25},{9... | collective-permute-start | bytes 294920 | tf_op jit(solution)/shard_map/ppermute | solution.py:213
  32.2 1.9 %collective-permute-done.1.high = bf16[3,128,128]{2,1,0:T(8,128)(2,1)S(1)} collective-permute-done((bf16[3,128,128]{2,1,0:T(8,128)(2,1)}, bf16[3,128,128]{2,1,0:T(8,128)(2,1)S(1)}, u32[]{:S(2)}, u32[]{:S(2)}) %collective-permute-start.1) | collective-permute-done | bytes 98336 | tf_op jit(solution)/shard_map/ppermute | solution.py:213
  35.7 2.0 %shard_map.166 = (bf16[2,64,1024]{2,1,0:T(8,128)(2,1)}, bf16[8,64,128]{2,1,0:T(8,128)(2,1)S(1)}, bf16[3,128,128]{2,1,0:T(8,128)(2,1)S(1)}, bf16[2,128,128]{2,1,0...) custom-call(s32[3]{0:T(128)S(1)} %copy-done.8, ...), custom_call_target="tpu_custom_call" | custom-call | tf_op jit(solution)/shard_map/pallas_call | solution.py:24
  37.8 7.4 %all-to-all-start.1 = ((bf16[8,3,256,128]{3,2,1,0:T(8,128)(2,1)}), bf16[8,3,256,128]{3,2,1,0:T(8,128)(2,1)S(1)}, u32[]{:S(2)}, u32[]{:S(2)}) async-start(bf16[8,3,256,128]{3,2,1,0:T(8,128)(2,1)} %get-tuple-element.32), calls=%async_computation.1 | async-start | bytes 3145728 | tf_op jit(solution)/shard_map/all_to_all | solution.py:217
  45.2 4.2 %collective-permute-start.2 = (bf16[2,128,128]{2,1,0:T(8,128)(2,1)S(1)}, bf16[2,128,128]{2,1,0:T(8,128)(2,1)S(1)}, u32[]{:S(2)}, u32[]{:S(2)}) collective-permute-start(bf16[2,128,128]{2,1,0:T(8,128)(2,1)S(1)} %get-tuple-element.34), channel_id=1, source_target_pairs={{0,128},{128,0},{1,129},{129,1},{2,130},{130,2},{3,131},{131,3},{4... | collective-permute-start | bytes 196616 | tf_op jit(solution)/shard_map/ppermute | solution.py:203
  49.4 4.8 %collective-permute-start.3 = (bf16[128,128]{1,0:T(8,128)(2,1)S(1)}, bf16[128,128]{1,0:T(8,128)(2,1)S(1)}, u32[]{:S(2)}, u32[]{:S(2)}) collective-permute-start(bf16[128,128]{1,0:T(8,128)(2,1)S(1)} %get-tuple-element.35), channel_id=1, source_target_pairs={{0,256},{256,0},{1,257},{257,1},{2,258},{258,2},{3,259},{259,3},{4... | collective-permute-start | bytes 98312 | tf_op jit(solution)/shard_map/ppermute | solution.py:203
  54.2 2.4 %collective-permute-start.4 = (bf16[128,128]{1,0:T(8,128)(2,1)S(1)}, bf16[128,128]{1,0:T(8,128)(2,1)S(1)}, u32[]{:S(2)}, u32[]{:S(2)}) collective-permute-start(bf16[128,128]{1,0:T(8,128)(2,1)S(1)} %get-tuple-element.35), channel_id=1, source_target_pairs={{0,384},{128,256},{256,128},{384,0},{1,385},{129,257},{257,129},{3... | collective-permute-start | bytes 98312 | tf_op jit(solution)/shard_map/ppermute | solution.py:258
  56.6 13.4 %collective-permute-done.3.across = bf16[128,128]{1,0:T(8,128)(2,1)S(1)} collective-permute-done((bf16[128,128]{1,0:T(8,128)(2,1)S(1)}, bf16[128,128]{1,0:T(8,128)(2,1)S(1)}, u32[]{:S(2)}, u32[]{:S(2)}) %collective-permute-start.3) | collective-permute-done | bytes 32800 | tf_op jit(solution)/shard_map/ppermute | solution.py:203
  70.1 1.8 %shard_map.167 = (bf16[8,3,128,128]{3,2,1,0:T(8,128)(2,1)}, bf16[16,64,128]{2,1,0:T(8,128)(2,1)}, bf16[8,2,256,128]{3,2,1,0:T(8,128)(2,1)S(1)}) custom-call(s32[3]{0:T(128)S(1)} %copy-done.9, bf16[3,128,128]{2,1,0:T(8,128)(2,1)S(1)} %get-tuple-element.33.kept, bf16[2,128,128]{2,1,0:T(8,128)(2,1)S(1)} %collective-permute-done.2.partner, ...), custom_call_target="tpu_custom_call" | custom-call | tf_op jit(solution)/shard_map/pallas_call | solution.py:24
  71.8 1.0 copy-done.16
  72.8 6.0 %all-to-all-start.2 = ((bf16[8,3,128,128]{3,2,1,0:T(8,128)(2,1)}), bf16[8,3,128,128]{3,2,1,0:T(8,128)(2,1)S(1)}, u32[]{:S(2)}, u32[]{:S(2)}) async-start(bf16[8,3,128,128]{3,2,1,0:T(8,128)(2,1)} %get-tuple-element.37), calls=%async_computation.2 | async-start | bytes 1572864 | tf_op jit(solution)/shard_map/all_to_all | solution.py:217
  78.9 2.2 %collective-permute-start.5 = (bf16[8,2,256,128]{3,2,1,0:T(8,128)(2,1)}, bf16[8,2,256,128]{3,2,1,0:T(8,128)(2,1)S(1)}, u32[]{:S(2)}, u32[]{:S(2)}) collective-permute-start(bf16[8,2,256,128]{3,2,1,0:T(8,128)(2,1)} %copy-done.16), channel_id=1, source_target_pairs={{0,8},{8,0},{1,9},{9,1},{2,10},{10,2},{3,11},{11,3},{4,12},{12,4},... | collective-permute-start | bytes 3145736 | tf_op jit(solution)/shard_map/ppermute | solution.py:203
  81.0 1.0 copy-done.1
  84.4 2.1 %collective-permute-start.6 = (f32[3,256,128]{2,1,0:T(8,128)S(1)}, f32[3,256,128]{2,1,0:T(8,128)S(1)}, u32[]{:S(2)}, u32[]{:S(2)}) collective-permute-start(f32[3,256,128]{2,1,0:T(8,128)S(1)} %get-tuple-element.39), channel_id=1, source_target_pairs={{0,8},{8,0},{1,9},{9,1},{2,10},{10,2},{3,11},{11,3},{4,12},{12,4},... | collective-permute-start | bytes 1179656 | tf_op jit(solution)/shard_map/ppermute | solution.py:203
  86.5 1.5 collective-permute-done.6.other_front
  88.8 12.4 %all-to-all-done.2.blocks = bf16[8,3,128,128]{3,2,1,0:T(8,128)(2,1)S(1)} async-done(((bf16[8,3,128,128]{3,2,1,0:T(8,128)(2,1)}), bf16[8,3,128,128]{3,2,1,0:T(8,128)(2,1)S(1)}, u32[]{:S(2)}, u32[]{:S(2)}) %all-to-all-start.2) | async-done | bytes 786464 | tf_op jit(solution)/shard_map/all_to_all | solution.py:217
  101.1 2.2 %copy-done = bf16[32,64,1024]{2,1,0:T(8,128)(2,1)S(1)} copy-done((bf16[32,64,1024]{2,1,0:T(8,128)(2,1)S(1)}, bf16[32,64,1024]{2,1,0:T(8,128)(2,1)}, u32[]{:S(2)}) %copy-start) | copy-done | bytes 4194328
  103.3 1.0 copy-done.3
  104.3 1.0 copy-done.5
  105.3 4.9 %shard_map.169 = (bf16[32,2,3,8,128]{4,3,2,1,0:T(8,128)(2,1)S(1)}, bf16[256,128]{1,0:T(8,128)(2,1)}, bf16[256,128]{1,0:T(8,128)(2,1)}) custom-call(s32[3]{0:T(128)S(1)} %copy-done.9, s32[4,16]{1,0:T(4,128)S(1)} %copy-done.10, s32[2,32]{1,0:T(2,128)S(1)} %copy-done.12, bf16[16,2,64,1024]{3,2,1,0:T(8,128)(2,1)S(1)} %bitcast.6, ...), custom_call_target="tpu_custom_call" | custom-call | tf_op jit(solution)/shard_map/pallas_call | solution.py:24
  110.2 21.9 %all_to_all.25.pieces = bf16[32,2,3,8,128]{4,3,2,1,0:T(8,128)(2,1)S(1)} all-to-all(bf16[32,2,3,8,128]{4,3,2,1,0:T(8,128)(2,1)S(1)} %get-tuple-element.49), channel_id=1, replica_groups=mesh['pair'=2,'half'=2,'z'=8,'core'=2,'ylo'=2,'x'=4] {'pair','half','z'}, dimensions={0} | all-to-all | bytes 786432 | tf_op jit(solution)/shard_map/all_to_all | solution.py:217
  132.1 2.2 %shard_map.171 = bf16[64,4,8,128]{3,2,1,0:T(8,128)(2,1)} custom-call(s32[3]{0:T(128)S(1)} %copy-done.9, s32[4,16]{1,0:T(4,128)S(1)} %copy-done.11, s32[2,32]{1,0:T(2,128)S(1)} %copy-done.13, bf16[32,2,3,8,128]{4,3,2,1,0:T(8,128)(2,1)S(1)} %all_to_all.25.pieces), custom_call_target="tpu_custom_call" | custom-call | tf_op jit(solution)/shard_map/pallas_call | solution.py:24
  134.3 9.0 %all-to-all-start.4 = ((bf16[64,4,8,128]{3,2,1,0:T(8,128)(2,1)}), bf16[64,4,8,128]{3,2,1,0:T(8,128)(2,1)S(1)}, u32[]{:S(2)}, u32[]{:S(2)}) async-start(bf16[64,4,8,128]{3,2,1,0:T(8,128)(2,1)} %shard_map.171), calls=%async_computation.4 | async-start | bytes 1048576 | tf_op jit(solution)/shard_map/all_to_all | solution.py:217
  143.3 2.4 %all-gather.7.cloned.1.call-done = bf16[256,64,128]{2,1,0:T(8,128)(2,1)} async-done(((bf16[16,64,128]{2,1,0:T(8,128)(2,1)}), bf16[256,64,128]{2,1,0:T(8,128)(2,1)}) %all-gather.7.cloned.1.call-update) | async-done | bytes 4194320 | tf_op jit(solution)/shard_map/all_gather | solution.py:265
  145.7 2.2 %copy-done.14 = bf16[256,64,128]{2,1,0:T(8,128)(2,1)S(1)} copy-done((bf16[256,64,128]{2,1,0:T(8,128)(2,1)S(1)}, bf16[256,64,128]{2,1,0:T(8,128)(2,1)}, u32[]{:S(2)}) %copy-start.14) | copy-done | bytes 4194328
  147.9 1.2 copy-done.15
  149.1 6.6 %shard_map.170 = (f32[256,1024]{1,0:T(8,128)S(1)}, bf16[256,128]{1,0:T(8,128)(2,1)}) custom-call(s32[3]{0:T(128)S(1)} %copy-done.9, s32[64]{0:T(128)S(1)} %copy-done.17, bf16[8,3,256,128]{3,2,1,0:T(8,128)(2,1)S(1)} %all-to-all-done.1.panels.own, bf16[16,16,64,128]{3,2,1,0:T(8,128)(2,1)S(1)} %bitcast.8, f32[256,1024]{1,0:T(8,128)S(1)} %copy-done.15), custom_call_target="tpu_custom_call" | custom-call | flops 4294967296 | bytes 8388608 | tf_op jit(solution)/shard_map/pallas_call | solution.py:292
  155.8 6.5 %all-to-all-done.4 = bf16[64,4,8,128]{3,2,1,0:T(8,128)(2,1)S(1)} async-done(((bf16[64,4,8,128]{3,2,1,0:T(8,128)(2,1)}), bf16[64,4,8,128]{3,2,1,0:T(8,128)(2,1)S(1)}, u32[]{:S(2)}, u32[]{:S(2)}) %all-to-all-start.4) | async-done | bytes 524320 | tf_op jit(solution)/shard_map/all_to_all | solution.py:217
  162.3 1.7 shard_map.172
  (42 shorter events, 5.5 us)
Async XLA Ops:
  7.8 62.2 %copy-start.9 = (s32[3]{0:T(128)S(1)}, s32[3]{0:T(128)}, u32[]{:S(2)}) copy-start(s32[3]{0:T(128)} %pad_add_fusion.where) | copy-start | bytes 40
  9.7 24.4 %all-to-all-start = ((bf16[8,3,64,128]{3,2,1,0:T(8,128)(2,1)}), bf16[8,3,64,128]{3,2,1,0:T(8,128)(2,1)S(1)}, u32[]{:S(2)}, u32[]{:S(2)}) async-start(bf16[8,3,64,128]{3,2,1,0:T(8,128)(2,1)} %get-tuple-element.27), calls=%async_computation | async-start | bytes 786432 | tf_op jit(solution)/shard_map/all_to_all | solution.py:217
  15.6 85.5 %all-gather.5.cloned.1.call-start = ((), (), s32[]{:S(2)}) async-start(), calls=%async_computation.5 | async-start | bytes 4456448 | tf_op jit(solution)/shard_map/all_gather | solution.py:255
  15.6 16.6 %collective-permute-start = (bf16[3,128,128]{2,1,0:T(8,128)(2,1)}, bf16[3,128,128]{2,1,0:T(8,128)(2,1)S(1)}, u32[]{:S(2)}, u32[]{:S(2)}) collective-permute-start(bf16[3,128,128]{2,1,0:T(8,128)(2,1)} %get-tuple-element.29), channel_id=1, source_target_pairs={{0,0},{1,16},{2,32},{3,48},{4,64},{5,80},{6,96},{7,112},{8,17},{9,... | collective-permute-start | bytes 294920 | tf_op jit(solution)/shard_map/ppermute | solution.py:213
  21.9 12.3 %collective-permute-start.1 = (bf16[3,128,128]{2,1,0:T(8,128)(2,1)}, bf16[3,128,128]{2,1,0:T(8,128)(2,1)S(1)}, u32[]{:S(2)}, u32[]{:S(2)}) collective-permute-start(bf16[3,128,128]{2,1,0:T(8,128)(2,1)} %get-tuple-element.30), channel_id=1, source_target_pairs={{0,8},{1,24},{2,40},{3,56},{4,72},{5,88},{6,104},{7,120},{8,25},{9... | collective-permute-start | bytes 294920 | tf_op jit(solution)/shard_map/ppermute | solution.py:213
  34.1 0.9 copy-start.7
  35.1 0.7 copy-start.8
  35.7 65.4 %copy-start.10 = (s32[4,16]{1,0:T(4,128)S(1)}, s32[4,16]{1,0:T(4,128)}, u32[]{:S(2)}) copy-start(s32[4,16]{1,0:T(4,128)} %leaf_fill.1) | copy-start | bytes 772
  35.7 65.4 %copy-start.12 = (s32[2,32]{1,0:T(2,128)S(1)}, s32[2,32]{1,0:T(2,128)}, u32[]{:S(2)}) copy-start(s32[2,32]{1,0:T(2,128)} %mid_fill.1) | copy-start | bytes 772
  37.8 32.3 %all-to-all-start.1 = ((bf16[8,3,256,128]{3,2,1,0:T(8,128)(2,1)}), bf16[8,3,256,128]{3,2,1,0:T(8,128)(2,1)S(1)}, u32[]{:S(2)}, u32[]{:S(2)}) async-start(bf16[8,3,256,128]{3,2,1,0:T(8,128)(2,1)} %get-tuple-element.32), calls=%async_computation.1 | async-start | bytes 3145728 | tf_op jit(solution)/shard_map/all_to_all | solution.py:217
  45.2 100.6 %all-gather.7.cloned.1.call-start = ((), (), s32[]{:S(2)}) async-start(), calls=%async_computation.6 | async-start | bytes 4456448 | tf_op jit(solution)/shard_map/all_gather | solution.py:265
  45.2 24.8 %collective-permute-start.2 = (bf16[2,128,128]{2,1,0:T(8,128)(2,1)S(1)}, bf16[2,128,128]{2,1,0:T(8,128)(2,1)S(1)}, u32[]{:S(2)}, u32[]{:S(2)}) collective-permute-start(bf16[2,128,128]{2,1,0:T(8,128)(2,1)S(1)} %get-tuple-element.34), channel_id=1, source_target_pairs={{0,128},{128,0},{1,129},{129,1},{2,130},{130,2},{3,131},{131,3},{4... | collective-permute-start | bytes 196616 | tf_op jit(solution)/shard_map/ppermute | solution.py:203
  49.4 20.6 %collective-permute-start.3 = (bf16[128,128]{1,0:T(8,128)(2,1)S(1)}, bf16[128,128]{1,0:T(8,128)(2,1)S(1)}, u32[]{:S(2)}, u32[]{:S(2)}) collective-permute-start(bf16[128,128]{1,0:T(8,128)(2,1)S(1)} %get-tuple-element.35), channel_id=1, source_target_pairs={{0,256},{256,0},{1,257},{257,1},{2,258},{258,2},{3,259},{259,3},{4... | collective-permute-start | bytes 98312 | tf_op jit(solution)/shard_map/ppermute | solution.py:203
  54.2 15.8 %collective-permute-start.4 = (bf16[128,128]{1,0:T(8,128)(2,1)S(1)}, bf16[128,128]{1,0:T(8,128)(2,1)S(1)}, u32[]{:S(2)}, u32[]{:S(2)}) collective-permute-start(bf16[128,128]{1,0:T(8,128)(2,1)S(1)} %get-tuple-element.35), channel_id=1, source_target_pairs={{0,384},{128,256},{256,128},{384,0},{1,385},{129,257},{257,129},{3... | collective-permute-start | bytes 98312 | tf_op jit(solution)/shard_map/ppermute | solution.py:258
  71.8 1.0 copy-start.16
  72.8 28.3 %all-to-all-start.2 = ((bf16[8,3,128,128]{3,2,1,0:T(8,128)(2,1)}), bf16[8,3,128,128]{3,2,1,0:T(8,128)(2,1)S(1)}, u32[]{:S(2)}, u32[]{:S(2)}) async-start(bf16[8,3,128,128]{3,2,1,0:T(8,128)(2,1)} %get-tuple-element.37), calls=%async_computation.2 | async-start | bytes 1572864 | tf_op jit(solution)/shard_map/all_to_all | solution.py:217
  78.9 9.9 %collective-permute-start.5 = (bf16[8,2,256,128]{3,2,1,0:T(8,128)(2,1)}, bf16[8,2,256,128]{3,2,1,0:T(8,128)(2,1)S(1)}, u32[]{:S(2)}, u32[]{:S(2)}) collective-permute-start(bf16[8,2,256,128]{3,2,1,0:T(8,128)(2,1)} %copy-done.16), channel_id=1, source_target_pairs={{0,8},{8,0},{1,9},{9,1},{2,10},{10,2},{3,11},{11,3},{4,12},{12,4},... | collective-permute-start | bytes 3145736 | tf_op jit(solution)/shard_map/ppermute | solution.py:203
  81.0 1.0 copy-start.1
  82.1 0.9 copy-start.6
  83.6 0.7 copy-start.2
  84.4 3.6 %collective-permute-start.6 = (f32[3,256,128]{2,1,0:T(8,128)S(1)}, f32[3,256,128]{2,1,0:T(8,128)S(1)}, u32[]{:S(2)}, u32[]{:S(2)}) collective-permute-start(f32[3,256,128]{2,1,0:T(8,128)S(1)} %get-tuple-element.39), channel_id=1, source_target_pairs={{0,8},{8,0},{1,9},{9,1},{2,10},{10,2},{3,11},{11,3},{4,12},{12,4},... | collective-permute-start | bytes 1179656 | tf_op jit(solution)/shard_map/ppermute | solution.py:203
  88.0 0.8 copy-start.4
  101.1 2.2 %copy-start = (bf16[32,64,1024]{2,1,0:T(8,128)(2,1)S(1)}, bf16[32,64,1024]{2,1,0:T(8,128)(2,1)}, u32[]{:S(2)}) copy-start(bf16[32,64,1024]{2,1,0:T(8,128)(2,1)} %all-gather.5.cloned.1.call-done) | copy-start | bytes 12582916
  103.3 1.0 copy-start.3
  104.3 1.0 copy-start.5
  105.3 26.8 %copy-start.11 = (s32[4,16]{1,0:T(4,128)S(1)}, s32[4,16]{1,0:T(4,128)}, u32[]{:S(2)}) copy-start(s32[4,16]{1,0:T(4,128)} %leaf_map.1) | copy-start | bytes 772
  105.3 26.8 %copy-start.13 = (s32[2,32]{1,0:T(2,128)S(1)}, s32[2,32]{1,0:T(2,128)}, u32[]{:S(2)}) copy-start(s32[2,32]{1,0:T(2,128)} %mid_map.1) | copy-start | bytes 772
  105.3 40.4 %copy-start.17 = (s32[64]{0:T(128)S(1)}, s32[64]{0:T(128)}, u32[]{:S(2)}) copy-start(s32[64]{0:T(128)} %fill.1) | copy-start | bytes 772
  134.3 28.0 %all-to-all-start.4 = ((bf16[64,4,8,128]{3,2,1,0:T(8,128)(2,1)}), bf16[64,4,8,128]{3,2,1,0:T(8,128)(2,1)S(1)}, u32[]{:S(2)}, u32[]{:S(2)}) async-start(bf16[64,4,8,128]{3,2,1,0:T(8,128)(2,1)} %shard_map.171), calls=%async_computation.4 | async-start | bytes 1048576 | tf_op jit(solution)/shard_map/all_to_all | solution.py:217
  145.7 2.2 %copy-start.14 = (bf16[256,64,128]{2,1,0:T(8,128)(2,1)S(1)}, bf16[256,64,128]{2,1,0:T(8,128)(2,1)}, u32[]{:S(2)}) copy-start(bf16[256,64,128]{2,1,0:T(8,128)(2,1)} %all-gather.7.cloned.1.call-done) | copy-start | bytes 12582916
  147.9 1.2 copy-start.15
Sparse Core Ops, SparseCore 0:
  37.9 50.7 all-gather.4
  90.8 54.8 all-gather.6

commit v5 on v4

v5 whole, which is shorter than its diff:
```python
import jax
import jax.numpy as jnp
from jax import lax
from jax.experimental import pallas as pl
from jax.experimental.pallas import tpu as pltpu
from jax.sharding import Mesh, PartitionSpec as P

CUBE = ("pair", "half")
ROW = ("z", "core")
COL = ("ylo", "x")
VMEM = pl.BlockSpec(memory_space=pltpu.VMEM)
SMEM = pl.BlockSpec(memory_space=pltpu.SMEM)
ANY = pl.BlockSpec(memory_space=pl.ANY)
BF = jnp.bfloat16
F32 = jnp.float32


def shape(dims, dtype=BF):
    return jax.ShapeDtypeStruct(dims, dtype)


def call(kernel, outs, ins, mebibytes=20, scratch=(), after=(), cost=None):
    tables = sum(1 for value in ins if value.dtype == jnp.int32)
    many = isinstance(outs, tuple)
    return pl.pallas_call(
        kernel,
        out_shape=outs,
        in_specs=[SMEM] * tables + [VMEM] * (len(ins) - tables) + [ANY] * len(after),
        out_specs=(VMEM,) * len(outs) if many else VMEM,
        scratch_shapes=list(scratch),
        compiler_params=pltpu.CompilerParams(vmem_limit_bytes=mebibytes * 1024 * 1024),
        cost_estimate=cost and pl.CostEstimate(cost[0], 0, cost[1]),
    )(*ins, *after)


def cube_at():
    return lax.axis_index(CUBE)


def row_at():
    return lax.axis_index(ROW)


def column_at():
    return lax.axis_index(COL)


def dot_t(left, right):
    return lax.dot_general(left, right, (((1,), (1,)), ((), ())), preferred_element_type=F32)


def inputs_kernel(
    leaf, mid, root, leaf_panel, mid_panel, root_panel, weights, spread, low, high
):
    for to in range(8):
        weights[to, 0] = leaf[0]
        weights[to, 1] = mid[cube_at() // 2]
        weights[to, 2] = root[...]
        for front, panel in enumerate((leaf_panel, mid_panel, root_panel)):
            spread[to, front] = panel[...]
    for front, panel in enumerate((leaf_panel, mid_panel, root_panel)):
        low[front] = panel[:128]
        high[front] = panel[128:]


def half_of(kind, side, leaf, mid):
    if kind == 0:
        return leaf[:, 128 * side : 128 * side + 128]
    at = 256 * (kind - 1) + 128 * side
    return mid[:, at : at + 128]


def fronts_kernel(leaf, mid, give):
    first = row_at() % 2 == 0
    for kind in range(3):
        give[kind] = jnp.where(first, half_of(kind, 1, leaf, mid), half_of(kind, 0, leaf, mid))


def whole_kernel(
    weights, low, high, whole, root, kept, cross, last
):
    first = row_at() % 2 == 0
    for front in range(2):
        for at in range(8):
            whole[front, :, 128 * at : 128 * at + 128] = weights[at, front]
    for at in range(8):
        root[at] = weights[at, 2]
    for front in range(3):
        kept[front] = jnp.where(first, low[front], high[front])
    for front in range(2):
        cross[front] = jnp.where(first, low[front + 1], high[front + 1])
    last[...] = kept[2]


def columns_kernel(
    kept, partner, across, corner, weights, _, sent, joined
):
    cube = cube_at()
    even = cube % 2 == 0
    for to in range(8):
        sent[to, 0] = kept[0]
        sent[to, 1] = jnp.where(even, kept[1], partner[0])
        sent[to, 2] = jnp.where(even, partner[0], kept[1])
    joined[:8] = weights[...]
    for slot in range(4):
        same_half, same_pair = cube % 2 == slot % 2, cube // 2 == slot // 2
        piece = jnp.where(
            same_pair,
            jnp.where(same_half, kept[2], partner[1]),
            jnp.where(same_half, across[...], corner[...]),
        )
        for half in range(2):
            joined[8 + 2 * slot + half] = piece[64 * half : 64 * half + 64]


def factor_kernel(
    leaf_fill, mid_fill, far_weights, far_own, far_other, _,
    turned, keep, give, panel, factor, total, weights, own, other, sems,
):
    cube, row, column = cube_at(), row_at(), column_at()
    front = row % 2
    first = front == 0
    upper = row - front
    pairs = ((far_own, own), (far_other, other), (far_weights, weights))
    moves = [
        pltpu.make_async_copy(far.at[:, front], near, sems.at[at])
        for at, (far, near) in enumerate(pairs)
    ]
    for move in moves:
        move.start()
    pair, base = cube // 2, 16 * (cube % 2) + upper
    fills = [
        jnp.where(first, leaf_fill[cube, upper + index], mid_fill[pair, base + index])
        for index in range(2)
    ]
    for move in moves:
        move.wait()
    for at in range(8):
        span = slice(128 * at, 128 * at + 128)
        panel[:256, span] = jnp.where(first, own[at], other[at])
        panel[256:, span] = jnp.where(first, other[at], own[at])
    for at in range(0, 16, 4):
        rows_of = weights[at : at + 4].reshape(256, 1024)
        part = dot_t(panel[...], rows_of)
        span = slice(64 * at, 64 * at + 256)
        for index, fill in enumerate(fills):
            rows = slice(256 * index, 256 * index + 256)
            factor[rows, span] = (part[rows] * fill.astype(F32)).astype(BF)
        more = jnp.dot(factor[:, span], rows_of, preferred_element_type=F32)
        total[...] = more if at == 0 else total[...] + more
    turned[...] = total[...].astype(BF)
    mine_at = pl.ds(pl.multiple_of(128 * column, 128), 128)
    keep[...] = jnp.where(first, factor[:256, mine_at], factor[256:, mine_at])
    give[...] = jnp.where(first, factor[256:, mine_at], factor[:256, mine_at])


def update_kernel(
    leaf_fill, mid_fill, turned, other_turned, blocks, leaf, mid, other_front, out, panel
):
    cube, row, column = cube_at(), row_at(), column_at()
    first = row % 2 == 0
    pair = cube // 2
    fills = [leaf_fill[cube, column], mid_fill[pair, column], mid_fill[pair, 16 + column]]
    for kind, fill in enumerate(fills):
        for at in range(8):
            panel[kind, :, 128 * at : 128 * at + 128] = blocks[(at + column) % 8, kind]
        if kind < 2:
            same = first if kind == 0 else jnp.logical_not(first)
            rows = jnp.where(same, turned[...], other_turned[...])
        product = dot_t(rows, panel[kind]) * fill.astype(F32)
        mine = jnp.where(first, half_of(kind, 0, leaf, mid), half_of(kind, 1, leaf, mid))
        theirs = other_front[kind]
        for block in range(2):
            matrix = jnp.where(first, theirs, mine) if block else jnp.where(first, mine, theirs)
            value = matrix - product[256 * block : 256 * block + 256]
            out[:, block, kind] = value.reshape(32, 8, 128).astype(BF)


def place_kernel(leaf_map, mid_map, pieces, out, total):
    column = column_at()
    total[...] = jnp.zeros_like(total)
    for front in range(4):
        pair = front // 2
        slot = mid_map[pair, leaf_map[front, column]] // 16
        for block in range(16):
            target = mid_map[pair, leaf_map[front, block]]
            piece = pieces[8 * front + block // 2, block % 2, 0]
            total[4 * target + slot] += piece.astype(F32)
    for pair in range(2):
        slots = [mid_map[pair, 16 * at + column] // 16 for at in range(2)]
        for block in range(32):
            target = mid_map[pair, block]
            for at in range(2):
                piece = pieces[16 * pair + block // 2, block % 2, 1 + at]
                total[4 * target + slots[at]] += piece.astype(F32)
    out[...] = total[...].reshape(64, 4, 8, 128).astype(BF)


def root_kernel(
    fill, panels, joined, front, out, root_factor, weights, panel, factor, turned
):
    cube, row, column = cube_at(), row_at(), column_at()
    slot = pl.program_id(0)

    @pl.when(slot == 0)
    def _():
        for at in range(8):
            span = slice(128 * at, 128 * at + 128)
            panel[:, span] = panels[at, 0]
            for owner in range(16):
                weights[64 * owner : 64 * owner + 64, span] = joined[owner, at]
        for at in range(0, 1024, 256):
            part = dot_t(panel[...], weights[at : at + 256])
            factor[:, at : at + 256] = (part * fill[16 * cube + row].astype(F32)).astype(BF)
        turned[...] = jnp.dot(factor[...], weights[...], preferred_element_type=F32).astype(BF)
        root_factor[...] = factor[:, pl.ds(pl.multiple_of(128 * column, 128), 128)]

    for half in range(2):
        for at in range(8):
            owner = 2 * ((at + column) % 8) + half
            piece = joined[owner, pl.ds(8 + 2 * slot, 2)].reshape(128, 128)
            panel[128 * half : 128 * half + 128, 128 * at : 128 * at + 128] = piece
    product = dot_t(turned[...], panel[...]) * fill[16 * slot + column].astype(F32)
    out[...] = front[...] - product


def add_kernel(base, arrived, out):
    for side in range(2):
        added = arrived[:, side, 0].astype(F32).reshape(256, 128)
        span = slice(128 * side, 128 * side + 128)
        out[:, span] = base[:, span] + added


def swap(value, axis):
    return lax.ppermute(value, axis, [(0, 1), (1, 0)])


def transpose(low, high):
    pairs = [[], []]
    for r in range(8):
        for c in range(8):
            for half in range(2):
                pairs[half].append((8 * r + c, 8 * (2 * ((c + r) % 8) + half) + r))
    plane = ROW + COL
    return lax.ppermute(low, plane, pairs[0]), lax.ppermute(high, plane, pairs[1])


def exchange(value, axes):
    return lax.all_to_all(value, axes, 0, 0, tiled=True)


def local(
    leaf_front,
    leaf_panel,
    leaf_inverse,
    leaf_fill,
    mid_front,
    mid_panel,
    mid_inverse,
    mid_fill,
    root_front,
    root_panel,
    root_inverse,
    root_fill,
    leaf_map,
    mid_map,
):
    piece = shape((256, 128))
    two, three = shape((2, 128, 128)), shape((3, 128, 128))
    panel_all = shape((8, 3, 256, 128))

    weights, spread, low, high = call(
        inputs_kernel,
        (shape((8, 3, 64, 128)), panel_all, three, three),
        (leaf_inverse, mid_inverse, root_inverse, leaf_panel, mid_panel, root_panel),
        60,
    )
    low, high = transpose(low, high)
    weights = exchange(weights, COL)
    whole, root_weights, kept, cross, last = call(
        whole_kernel,
        (shape((2, 64, 1024)), shape((8, 64, 128)), three, two, shape((128, 128))),
        (weights, low, high),
    )
    whole, spread = lax.optimization_barrier((whole, spread))
    weights = lax.all_gather(whole, ROW, axis=0, tiled=False)
    partner = swap(cross, "half")
    across = swap(last, "pair")
    corner = lax.ppermute(last, CUBE, [(0, 3), (1, 2), (2, 1), (3, 0)])
    panels = exchange(spread, COL)
    sent, joined = call(
        columns_kernel,
        (shape((8, 3, 128, 128)), shape((16, 64, 128))),
        (kept, partner, across, corner, root_weights),
        after=(panels,),
    )
    sent, joined, panels = lax.optimization_barrier((sent, joined, panels))
    joined = lax.all_gather(joined, ROW, axis=0, tiled=False)
    other_panels = swap(panels, "core")
    half_front = shape((3, 256, 128), F32)
    give_front = call(fronts_kernel, half_front, (leaf_front, mid_front))
    other_front = swap(give_front, "core")
    blocks = exchange(sent, "z")
    turned, keep, give = call(
        factor_kernel,
        (shape((512, 1024)), piece, piece),
        (leaf_fill, mid_fill),
        60,
        scratch=(
            pltpu.VMEM((512, 1024), BF),
            pltpu.VMEM((512, 1024), BF),
            pltpu.VMEM((512, 1024), F32),
            pltpu.VMEM((16, 64, 1024), BF),
            pltpu.VMEM((8, 256, 128), BF),
            pltpu.VMEM((8, 256, 128), BF),
            pltpu.SemaphoreType.DMA((3,)),
        ),
        after=(weights, panels, other_panels, other_front),
        cost=(2**31, 2**22),
    )
    other_turned = swap(turned, "core")
    blocks, other_turned = lax.optimization_barrier((blocks, other_turned))
    updates = call(
        update_kernel,
        shape((32, 2, 3, 8, 128)),
        (leaf_fill, mid_fill, turned, other_turned, blocks, leaf_front, mid_front, other_front),
        60,
        scratch=(pltpu.VMEM((3, 128, 1024), BF),),
    )
    given = swap(give, "core")
    leaf_first = lax.axis_index("core") == 0
    leaf_factor = jnp.where(leaf_first, keep, given)
    mid_factor = jnp.where(leaf_first, given, keep)
    pieces = exchange(updates, CUBE + ("z",))
    placed = call(
        place_kernel,
        shape((64, 4, 8, 128)),
        (leaf_map, mid_map, pieces),
        scratch=(pltpu.VMEM((256, 8, 128), F32),),
    )
    arrived = exchange(placed, CUBE + ROW)
    spot = pl.BlockSpec((256, 256), lambda s: (0, s))
    limit = pltpu.CompilerParams(vmem_limit_bytes=24 * 1024 * 1024)
    base, root_factor = pl.pallas_call(
        root_kernel,
        grid=(4,),
        out_shape=(shape((256, 1024), F32), piece),
        in_specs=[
            SMEM,
            pl.BlockSpec((8, 1, 256, 128), lambda s: (0, 2, 0, 0)),
            pl.BlockSpec((16, 16, 64, 128), lambda s: (0, 0, 0, 0)),
            spot,
        ],
        out_specs=(spot, pl.BlockSpec((256, 128), lambda s: (0, 0))),
        scratch_shapes=[
            pltpu.VMEM((1024, 1024), BF),
            pltpu.VMEM((256, 1024), BF),
            pltpu.VMEM((256, 1024), BF),
            pltpu.VMEM((256, 1024), BF),
        ],
        compiler_params=limit,
        cost_estimate=pl.CostEstimate(flops=2**32, bytes_accessed=2**23, transcendentals=0),
    )(root_fill, panels, joined, root_front)
    root_update = pl.pallas_call(
        add_kernel,
        grid=(4,),
        out_shape=shape((256, 1024), F32),
        in_specs=[spot, pl.BlockSpec((32, 2, 1, 8, 128), lambda s: (0, 0, s, 0, 0))],
        out_specs=spot,
        compiler_params=limit,
    )(base, arrived.reshape(32, 2, 4, 8, 128))
    return leaf_factor, mid_factor, root_factor, root_update


def solution(mesh):
    fine = Mesh(
        mesh.devices.reshape(2, 2, 8, 2, 2, 4), ("pair", "half", "z", "core", "ylo", "x")
    )
    block = P(CUBE + ROW, COL)
    in_specs = (
        block,
        block,
        P(CUBE, ROW, COL),
        P(),
        block,
        block,
        P(None, ROW, COL),
        P(),
        block,
        block,
        P(ROW, COL),
        P(),
        P(),
        P(),
    )
    return jax.shard_map(
        local, mesh=fine, in_specs=in_specs, out_specs=(block,) * 4, check_vma=False
    )
```

time: 172 us -> 167 us (0.971)
  local copies, waits for them, and re-layouts: 13.7 us -> 5.37 us
  starting transfers between devices: 60.7 us -> 66.8 us
  blocking collectives: 21.9 us -> 17.1 us
  Pallas kernels: 21.6 us -> 23.4 us
    unnamed x36 -> x28, local copies, waits for them, and re-layouts: 13.7 us -> 5.37 us
    ppermute x4 -> x6, starting transfers between devices: 13.3 us -> 19.2 us  [swap(): return lax.ppermute(value, axis, [(0, 1), (1, 0)])]
    all_to_all x1, blocking collectives: 21.9 us -> 17.1 us  [exchange(): return lax.all_to_all(value, axes, 0, 0, tiled=True)]
    pallas_call x6 -> x7, Pallas kernels: 13.3 us -> 17.3 us  [call(): pl.pallas_call(kernel, out_shape=outs, in_specs=[SMEM] * tables + [VMEM]...]
    all_gather x1, waiting for transfers between devices: 0.01 us -> 4 us  [local(): weights = lax.all_gather(whole, ROW, axis=0, tiled=False)]
    all_gather x1, waiting for transfers between devices: 2.42 us -> 0.01 us  [local(): joined = lax.all_gather(joined, ROW, axis=0, tiled=False)]
    pallas_call x1, Pallas kernels: 6.64 us -> 4.42 us  [local(): pl.pallas_call(root_kernel, grid=(4,), out_shape=(shape((256, 1024), F32)...]
    ppermute x4 -> x6, waiting for transfers between devices: 14.9 us -> 14.2 us  [swap(): return lax.ppermute(value, axis, [(0, 1), (1, 0)])]
  transfers between devices with their start and end apart: 13 -> 15, of which waited for: 6 -> 6; matrix products, arithmetic and copies ran while one was open for 0% -> 0% of each run, Pallas kernels for 9% -> 11%
where the time goes in v5:
time: 167 us; the launch traced here: 166 us
  starting transfers between devices  66.8 us (40%)
  waiting for transfers between devices  37.9 us (23%)
  Pallas kernels  23.4 us (14%)
  blocking collectives  17.1 us (10%)
  between operations  14.3 us (9%)
  local copies, waits for them, and re-layouts  5.37 us (3%)
    all_to_all x4, starting transfers between devices, exchange(): return lax.all_to_all(value, axes, 0, 0, tiled=True)  28.5 us
    ppermute x6, starting transfers between devices, swap(): return lax.ppermute(value, axis, [(0, 1), (1, 0)])  19.2 us
    all_to_all x4, waiting for transfers between devices, exchange(): return lax.all_to_all(value, axes, 0, 0, tiled=True)  17.8 us
    pallas_call x7, Pallas kernels, call(): pl.pallas_call(kernel, out_shape=outs, in_specs=[SMEM] * tables + [VMEM]...  17.3 us
    all_to_all x1, blocking collectives, exchange(): return lax.all_to_all(value, axes, 0, 0, tiled=True)  17.1 us
    ppermute x6, waiting for transfers between devices, swap(): return lax.ppermute(value, axis, [(0, 1), (1, 0)])  14.2 us
    ppermute x1, starting transfers between devices, transpose(): lax.ppermute(high, plane, pairs[1])  10.3 us
    ppermute x1, starting transfers between devices, transpose(): lax.ppermute(low, plane, pairs[0])  6.25 us
  transfers between devices with their start and end apart: 15, of which 6 were waited for; matrix products, arithmetic and copies ran while one was open for 0% of the time, Pallas kernels for 11%

profile of v5, /device:TPU:1, one launch (start us, length us, event | category | flops | bytes accessed | tf_op | source)
XLA Modules:
  0.0 165.6 jit_solution(7195085804100412631)
XLA Ops:
  7.2 2.5 %shard_map.165 = (bf16[8,3,64,128]{3,2,1,0:T(8,128)(2,1)}, bf16[8,3,256,128]{3,2,1,0:T(8,128)(2,1)}, bf16[3,128,128]{2,1,0:T(8,128)(2,1)}, bf16[3,128,128]{2,1,0:T(8,128)(2,1)}) custom-call(bf16[1,64,128]{2,1,0:T(8,128)(2,1)} %leaf.3, bf16[2,64,128]{2,1,0:T(8,128)(2,1)} %mid.3, bf16[64,128]{1,0:T(8,128)(2,1)} %root.1, bf16[256,128]{1,0:T(8,128)(2,1)} %leaf_panel.1, ...), custom_call_target="tpu_custom_call" | custom-call | tf_op jit(solution)/shard_map/pallas_call | solution.py:25
  9.7 5.9 %all-to-all-start = ((bf16[8,3,64,128]{3,2,1,0:T(8,128)(2,1)}), bf16[8,3,64,128]{3,2,1,0:T(8,128)(2,1)S(1)}, u32[]{:S(2)}, u32[]{:S(2)}) async-start(bf16[8,3,64,128]{3,2,1,0:T(8,128)(2,1)} %get-tuple-element.27), calls=%async_computation | async-start | bytes 786432 | tf_op jit(solution)/shard_map/all_to_all | solution.py:249
  15.6 6.2 %collective-permute-start = (bf16[3,128,128]{2,1,0:T(8,128)(2,1)}, bf16[3,128,128]{2,1,0:T(8,128)(2,1)S(1)}, u32[]{:S(2)}, u32[]{:S(2)}) collective-permute-start(bf16[3,128,128]{2,1,0:T(8,128)(2,1)} %get-tuple-element.28), channel_id=1, source_target_pairs={{0,0},{1,16},{2,32},{3,48},{4,64},{5,80},{6,96},{7,112},{8,17},{9,... | collective-permute-start | bytes 294920 | tf_op jit(solution)/shard_map/ppermute | solution.py:245
  21.8 10.3 %collective-permute-start.1 = (bf16[3,128,128]{2,1,0:T(8,128)(2,1)}, bf16[3,128,128]{2,1,0:T(8,128)(2,1)S(1)}, u32[]{:S(2)}, u32[]{:S(2)}) collective-permute-start(bf16[3,128,128]{2,1,0:T(8,128)(2,1)} %get-tuple-element.29), channel_id=1, source_target_pairs={{0,8},{1,24},{2,40},{3,56},{4,72},{5,88},{6,104},{7,120},{8,25},{9... | collective-permute-start | bytes 294920 | tf_op jit(solution)/shard_map/ppermute | solution.py:245
  32.2 1.9 %collective-permute-done.1.high = bf16[3,128,128]{2,1,0:T(8,128)(2,1)S(1)} collective-permute-done((bf16[3,128,128]{2,1,0:T(8,128)(2,1)}, bf16[3,128,128]{2,1,0:T(8,128)(2,1)S(1)}, u32[]{:S(2)}, u32[]{:S(2)}) %collective-permute-start.1) | collective-permute-done | bytes 98336 | tf_op jit(solution)/shard_map/ppermute | solution.py:245
  34.1 0.8 shard_map.166
  34.9 7.4 %all-to-all-start.1 = ((bf16[8,3,256,128]{3,2,1,0:T(8,128)(2,1)}), bf16[8,3,256,128]{3,2,1,0:T(8,128)(2,1)S(1)}, u32[]{:S(2)}, u32[]{:S(2)}) async-start(bf16[8,3,256,128]{3,2,1,0:T(8,128)(2,1)} %get-tuple-element.37), calls=%async_computation.1 | async-start | bytes 3145728 | tf_op jit(solution)/shard_map/all_to_all | solution.py:249
  42.4 4.3 %collective-permute-start.2 = (bf16[2,128,128]{2,1,0:T(8,128)(2,1)S(1)}, bf16[2,128,128]{2,1,0:T(8,128)(2,1)S(1)}, u32[]{:S(2)}, u32[]{:S(2)}) collective-permute-start(bf16[2,128,128]{2,1,0:T(8,128)(2,1)S(1)} %get-tuple-element.34), channel_id=1, source_target_pairs={{0,128},{128,0},{1,129},{129,1},{2,130},{130,2},{3,131},{131,3},{4... | collective-permute-start | bytes 196616 | tf_op jit(solution)/shard_map/ppermute | solution.py:235
  46.8 4.8 %collective-permute-start.3 = (bf16[128,128]{1,0:T(8,128)(2,1)S(1)}, bf16[128,128]{1,0:T(8,128)(2,1)S(1)}, u32[]{:S(2)}, u32[]{:S(2)}) collective-permute-start(bf16[128,128]{1,0:T(8,128)(2,1)S(1)} %get-tuple-element.35), channel_id=1, source_target_pairs={{0,256},{256,0},{1,257},{257,1},{2,258},{258,2},{3,259},{259,3},{4... | collective-permute-start | bytes 98312 | tf_op jit(solution)/shard_map/ppermute | solution.py:235
  51.5 2.4 %collective-permute-start.4 = (bf16[128,128]{1,0:T(8,128)(2,1)S(1)}, bf16[128,128]{1,0:T(8,128)(2,1)S(1)}, u32[]{:S(2)}, u32[]{:S(2)}) collective-permute-start(bf16[128,128]{1,0:T(8,128)(2,1)S(1)} %get-tuple-element.35), channel_id=1, source_target_pairs={{0,384},{128,256},{256,128},{384,0},{1,385},{129,257},{257,129},{3... | collective-permute-start | bytes 98312 | tf_op jit(solution)/shard_map/ppermute | solution.py:289
  53.9 13.3 %collective-permute-done.3.across = bf16[128,128]{1,0:T(8,128)(2,1)S(1)} collective-permute-done((bf16[128,128]{1,0:T(8,128)(2,1)S(1)}, bf16[128,128]{1,0:T(8,128)(2,1)S(1)}, u32[]{:S(2)}, u32[]{:S(2)}) %collective-permute-start.3) | collective-permute-done | bytes 32800 | tf_op jit(solution)/shard_map/ppermute | solution.py:235
  67.2 1.2 shard_map.167
  68.5 3.6 %collective-permute-start.5 = (bf16[8,3,256,128]{3,2,1,0:T(8,128)(2,1)S(1)}, bf16[8,3,256,128]{3,2,1,0:T(8,128)(2,1)}, u32[]{:S(2)}, u32[]{:S(2)}) collective-permute-start(bf16[8,3,256,128]{3,2,1,0:T(8,128)(2,1)S(1)} %all-to-all-done.1._.far_own.panels), channel_id=1, source_target_pairs={{0,8},{8,0},{1,9},{9,1},{2,10},{10,2},{3,11},{11,3},{4,12},{12,4},... | collective-permute-start | bytes 4718600 | tf_op jit(solution)/shard_map/ppermute | solution.py:235
  72.2 1.9 %collective-permute-start.6 = (f32[3,256,128]{2,1,0:T(8,128)S(1)}, f32[3,256,128]{2,1,0:T(8,128)S(1)}, u32[]{:S(2)}, u32[]{:S(2)}) collective-permute-start(f32[3,256,128]{2,1,0:T(8,128)S(1)} %shard_map.168), channel_id=1, source_target_pairs={{0,8},{8,0},{1,9},{9,1},{2,10},{10,2},{3,11},{11,3},{4,12},{12,4},... | collective-permute-start | bytes 1179656 | tf_op jit(solution)/shard_map/ppermute | solution.py:235
  74.1 4.8 %all-to-all-start.2 = ((bf16[8,3,128,128]{3,2,1,0:T(8,128)(2,1)}), bf16[8,3,128,128]{3,2,1,0:T(8,128)(2,1)S(1)}, u32[]{:S(2)}, u32[]{:S(2)}) async-start(bf16[8,3,128,128]{3,2,1,0:T(8,128)(2,1)} %get-tuple-element.47), calls=%async_computation.2 | async-start | bytes 1572864 | tf_op jit(solution)/shard_map/all_to_all | solution.py:249
  78.9 4.0 %all-gather.5.cloned.1.call-done = bf16[32,64,1024]{2,1,0:T(8,128)(2,1)} async-done(((bf16[2,64,1024]{2,1,0:T(8,128)(2,1)}), bf16[32,64,1024]{2,1,0:T(8,128)(2,1)}) %all-gather.5.cloned.1.call-update) | async-done | bytes 4194320 | tf_op jit(solution)/shard_map/all_gather | solution.py:286
  82.9 6.6 %shard_map.169 = (bf16[512,1024]{1,0:T(8,128)(2,1)}, bf16[256,128]{1,0:T(8,128)(2,1)}, bf16[256,128]{1,0:T(8,128)(2,1)}) custom-call(s32[4,16]{1,0:T(4,128)} %leaf_fill.3, s32[2,32]{1,0:T(2,128)} %mid_fill.3, bf16[16,2,64,1024]{3,2,1,0:T(8,128)(2,1)} %bitcast.5, bf16[8,3,256,128]{3,2,1,0:T(8,128)(2,1)} %copy-done, ...), custom_call_target="tpu_custom_call" | custom-call | flops 2147483648 | bytes 4194304 | tf_op jit(solution)/shard_map/pallas_call | solution.py:25
  89.6 2.2 %collective-permute-start.8 = (bf16[512,1024]{1,0:T(8,128)(2,1)}, bf16[512,1024]{1,0:T(8,128)(2,1)S(1)}, u32[]{:S(2)}, u32[]{:S(2)}) collective-permute-start(bf16[512,1024]{1,0:T(8,128)(2,1)} %get-tuple-element.46.turned), channel_id=1, source_target_pairs={{0,8},{8,0},{1,9},{9,1},{2,10},{10,2},{3,11},{11,3},{4,12},{12,4},... | collective-permute-start | bytes 3145736 | tf_op jit(solution)/shard_map/ppermute | solution.py:235
  91.8 10.8 %all-to-all-done.2.blocks = bf16[8,3,128,128]{3,2,1,0:T(8,128)(2,1)S(1)} async-done(((bf16[8,3,128,128]{3,2,1,0:T(8,128)(2,1)}), bf16[8,3,128,128]{3,2,1,0:T(8,128)(2,1)S(1)}, u32[]{:S(2)}, u32[]{:S(2)}) %all-to-all-start.2) | async-done | bytes 786464 | tf_op jit(solution)/shard_map/all_to_all | solution.py:249
  102.6 0.9 copy-done.9
  103.5 1.0 copy-done.10
  104.5 4.0 %shard_map.171 = bf16[32,2,3,8,128]{4,3,2,1,0:T(8,128)(2,1)} custom-call(s32[4,16]{1,0:T(4,128)} %leaf_fill.3, s32[2,32]{1,0:T(2,128)} %mid_fill.3, bf16[512,1024]{1,0:T(8,128)(2,1)} %get-tuple-element.46.turned, bf16[512,1024]{1,0:T(8,128)(2,1)} %copy-done.10, bf16[8,3,128,128]{3,2,1,0:T(8,128)(2,1)} %copy-done.9, f32[256,256]{1,0:T(8,128)} %leaf.5, ...), custom_call_target="tpu_custom_call" | custom-call | tf_op jit(solution)/shard_map/pallas_call | solution.py:25
  108.5 17.1 %all_to_all.25.pieces = bf16[32,2,3,8,128]{4,3,2,1,0:T(8,128)(2,1)S(1)} all-to-all(bf16[32,2,3,8,128]{4,3,2,1,0:T(8,128)(2,1)} %shard_map.171), channel_id=1, replica_groups=mesh['pair'=2,'half'=2,'z'=8,'core'=2,'ylo'=2,'x'=4] {'pair','half','z'}, dimensions={0} | all-to-all | bytes 786432 | tf_op jit(solution)/shard_map/all_to_all | solution.py:249
  125.6 2.2 %shard_map.172 = bf16[64,4,8,128]{3,2,1,0:T(8,128)(2,1)} custom-call(s32[4,16]{1,0:T(4,128)S(1)} %copy-done.4, s32[2,32]{1,0:T(2,128)S(1)} %copy-done.5, bf16[32,2,3,8,128]{4,3,2,1,0:T(8,128)(2,1)S(1)} %all_to_all.25.pieces), custom_call_target="tpu_custom_call" | custom-call | tf_op jit(solution)/shard_map/pallas_call | solution.py:25
  127.8 10.5 %all-to-all-start.4 = ((bf16[64,4,8,128]{3,2,1,0:T(8,128)(2,1)}), bf16[64,4,8,128]{3,2,1,0:T(8,128)(2,1)S(1)}, u32[]{:S(2)}, u32[]{:S(2)}) async-start(bf16[64,4,8,128]{3,2,1,0:T(8,128)(2,1)} %shard_map.172), calls=%async_computation.4 | async-start | bytes 1048576 | tf_op jit(solution)/shard_map/all_to_all | solution.py:249
  138.3 2.4 %collective-permute-start.7 = (bf16[256,128]{1,0:T(8,128)(2,1)S(1)}, bf16[256,128]{1,0:T(8,128)(2,1)S(1)}, u32[]{:S(2)}, u32[]{:S(2)}) collective-permute-start(bf16[256,128]{1,0:T(8,128)(2,1)S(1)} %copy-done.13), channel_id=1, source_target_pairs={{0,8},{8,0},{1,9},{9,1},{2,10},{10,2},{3,11},{11,3},{4,12},{12,4},... | collective-permute-start | bytes 196616 | tf_op jit(solution)/shard_map/ppermute | solution.py:235
  140.7 0.9 collective-permute-done.7
  142.2 2.2 %copy-done.6 = bf16[256,64,128]{2,1,0:T(8,128)(2,1)S(1)} copy-done((bf16[256,64,128]{2,1,0:T(8,128)(2,1)S(1)}, bf16[256,64,128]{2,1,0:T(8,128)(2,1)}, u32[]{:S(2)}) %copy-start.6) | copy-done | bytes 4194328
  144.4 1.2 copy-done.7
  145.6 4.4 %shard_map.170 = (f32[256,1024]{1,0:T(8,128)S(1)}, bf16[256,128]{1,0:T(8,128)(2,1)}) custom-call(s32[64]{0:T(128)S(1)} %copy-done.8, bf16[8,3,256,128]{3,2,1,0:T(8,128)(2,1)S(1)} %copy-done.1, bf16[16,16,64,128]{3,2,1,0:T(8,128)(2,1)S(1)} %bitcast.4, f32[256,1024]{1,0:T(8,128)S(1)} %copy-done.7), custom_call_target="tpu_custom_call" | custom-call | flops 4294967296 | bytes 8388608 | tf_op jit(solution)/shard_map/pallas_call | solution.py:344
  150.0 7.0 %all-to-all-done.4 = bf16[64,4,8,128]{3,2,1,0:T(8,128)(2,1)S(1)} async-done(((bf16[64,4,8,128]{3,2,1,0:T(8,128)(2,1)}), bf16[64,4,8,128]{3,2,1,0:T(8,128)(2,1)S(1)}, u32[]{:S(2)}, u32[]{:S(2)}) %all-to-all-start.4) | async-done | bytes 524320 | tf_op jit(solution)/shard_map/all_to_all | solution.py:249
  157.1 1.7 %shard_map.173 = f32[256,1024]{1,0:T(8,128)} custom-call(f32[256,1024]{1,0:T(8,128)S(1)} %get-tuple-element.45.base, bf16[32,2,4,8,128]{4,3,2,1,0:T(8,128)(2,1)S(1)} %bitcast.3), custom_call_target="tpu_custom_call" | custom-call | tf_op jit(solution)/shard_map/pallas_call | solution.py:364
  (39 shorter events, 0.9 us)
Async XLA Ops:
  9.7 24.4 %all-to-all-start = ((bf16[8,3,64,128]{3,2,1,0:T(8,128)(2,1)}), bf16[8,3,64,128]{3,2,1,0:T(8,128)(2,1)S(1)}, u32[]{:S(2)}, u32[]{:S(2)}) async-start(bf16[8,3,64,128]{3,2,1,0:T(8,128)(2,1)} %get-tuple-element.27), calls=%async_computation | async-start | bytes 786432 | tf_op jit(solution)/shard_map/all_to_all | solution.py:249
  15.5 67.4 %all-gather.5.cloned.1.call-start = ((), (), s32[]{:S(2)}) async-start(), calls=%async_computation.5 | async-start | bytes 4456448 | tf_op jit(solution)/shard_map/all_gather | solution.py:286
  15.6 16.6 %collective-permute-start = (bf16[3,128,128]{2,1,0:T(8,128)(2,1)}, bf16[3,128,128]{2,1,0:T(8,128)(2,1)S(1)}, u32[]{:S(2)}, u32[]{:S(2)}) collective-permute-start(bf16[3,128,128]{2,1,0:T(8,128)(2,1)} %get-tuple-element.28), channel_id=1, source_target_pairs={{0,0},{1,16},{2,32},{3,48},{4,64},{5,80},{6,96},{7,112},{8,17},{9,... | collective-permute-start | bytes 294920 | tf_op jit(solution)/shard_map/ppermute | solution.py:245
  21.8 12.3 %collective-permute-start.1 = (bf16[3,128,128]{2,1,0:T(8,128)(2,1)}, bf16[3,128,128]{2,1,0:T(8,128)(2,1)S(1)}, u32[]{:S(2)}, u32[]{:S(2)}) collective-permute-start(bf16[3,128,128]{2,1,0:T(8,128)(2,1)} %get-tuple-element.29), channel_id=1, source_target_pairs={{0,8},{1,24},{2,40},{3,56},{4,72},{5,88},{6,104},{7,120},{8,25},{9... | collective-permute-start | bytes 294920 | tf_op jit(solution)/shard_map/ppermute | solution.py:245
  34.9 32.3 %all-to-all-start.1 = ((bf16[8,3,256,128]{3,2,1,0:T(8,128)(2,1)}), bf16[8,3,256,128]{3,2,1,0:T(8,128)(2,1)S(1)}, u32[]{:S(2)}, u32[]{:S(2)}) async-start(bf16[8,3,256,128]{3,2,1,0:T(8,128)(2,1)} %get-tuple-element.37), calls=%async_computation.1 | async-start | bytes 3145728 | tf_op jit(solution)/shard_map/all_to_all | solution.py:249
  42.3 29.8 %copy-start.2 = (f32[256,512]{1,0:T(8,128)S(1)}, f32[256,512]{1,0:T(8,128)}, u32[]{:S(2)}) copy-start(f32[256,512]{1,0:T(8,128)} %mid.5) | copy-start | bytes 1572868
  42.3 29.8 %copy-start.3 = (f32[256,256]{1,0:T(8,128)S(1)}, f32[256,256]{1,0:T(8,128)}, u32[]{:S(2)}) copy-start(f32[256,256]{1,0:T(8,128)} %leaf.5) | copy-start | bytes 786436
  42.4 99.8 %all-gather.7.cloned.1.call-start = ((), (), s32[]{:S(2)}) async-start(), calls=%async_computation.6 | async-start | bytes 4456448 | tf_op jit(solution)/shard_map/all_gather | solution.py:298
  42.4 24.8 %collective-permute-start.2 = (bf16[2,128,128]{2,1,0:T(8,128)(2,1)S(1)}, bf16[2,128,128]{2,1,0:T(8,128)(2,1)S(1)}, u32[]{:S(2)}, u32[]{:S(2)}) collective-permute-start(bf16[2,128,128]{2,1,0:T(8,128)(2,1)S(1)} %get-tuple-element.34), channel_id=1, source_target_pairs={{0,128},{128,0},{1,129},{129,1},{2,130},{130,2},{3,131},{131,3},{4... | collective-permute-start | bytes 196616 | tf_op jit(solution)/shard_map/ppermute | solution.py:235
  46.8 20.4 %collective-permute-start.3 = (bf16[128,128]{1,0:T(8,128)(2,1)S(1)}, bf16[128,128]{1,0:T(8,128)(2,1)S(1)}, u32[]{:S(2)}, u32[]{:S(2)}) collective-permute-start(bf16[128,128]{1,0:T(8,128)(2,1)S(1)} %get-tuple-element.35), channel_id=1, source_target_pairs={{0,256},{256,0},{1,257},{257,1},{2,258},{258,2},{3,259},{259,3},{4... | collective-permute-start | bytes 98312 | tf_op jit(solution)/shard_map/ppermute | solution.py:235
  51.5 15.7 %collective-permute-start.4 = (bf16[128,128]{1,0:T(8,128)(2,1)S(1)}, bf16[128,128]{1,0:T(8,128)(2,1)S(1)}, u32[]{:S(2)}, u32[]{:S(2)}) collective-permute-start(bf16[128,128]{1,0:T(8,128)(2,1)S(1)} %get-tuple-element.35), channel_id=1, source_target_pairs={{0,384},{128,256},{256,128},{384,0},{1,385},{129,257},{257,129},{3... | collective-permute-start | bytes 98312 | tf_op jit(solution)/shard_map/ppermute | solution.py:289
  67.2 5.0 %copy-start = (bf16[8,3,256,128]{3,2,1,0:T(8,128)(2,1)}, bf16[8,3,256,128]{3,2,1,0:T(8,128)(2,1)S(1)}, u32[]{:S(2)}) copy-start(bf16[8,3,256,128]{3,2,1,0:T(8,128)(2,1)S(1)} %all-to-all-done.1._.far_own.panels) | copy-start | bytes 4718596
  68.5 10.5 %collective-permute-start.5 = (bf16[8,3,256,128]{3,2,1,0:T(8,128)(2,1)S(1)}, bf16[8,3,256,128]{3,2,1,0:T(8,128)(2,1)}, u32[]{:S(2)}, u32[]{:S(2)}) collective-permute-start(bf16[8,3,256,128]{3,2,1,0:T(8,128)(2,1)S(1)} %all-to-all-done.1._.far_own.panels), channel_id=1, source_target_pairs={{0,8},{8,0},{1,9},{9,1},{2,10},{10,2},{3,11},{11,3},{4,12},{12,4},... | collective-permute-start | bytes 4718600 | tf_op jit(solution)/shard_map/ppermute | solution.py:235
  72.2 6.7 %collective-permute-start.6 = (f32[3,256,128]{2,1,0:T(8,128)S(1)}, f32[3,256,128]{2,1,0:T(8,128)S(1)}, u32[]{:S(2)}, u32[]{:S(2)}) collective-permute-start(f32[3,256,128]{2,1,0:T(8,128)S(1)} %shard_map.168), channel_id=1, source_target_pairs={{0,8},{8,0},{1,9},{9,1},{2,10},{10,2},{3,11},{11,3},{4,12},{12,4},... | collective-permute-start | bytes 1179656 | tf_op jit(solution)/shard_map/ppermute | solution.py:235
  74.1 28.4 %all-to-all-start.2 = ((bf16[8,3,128,128]{3,2,1,0:T(8,128)(2,1)}), bf16[8,3,128,128]{3,2,1,0:T(8,128)(2,1)S(1)}, u32[]{:S(2)}, u32[]{:S(2)}) async-start(bf16[8,3,128,128]{3,2,1,0:T(8,128)(2,1)} %get-tuple-element.47), calls=%async_computation.2 | async-start | bytes 1572864 | tf_op jit(solution)/shard_map/all_to_all | solution.py:249
  78.9 4.0 %copy-start.11 = (f32[3,256,128]{2,1,0:T(8,128)}, f32[3,256,128]{2,1,0:T(8,128)S(1)}, u32[]{:S(2)}) copy-start(f32[3,256,128]{2,1,0:T(8,128)S(1)} %collective-permute-done.6._.other_front) | copy-start | bytes 1179652
  89.6 36.1 %copy-start.4 = (s32[4,16]{1,0:T(4,128)S(1)}, s32[4,16]{1,0:T(4,128)}, u32[]{:S(2)}) copy-start(s32[4,16]{1,0:T(4,128)} %leaf_map.1) | copy-start | bytes 772
  89.6 36.1 %copy-start.5 = (s32[2,32]{1,0:T(2,128)S(1)}, s32[2,32]{1,0:T(2,128)}, u32[]{:S(2)}) copy-start(s32[2,32]{1,0:T(2,128)} %mid_map.1) | copy-start | bytes 772
  89.6 13.0 %collective-permute-start.8 = (bf16[512,1024]{1,0:T(8,128)(2,1)}, bf16[512,1024]{1,0:T(8,128)(2,1)S(1)}, u32[]{:S(2)}, u32[]{:S(2)}) collective-permute-start(bf16[512,1024]{1,0:T(8,128)(2,1)} %get-tuple-element.46.turned), channel_id=1, source_target_pairs={{0,8},{8,0},{1,9},{9,1},{2,10},{10,2},{3,11},{11,3},{4,12},{12,4},... | collective-permute-start | bytes 3145736 | tf_op jit(solution)/shard_map/ppermute | solution.py:235
  102.6 0.9 copy-start.9
  103.5 1.0 copy-start.10
  108.5 29.8 %copy-start.13 = (bf16[256,128]{1,0:T(8,128)(2,1)S(1)}, bf16[256,128]{1,0:T(8,128)(2,1)}, u32[]{:S(2)}) copy-start(bf16[256,128]{1,0:T(8,128)(2,1)} %get-tuple-element.42) | copy-start | bytes 196612
  108.5 33.0 %copy-start.12 = (bf16[256,128]{1,0:T(8,128)(2,1)S(1)}, bf16[256,128]{1,0:T(8,128)(2,1)}, u32[]{:S(2)}) copy-start(bf16[256,128]{1,0:T(8,128)(2,1)} %get-tuple-element.41) | copy-start | bytes 196612
  108.5 33.7 %copy-start.1 = (bf16[8,3,256,128]{3,2,1,0:T(8,128)(2,1)S(1)}, bf16[8,3,256,128]{3,2,1,0:T(8,128)(2,1)}, u32[]{:S(2)}) copy-start(bf16[8,3,256,128]{3,2,1,0:T(8,128)(2,1)} %copy-done) | copy-start | bytes 4718596
  108.5 33.7 %copy-start.8 = (s32[64]{0:T(128)S(1)}, s32[64]{0:T(128)}, u32[]{:S(2)}) copy-start(s32[64]{0:T(128)} %fill.1) | copy-start | bytes 772
  127.8 29.2 %all-to-all-start.4 = ((bf16[64,4,8,128]{3,2,1,0:T(8,128)(2,1)}), bf16[64,4,8,128]{3,2,1,0:T(8,128)(2,1)S(1)}, u32[]{:S(2)}, u32[]{:S(2)}) async-start(bf16[64,4,8,128]{3,2,1,0:T(8,128)(2,1)} %shard_map.172), calls=%async_computation.4 | async-start | bytes 1048576 | tf_op jit(solution)/shard_map/all_to_all | solution.py:249
  138.3 3.3 %collective-permute-start.7 = (bf16[256,128]{1,0:T(8,128)(2,1)S(1)}, bf16[256,128]{1,0:T(8,128)(2,1)S(1)}, u32[]{:S(2)}, u32[]{:S(2)}) collective-permute-start(bf16[256,128]{1,0:T(8,128)(2,1)S(1)} %copy-done.13), channel_id=1, source_target_pairs={{0,8},{8,0},{1,9},{9,1},{2,10},{10,2},{3,11},{11,3},{4,12},{12,4},... | collective-permute-start | bytes 196616 | tf_op jit(solution)/shard_map/ppermute | solution.py:235
  142.2 2.2 %copy-start.6 = (bf16[256,64,128]{2,1,0:T(8,128)(2,1)S(1)}, bf16[256,64,128]{2,1,0:T(8,128)(2,1)}, u32[]{:S(2)}) copy-start(bf16[256,64,128]{2,1,0:T(8,128)(2,1)} %all-gather.7.cloned.1.call-done) | copy-start | bytes 12582916
  144.4 1.2 copy-start.7
Sparse Core Ops, SparseCore 0:
  35.0 47.8 all-gather.4
  85.1 54.0 all-gather.6

commit v6 on v5

--- a/solution.py
+++ b/solution.py
@@ -324,7 +324,7 @@
         update_kernel,
         shape((32, 2, 3, 8, 128)),
         (leaf_fill, mid_fill, turned, other_turned, blocks, leaf_front, mid_front, other_front),
-        60,
+        44,
         scratch=(pltpu.VMEM((3, 128, 1024), BF),),
     )
     given = swap(give, "core")

time: 167 us -> 166 us (level)
  Pallas kernels: 23.4 us -> 21.7 us
    all_to_all x4, waiting for transfers between devices: 17.8 us -> 19.8 us  [exchange(): return lax.all_to_all(value, axes, 0, 0, tiled=True)]
    pallas_call x7, Pallas kernels: 17.3 us -> 15.6 us  [call(): pl.pallas_call(kernel, out_shape=outs, in_specs=[SMEM] * tables + [VMEM]...]
    unnamed x28 -> x34, local copies, waits for them, and re-layouts: 5.37 us -> 6.62 us
  transfers between devices with their start and end apart: 15 -> 15, of which waited for: 6 -> 6; matrix products, arithmetic and copies ran while one was open for 0% -> 0% of each run, Pallas kernels for 11% -> 10%
where the time goes in v6:
time: 166 us; the launch traced here: 165 us
  starting transfers between devices  66.7 us (40%)
  waiting for transfers between devices  38.5 us (23%)
  Pallas kernels  21.7 us (13%)
  blocking collectives  16.3 us (10%)
  between operations  14.3 us (9%)
  local copies, waits for them, and re-layouts  6.62 us (4%)
    all_to_all x4, starting transfers between devices, exchange(): return lax.all_to_all(value, axes, 0, 0, tiled=True)  28.4 us
    all_to_all x4, waiting for transfers between devices, exchange(): return lax.all_to_all(value, axes, 0, 0, tiled=True)  19.8 us
    ppermute x6, starting transfers between devices, swap(): return lax.ppermute(value, axis, [(0, 1), (1, 0)])  19.2 us
    all_to_all x1, blocking collectives, exchange(): return lax.all_to_all(value, axes, 0, 0, tiled=True)  16.3 us
    pallas_call x7, Pallas kernels, call(): pl.pallas_call(kernel, out_shape=outs, in_specs=[SMEM] * tables + [VMEM]...  15.6 us
    ppermute x6, waiting for transfers between devices, swap(): return lax.ppermute(value, axis, [(0, 1), (1, 0)])  14.2 us
    ppermute x1, starting transfers between devices, transpose(): lax.ppermute(high, plane, pairs[1])  10.3 us
    unnamed x34, local copies, waits for them, and re-layouts  6.62 us
  transfers between devices with their start and end apart: 15, of which 6 were waited for; matrix products, arithmetic and copies ran while one was open for 0% of the time, Pallas kernels for 10%

profile of v6, /device:TPU:1, one launch (start us, length us, event | category | flops | bytes accessed | tf_op | source)
XLA Modules:
  0.0 164.7 jit_solution(17967320926497030006)
XLA Ops:
  7.2 2.5 %shard_map.165 = (bf16[8,3,64,128]{3,2,1,0:T(8,128)(2,1)}, bf16[8,3,256,128]{3,2,1,0:T(8,128)(2,1)}, bf16[3,128,128]{2,1,0:T(8,128)(2,1)}, bf16[3,128,128]{2,1,0:T(8,128)(2,1)}) custom-call(bf16[1,64,128]{2,1,0:T(8,128)(2,1)} %leaf.3, bf16[2,64,128]{2,1,0:T(8,128)(2,1)} %mid.3, bf16[64,128]{1,0:T(8,128)(2,1)} %root.1, bf16[256,128]{1,0:T(8,128)(2,1)} %leaf_panel.1, ...), custom_call_target="tpu_custom_call" | custom-call | tf_op jit(solution)/shard_map/pallas_call | solution.py:25
  9.7 5.9 %all-to-all-start = ((bf16[8,3,64,128]{3,2,1,0:T(8,128)(2,1)}), bf16[8,3,64,128]{3,2,1,0:T(8,128)(2,1)S(1)}, u32[]{:S(2)}, u32[]{:S(2)}) async-start(bf16[8,3,64,128]{3,2,1,0:T(8,128)(2,1)} %get-tuple-element.27), calls=%async_computation | async-start | bytes 786432 | tf_op jit(solution)/shard_map/all_to_all | solution.py:249
  15.6 6.2 %collective-permute-start = (bf16[3,128,128]{2,1,0:T(8,128)(2,1)}, bf16[3,128,128]{2,1,0:T(8,128)(2,1)S(1)}, u32[]{:S(2)}, u32[]{:S(2)}) collective-permute-start(bf16[3,128,128]{2,1,0:T(8,128)(2,1)} %get-tuple-element.28), channel_id=1, source_target_pairs={{0,0},{1,16},{2,32},{3,48},{4,64},{5,80},{6,96},{7,112},{8,17},{9,... | collective-permute-start | bytes 294920 | tf_op jit(solution)/shard_map/ppermute | solution.py:245
  21.8 10.3 %collective-permute-start.1 = (bf16[3,128,128]{2,1,0:T(8,128)(2,1)}, bf16[3,128,128]{2,1,0:T(8,128)(2,1)S(1)}, u32[]{:S(2)}, u32[]{:S(2)}) collective-permute-start(bf16[3,128,128]{2,1,0:T(8,128)(2,1)} %get-tuple-element.29), channel_id=1, source_target_pairs={{0,8},{1,24},{2,40},{3,56},{4,72},{5,88},{6,104},{7,120},{8,25},{9... | collective-permute-start | bytes 294920 | tf_op jit(solution)/shard_map/ppermute | solution.py:245
  32.2 1.9 %collective-permute-done.1.high = bf16[3,128,128]{2,1,0:T(8,128)(2,1)S(1)} collective-permute-done((bf16[3,128,128]{2,1,0:T(8,128)(2,1)}, bf16[3,128,128]{2,1,0:T(8,128)(2,1)S(1)}, u32[]{:S(2)}, u32[]{:S(2)}) %collective-permute-start.1) | collective-permute-done | bytes 98336 | tf_op jit(solution)/shard_map/ppermute | solution.py:245
  34.9 7.4 %all-to-all-start.1 = ((bf16[8,3,256,128]{3,2,1,0:T(8,128)(2,1)}), bf16[8,3,256,128]{3,2,1,0:T(8,128)(2,1)S(1)}, u32[]{:S(2)}, u32[]{:S(2)}) async-start(bf16[8,3,256,128]{3,2,1,0:T(8,128)(2,1)} %get-tuple-element.37), calls=%async_computation.1 | async-start | bytes 3145728 | tf_op jit(solution)/shard_map/all_to_all | solution.py:249
  42.4 4.3 %collective-permute-start.2 = (bf16[2,128,128]{2,1,0:T(8,128)(2,1)S(1)}, bf16[2,128,128]{2,1,0:T(8,128)(2,1)S(1)}, u32[]{:S(2)}, u32[]{:S(2)}) collective-permute-start(bf16[2,128,128]{2,1,0:T(8,128)(2,1)S(1)} %get-tuple-element.34), channel_id=1, source_target_pairs={{0,128},{128,0},{1,129},{129,1},{2,130},{130,2},{3,131},{131,3},{4... | collective-permute-start | bytes 196616 | tf_op jit(solution)/shard_map/ppermute | solution.py:235
  46.8 4.8 %collective-permute-start.3 = (bf16[128,128]{1,0:T(8,128)(2,1)S(1)}, bf16[128,128]{1,0:T(8,128)(2,1)S(1)}, u32[]{:S(2)}, u32[]{:S(2)}) collective-permute-start(bf16[128,128]{1,0:T(8,128)(2,1)S(1)} %get-tuple-element.35), channel_id=1, source_target_pairs={{0,256},{256,0},{1,257},{257,1},{2,258},{258,2},{3,259},{259,3},{4... | collective-permute-start | bytes 98312 | tf_op jit(solution)/shard_map/ppermute | solution.py:235
  51.5 2.4 %collective-permute-start.4 = (bf16[128,128]{1,0:T(8,128)(2,1)S(1)}, bf16[128,128]{1,0:T(8,128)(2,1)S(1)}, u32[]{:S(2)}, u32[]{:S(2)}) collective-permute-start(bf16[128,128]{1,0:T(8,128)(2,1)S(1)} %get-tuple-element.35), channel_id=1, source_target_pairs={{0,384},{128,256},{256,128},{384,0},{1,385},{129,257},{257,129},{3... | collective-permute-start | bytes 98312 | tf_op jit(solution)/shard_map/ppermute | solution.py:289
  53.9 13.3 %collective-permute-done.3.across = bf16[128,128]{1,0:T(8,128)(2,1)S(1)} collective-permute-done((bf16[128,128]{1,0:T(8,128)(2,1)S(1)}, bf16[128,128]{1,0:T(8,128)(2,1)S(1)}, u32[]{:S(2)}, u32[]{:S(2)}) %collective-permute-start.3) | collective-permute-done | bytes 32800 | tf_op jit(solution)/shard_map/ppermute | solution.py:235
  67.2 0.9 shard_map.167
  68.2 0.9 copy-done.5
  69.1 3.6 %collective-permute-start.5 = (bf16[8,3,256,128]{3,2,1,0:T(8,128)(2,1)S(1)}, bf16[8,3,256,128]{3,2,1,0:T(8,128)(2,1)}, u32[]{:S(2)}, u32[]{:S(2)}) collective-permute-start(bf16[8,3,256,128]{3,2,1,0:T(8,128)(2,1)S(1)} %all-to-all-done.1._.far_own.panels), channel_id=1, source_target_pairs={{0,8},{8,0},{1,9},{9,1},{2,10},{10,2},{3,11},{11,3},{4,12},{12,4},... | collective-permute-start | bytes 4718600 | tf_op jit(solution)/shard_map/ppermute | solution.py:235
  73.5 1.9 %collective-permute-start.6 = (f32[3,256,128]{2,1,0:T(8,128)}, f32[3,256,128]{2,1,0:T(8,128)S(1)}, u32[]{:S(2)}, u32[]{:S(2)}) collective-permute-start(f32[3,256,128]{2,1,0:T(8,128)} %shard_map.168), channel_id=1, source_target_pairs={{0,8},{8,0},{1,9},{9,1},{2,10},{10,2},{3,11},{11,3},{4,12},{12,4},... | collective-permute-start | bytes 1179656 | tf_op jit(solution)/shard_map/ppermute | solution.py:235
  75.5 4.8 %all-to-all-start.2 = ((bf16[8,3,128,128]{3,2,1,0:T(8,128)(2,1)}), bf16[8,3,128,128]{3,2,1,0:T(8,128)(2,1)S(1)}, u32[]{:S(2)}, u32[]{:S(2)}) async-start(bf16[8,3,128,128]{3,2,1,0:T(8,128)(2,1)} %copy-done.5), calls=%async_computation.2 | async-start | bytes 1572864 | tf_op jit(solution)/shard_map/all_to_all | solution.py:249
  80.3 2.7 %all-gather.5.cloned.1.call-done = bf16[32,64,1024]{2,1,0:T(8,128)(2,1)} async-done(((bf16[2,64,1024]{2,1,0:T(8,128)(2,1)}), bf16[32,64,1024]{2,1,0:T(8,128)(2,1)}) %all-gather.5.cloned.1.call-update) | async-done | bytes 4194320 | tf_op jit(solution)/shard_map/all_gather | solution.py:286
  83.0 6.7 %shard_map.169 = (bf16[512,1024]{1,0:T(8,128)(2,1)}, bf16[256,128]{1,0:T(8,128)(2,1)}, bf16[256,128]{1,0:T(8,128)(2,1)}) custom-call(s32[4,16]{1,0:T(4,128)} %leaf_fill.3, s32[2,32]{1,0:T(2,128)} %mid_fill.3, bf16[16,2,64,1024]{3,2,1,0:T(8,128)(2,1)} %bitcast.5, bf16[8,3,256,128]{3,2,1,0:T(8,128)(2,1)} %copy-done, ...), custom_call_target="tpu_custom_call" | custom-call | flops 2147483648 | bytes 4194304 | tf_op jit(solution)/shard_map/pallas_call | solution.py:25
  89.7 2.2 %collective-permute-start.8 = (bf16[512,1024]{1,0:T(8,128)(2,1)}, bf16[512,1024]{1,0:T(8,128)(2,1)S(1)}, u32[]{:S(2)}, u32[]{:S(2)}) collective-permute-start(bf16[512,1024]{1,0:T(8,128)(2,1)} %get-tuple-element.46.turned), channel_id=1, source_target_pairs={{0,8},{8,0},{1,9},{9,1},{2,10},{10,2},{3,11},{11,3},{4,12},{12,4},... | collective-permute-start | bytes 3145736 | tf_op jit(solution)/shard_map/ppermute | solution.py:235
  91.9 12.0 %all-to-all-done.2.blocks = bf16[8,3,128,128]{3,2,1,0:T(8,128)(2,1)S(1)} async-done(((bf16[8,3,128,128]{3,2,1,0:T(8,128)(2,1)}), bf16[8,3,128,128]{3,2,1,0:T(8,128)(2,1)S(1)}, u32[]{:S(2)}, u32[]{:S(2)}) %all-to-all-start.2) | async-done | bytes 786464 | tf_op jit(solution)/shard_map/all_to_all | solution.py:249
  103.9 1.2 copy-done.3
  105.1 1.0 copy-done.7
  106.2 1.7 %shard_map.171 = bf16[32,2,3,8,128]{4,3,2,1,0:T(8,128)(2,1)S(1)} custom-call(s32[4,16]{1,0:T(4,128)S(1)} %copy-done.8, s32[2,32]{1,0:T(2,128)S(1)} %copy-done.10, bf16[512,1024]{1,0:T(8,128)(2,1)S(1)} %copy-done.3, bf16[512,1024]{1,0:T(8,128)(2,1)S(1)} %collective-permute-done.8.other_turned, bf16[8,3,128,128]{3,2,1,0:T(8,128)(2,1)S(1)} %all-to-all-done.2.blocks, ...), custom_call_target="tpu_custom_call" | custom-call | tf_op jit(solution)/shard_map/pallas_call | solution.py:25
  107.9 16.3 %all_to_all.25.pieces = bf16[32,2,3,8,128]{4,3,2,1,0:T(8,128)(2,1)S(1)} all-to-all(bf16[32,2,3,8,128]{4,3,2,1,0:T(8,128)(2,1)S(1)} %shard_map.171), channel_id=1, replica_groups=mesh['pair'=2,'half'=2,'z'=8,'core'=2,'ylo'=2,'x'=4] {'pair','half','z'}, dimensions={0} | all-to-all | bytes 786432 | tf_op jit(solution)/shard_map/all_to_all | solution.py:249
  124.2 2.2 %shard_map.172 = bf16[64,4,8,128]{3,2,1,0:T(8,128)(2,1)} custom-call(s32[4,16]{1,0:T(4,128)S(1)} %copy-done.9, s32[2,32]{1,0:T(2,128)S(1)} %copy-done.11, bf16[32,2,3,8,128]{4,3,2,1,0:T(8,128)(2,1)S(1)} %all_to_all.25.pieces), custom_call_target="tpu_custom_call" | custom-call | tf_op jit(solution)/shard_map/pallas_call | solution.py:25
  126.3 10.4 %all-to-all-start.4 = ((bf16[64,4,8,128]{3,2,1,0:T(8,128)(2,1)}), bf16[64,4,8,128]{3,2,1,0:T(8,128)(2,1)S(1)}, u32[]{:S(2)}, u32[]{:S(2)}) async-start(bf16[64,4,8,128]{3,2,1,0:T(8,128)(2,1)} %shard_map.172), calls=%async_computation.4 | async-start | bytes 1048576 | tf_op jit(solution)/shard_map/all_to_all | solution.py:249
  136.7 2.4 %collective-permute-start.7 = (bf16[256,128]{1,0:T(8,128)(2,1)S(1)}, bf16[256,128]{1,0:T(8,128)(2,1)S(1)}, u32[]{:S(2)}, u32[]{:S(2)}) collective-permute-start(bf16[256,128]{1,0:T(8,128)(2,1)S(1)} %copy-done.16), channel_id=1, source_target_pairs={{0,8},{8,0},{1,9},{9,1},{2,10},{10,2},{3,11},{11,3},{4,12},{12,4},... | collective-permute-start | bytes 196616 | tf_op jit(solution)/shard_map/ppermute | solution.py:235
  139.1 0.9 collective-permute-done.7
  140.6 2.2 %copy-done.12 = bf16[256,64,128]{2,1,0:T(8,128)(2,1)S(1)} copy-done((bf16[256,64,128]{2,1,0:T(8,128)(2,1)S(1)}, bf16[256,64,128]{2,1,0:T(8,128)(2,1)}, u32[]{:S(2)}) %copy-start.12) | copy-done | bytes 4194328
  142.8 1.2 copy-done.13
  144.0 4.4 %shard_map.170 = (f32[256,1024]{1,0:T(8,128)S(1)}, bf16[256,128]{1,0:T(8,128)(2,1)}) custom-call(s32[64]{0:T(128)S(1)} %copy-done.14, bf16[8,3,256,128]{3,2,1,0:T(8,128)(2,1)S(1)} %copy-done.1, bf16[16,16,64,128]{3,2,1,0:T(8,128)(2,1)S(1)} %bitcast.4, f32[256,1024]{1,0:T(8,128)S(1)} %copy-done.13), custom_call_target="tpu_custom_call" | custom-call | flops 4294967296 | bytes 8388608 | tf_op jit(solution)/shard_map/pallas_call | solution.py:344
  148.5 7.8 %all-to-all-done.4 = bf16[64,4,8,128]{3,2,1,0:T(8,128)(2,1)S(1)} async-done(((bf16[64,4,8,128]{3,2,1,0:T(8,128)(2,1)}), bf16[64,4,8,128]{3,2,1,0:T(8,128)(2,1)S(1)}, u32[]{:S(2)}, u32[]{:S(2)}) %all-to-all-start.4) | async-done | bytes 524320 | tf_op jit(solution)/shard_map/all_to_all | solution.py:249
  156.2 1.7 %shard_map.173 = f32[256,1024]{1,0:T(8,128)} custom-call(f32[256,1024]{1,0:T(8,128)S(1)} %get-tuple-element.45.base, bf16[32,2,4,8,128]{4,3,2,1,0:T(8,128)(2,1)S(1)} %bitcast.3), custom_call_target="tpu_custom_call" | custom-call | tf_op jit(solution)/shard_map/pallas_call | solution.py:364
  (45 shorter events, 2.5 us)
Async XLA Ops:
  9.7 24.4 %all-to-all-start = ((bf16[8,3,64,128]{3,2,1,0:T(8,128)(2,1)}), bf16[8,3,64,128]{3,2,1,0:T(8,128)(2,1)S(1)}, u32[]{:S(2)}, u32[]{:S(2)}) async-start(bf16[8,3,64,128]{3,2,1,0:T(8,128)(2,1)} %get-tuple-element.27), calls=%async_computation | async-start | bytes 786432 | tf_op jit(solution)/shard_map/all_to_all | solution.py:249
  15.5 67.4 %all-gather.5.cloned.1.call-start = ((), (), s32[]{:S(2)}) async-start(), calls=%async_computation.5 | async-start | bytes 4456448 | tf_op jit(solution)/shard_map/all_gather | solution.py:286
  15.6 16.6 %collective-permute-start = (bf16[3,128,128]{2,1,0:T(8,128)(2,1)}, bf16[3,128,128]{2,1,0:T(8,128)(2,1)S(1)}, u32[]{:S(2)}, u32[]{:S(2)}) collective-permute-start(bf16[3,128,128]{2,1,0:T(8,128)(2,1)} %get-tuple-element.28), channel_id=1, source_target_pairs={{0,0},{1,16},{2,32},{3,48},{4,64},{5,80},{6,96},{7,112},{8,17},{9,... | collective-permute-start | bytes 294920 | tf_op jit(solution)/shard_map/ppermute | solution.py:245
  21.8 12.3 %collective-permute-start.1 = (bf16[3,128,128]{2,1,0:T(8,128)(2,1)}, bf16[3,128,128]{2,1,0:T(8,128)(2,1)S(1)}, u32[]{:S(2)}, u32[]{:S(2)}) collective-permute-start(bf16[3,128,128]{2,1,0:T(8,128)(2,1)} %get-tuple-element.29), channel_id=1, source_target_pairs={{0,8},{1,24},{2,40},{3,56},{4,72},{5,88},{6,104},{7,120},{8,25},{9... | collective-permute-start | bytes 294920 | tf_op jit(solution)/shard_map/ppermute | solution.py:245
  34.9 32.3 %all-to-all-start.1 = ((bf16[8,3,256,128]{3,2,1,0:T(8,128)(2,1)}), bf16[8,3,256,128]{3,2,1,0:T(8,128)(2,1)S(1)}, u32[]{:S(2)}, u32[]{:S(2)}) async-start(bf16[8,3,256,128]{3,2,1,0:T(8,128)(2,1)} %get-tuple-element.37), calls=%async_computation.1 | async-start | bytes 3145728 | tf_op jit(solution)/shard_map/all_to_all | solution.py:249
  42.3 30.4 %copy-start.2 = (f32[256,512]{1,0:T(8,128)S(1)}, f32[256,512]{1,0:T(8,128)}, u32[]{:S(2)}) copy-start(f32[256,512]{1,0:T(8,128)} %mid.5) | copy-start | bytes 1572868
  42.3 30.4 %copy-start.4 = (f32[256,256]{1,0:T(8,128)S(1)}, f32[256,256]{1,0:T(8,128)}, u32[]{:S(2)}) copy-start(f32[256,256]{1,0:T(8,128)} %leaf.5) | copy-start | bytes 786436
  42.4 98.3 %all-gather.7.cloned.1.call-start = ((), (), s32[]{:S(2)}) async-start(), calls=%async_computation.6 | async-start | bytes 4456448 | tf_op jit(solution)/shard_map/all_gather | solution.py:298
  42.4 24.8 %collective-permute-start.2 = (bf16[2,128,128]{2,1,0:T(8,128)(2,1)S(1)}, bf16[2,128,128]{2,1,0:T(8,128)(2,1)S(1)}, u32[]{:S(2)}, u32[]{:S(2)}) collective-permute-start(bf16[2,128,128]{2,1,0:T(8,128)(2,1)S(1)} %get-tuple-element.34), channel_id=1, source_target_pairs={{0,128},{128,0},{1,129},{129,1},{2,130},{130,2},{3,131},{131,3},{4... | collective-permute-start | bytes 196616 | tf_op jit(solution)/shard_map/ppermute | solution.py:235
  46.8 20.4 %collective-permute-start.3 = (bf16[128,128]{1,0:T(8,128)(2,1)S(1)}, bf16[128,128]{1,0:T(8,128)(2,1)S(1)}, u32[]{:S(2)}, u32[]{:S(2)}) collective-permute-start(bf16[128,128]{1,0:T(8,128)(2,1)S(1)} %get-tuple-element.35), channel_id=1, source_target_pairs={{0,256},{256,0},{1,257},{257,1},{2,258},{258,2},{3,259},{259,3},{4... | collective-permute-start | bytes 98312 | tf_op jit(solution)/shard_map/ppermute | solution.py:235
  51.5 15.7 %collective-permute-start.4 = (bf16[128,128]{1,0:T(8,128)(2,1)S(1)}, bf16[128,128]{1,0:T(8,128)(2,1)S(1)}, u32[]{:S(2)}, u32[]{:S(2)}) collective-permute-start(bf16[128,128]{1,0:T(8,128)(2,1)S(1)} %get-tuple-element.35), channel_id=1, source_target_pairs={{0,384},{128,256},{256,128},{384,0},{1,385},{129,257},{257,129},{3... | collective-permute-start | bytes 98312 | tf_op jit(solution)/shard_map/ppermute | solution.py:289
  67.2 6.3 %copy-start = (bf16[8,3,256,128]{3,2,1,0:T(8,128)(2,1)}, bf16[8,3,256,128]{3,2,1,0:T(8,128)(2,1)S(1)}, u32[]{:S(2)}) copy-start(bf16[8,3,256,128]{3,2,1,0:T(8,128)(2,1)S(1)} %all-to-all-done.1._.far_own.panels) | copy-start | bytes 4718596
  68.2 0.9 copy-start.5
  69.1 11.2 %collective-permute-start.5 = (bf16[8,3,256,128]{3,2,1,0:T(8,128)(2,1)S(1)}, bf16[8,3,256,128]{3,2,1,0:T(8,128)(2,1)}, u32[]{:S(2)}, u32[]{:S(2)}) collective-permute-start(bf16[8,3,256,128]{3,2,1,0:T(8,128)(2,1)S(1)} %all-to-all-done.1._.far_own.panels), channel_id=1, source_target_pairs={{0,8},{8,0},{1,9},{9,1},{2,10},{10,2},{3,11},{11,3},{4,12},{12,4},... | collective-permute-start | bytes 4718600 | tf_op jit(solution)/shard_map/ppermute | solution.py:235
  73.5 6.7 %collective-permute-start.6 = (f32[3,256,128]{2,1,0:T(8,128)}, f32[3,256,128]{2,1,0:T(8,128)S(1)}, u32[]{:S(2)}, u32[]{:S(2)}) collective-permute-start(f32[3,256,128]{2,1,0:T(8,128)} %shard_map.168), channel_id=1, source_target_pairs={{0,8},{8,0},{1,9},{9,1},{2,10},{10,2},{3,11},{11,3},{4,12},{12,4},... | collective-permute-start | bytes 1179656 | tf_op jit(solution)/shard_map/ppermute | solution.py:235
  75.5 28.4 %all-to-all-start.2 = ((bf16[8,3,128,128]{3,2,1,0:T(8,128)(2,1)}), bf16[8,3,128,128]{3,2,1,0:T(8,128)(2,1)S(1)}, u32[]{:S(2)}, u32[]{:S(2)}) async-start(bf16[8,3,128,128]{3,2,1,0:T(8,128)(2,1)} %copy-done.5), calls=%async_computation.2 | async-start | bytes 1572864 | tf_op jit(solution)/shard_map/all_to_all | solution.py:249
  80.3 2.7 %copy-start.6 = (f32[3,256,128]{2,1,0:T(8,128)}, f32[3,256,128]{2,1,0:T(8,128)S(1)}, u32[]{:S(2)}) copy-start(f32[3,256,128]{2,1,0:T(8,128)S(1)} %collective-permute-done.6._.other_front) | copy-start | bytes 1179652
  82.9 21.0 %copy-start.8 = (s32[4,16]{1,0:T(4,128)S(1)}, s32[4,16]{1,0:T(4,128)}, u32[]{:S(2)}) copy-start(s32[4,16]{1,0:T(4,128)} %leaf_fill.3) | copy-start | bytes 772
  82.9 21.0 %copy-start.10 = (s32[2,32]{1,0:T(2,128)S(1)}, s32[2,32]{1,0:T(2,128)}, u32[]{:S(2)}) copy-start(s32[2,32]{1,0:T(2,128)} %mid_fill.3) | copy-start | bytes 772
  82.9 41.2 %copy-start.9 = (s32[4,16]{1,0:T(4,128)S(1)}, s32[4,16]{1,0:T(4,128)}, u32[]{:S(2)}) copy-start(s32[4,16]{1,0:T(4,128)} %leaf_map.1) | copy-start | bytes 772
  89.7 34.5 %copy-start.11 = (s32[2,32]{1,0:T(2,128)S(1)}, s32[2,32]{1,0:T(2,128)}, u32[]{:S(2)}) copy-start(s32[2,32]{1,0:T(2,128)} %mid_map.1) | copy-start | bytes 772
  89.7 14.2 %collective-permute-start.8 = (bf16[512,1024]{1,0:T(8,128)(2,1)}, bf16[512,1024]{1,0:T(8,128)(2,1)S(1)}, u32[]{:S(2)}, u32[]{:S(2)}) collective-permute-start(bf16[512,1024]{1,0:T(8,128)(2,1)} %get-tuple-element.46.turned), channel_id=1, source_target_pairs={{0,8},{8,0},{1,9},{9,1},{2,10},{10,2},{3,11},{11,3},{4,12},{12,4},... | collective-permute-start | bytes 3145736 | tf_op jit(solution)/shard_map/ppermute | solution.py:235
  103.9 1.2 copy-start.3
  105.1 1.0 copy-start.7
  107.8 28.9 %copy-start.16 = (bf16[256,128]{1,0:T(8,128)(2,1)S(1)}, bf16[256,128]{1,0:T(8,128)(2,1)}, u32[]{:S(2)}) copy-start(bf16[256,128]{1,0:T(8,128)(2,1)} %get-tuple-element.42) | copy-start | bytes 196612
  107.9 32.1 %copy-start.15 = (bf16[256,128]{1,0:T(8,128)(2,1)S(1)}, bf16[256,128]{1,0:T(8,128)(2,1)}, u32[]{:S(2)}) copy-start(bf16[256,128]{1,0:T(8,128)(2,1)} %get-tuple-element.41) | copy-start | bytes 196612
  107.9 32.8 %copy-start.1 = (bf16[8,3,256,128]{3,2,1,0:T(8,128)(2,1)S(1)}, bf16[8,3,256,128]{3,2,1,0:T(8,128)(2,1)}, u32[]{:S(2)}) copy-start(bf16[8,3,256,128]{3,2,1,0:T(8,128)(2,1)} %copy-done) | copy-start | bytes 4718596
  107.9 32.8 %copy-start.14 = (s32[64]{0:T(128)S(1)}, s32[64]{0:T(128)}, u32[]{:S(2)}) copy-start(s32[64]{0:T(128)} %fill.1) | copy-start | bytes 772
  126.3 29.9 %all-to-all-start.4 = ((bf16[64,4,8,128]{3,2,1,0:T(8,128)(2,1)}), bf16[64,4,8,128]{3,2,1,0:T(8,128)(2,1)S(1)}, u32[]{:S(2)}, u32[]{:S(2)}) async-start(bf16[64,4,8,128]{3,2,1,0:T(8,128)(2,1)} %shard_map.172), calls=%async_computation.4 | async-start | bytes 1048576 | tf_op jit(solution)/shard_map/all_to_all | solution.py:249
  136.7 3.3 %collective-permute-start.7 = (bf16[256,128]{1,0:T(8,128)(2,1)S(1)}, bf16[256,128]{1,0:T(8,128)(2,1)S(1)}, u32[]{:S(2)}, u32[]{:S(2)}) collective-permute-start(bf16[256,128]{1,0:T(8,128)(2,1)S(1)} %copy-done.16), channel_id=1, source_target_pairs={{0,8},{8,0},{1,9},{9,1},{2,10},{10,2},{3,11},{11,3},{4,12},{12,4},... | collective-permute-start | bytes 196616 | tf_op jit(solution)/shard_map/ppermute | solution.py:235
  140.6 2.2 %copy-start.12 = (bf16[256,64,128]{2,1,0:T(8,128)(2,1)S(1)}, bf16[256,64,128]{2,1,0:T(8,128)(2,1)}, u32[]{:S(2)}) copy-start(bf16[256,64,128]{2,1,0:T(8,128)(2,1)} %all-gather.7.cloned.1.call-done) | copy-start | bytes 12582916
  142.8 1.2 copy-start.13
Sparse Core Ops, SparseCore 0:
  35.0 47.8 all-gather.4
  85.1 52.2 all-gather.6

commit v7 on v6

--- a/solution.py
+++ b/solution.py
@@ -305,7 +305,7 @@
         factor_kernel,
         (shape((512, 1024)), piece, piece),
         (leaf_fill, mid_fill),
-        60,
+        44,
         scratch=(
             pltpu.VMEM((512, 1024), BF),
             pltpu.VMEM((512, 1024), BF),

time: 166 us -> 166 us (level)
  blocking collectives: 16.3 us -> 20.7 us
  starting transfers between devices: 66.7 us -> 64 us
  waiting for transfers between devices: 38.5 us -> 36 us
    all_to_all x1, blocking collectives: 16.3 us -> 20.7 us  [exchange(): return lax.all_to_all(value, axes, 0, 0, tiled=True)]
    all_to_all x4, starting transfers between devices: 28.4 us -> 25.6 us  [exchange(): return lax.all_to_all(value, axes, 0, 0, tiled=True)]
    all_to_all x4, waiting for transfers between devices: 19.8 us -> 17.1 us  [exchange(): return lax.all_to_all(value, axes, 0, 0, tiled=True)]
    unnamed x34 -> x30, local copies, waits for them, and re-layouts: 6.62 us -> 7.79 us
where the time goes in v7:
time: 166 us; the launch traced here: 165 us
  starting transfers between devices  64 us (39%)
  waiting for transfers between devices  36 us (22%)
  Pallas kernels  21.4 us (13%)
  blocking collectives  20.7 us (12%)
  between operations  14.2 us (9%)
  local copies, waits for them, and re-layouts  7.79 us (5%)
    all_to_all x4, starting transfers between devices, exchange(): return lax.all_to_all(value, axes, 0, 0, tiled=True)  25.6 us
    all_to_all x1, blocking collectives, exchange(): return lax.all_to_all(value, axes, 0, 0, tiled=True)  20.7 us
    ppermute x6, starting transfers between devices, swap(): return lax.ppermute(value, axis, [(0, 1), (1, 0)])  19.3 us
    all_to_all x4, waiting for transfers between devices, exchange(): return lax.all_to_all(value, axes, 0, 0, tiled=True)  17.1 us
    pallas_call x7, Pallas kernels, call(): pl.pallas_call(kernel, out_shape=outs, in_specs=[SMEM] * tables + [VMEM]...  15.3 us
    ppermute x6, waiting for transfers between devices, swap(): return lax.ppermute(value, axis, [(0, 1), (1, 0)])  14.2 us
    ppermute x1, starting transfers between devices, transpose(): lax.ppermute(high, plane, pairs[1])  10.3 us
    unnamed x30, local copies, waits for them, and re-layouts  7.79 us
  transfers between devices with their start and end apart: 15, of which 6 were waited for; matrix products, arithmetic and copies ran while one was open for 0% of the time, Pallas kernels for 10%

profile of v7, /device:TPU:1, one launch (start us, length us, event | category | flops | bytes accessed | tf_op | source)
XLA Modules:
  0.0 164.8 jit_solution(8961365640378526860)
XLA Ops:
  7.2 2.5 %shard_map.165 = (bf16[8,3,64,128]{3,2,1,0:T(8,128)(2,1)}, bf16[8,3,256,128]{3,2,1,0:T(8,128)(2,1)}, bf16[3,128,128]{2,1,0:T(8,128)(2,1)}, bf16[3,128,128]{2,1,0:T(8,128)(2,1)}) custom-call(bf16[1,64,128]{2,1,0:T(8,128)(2,1)} %leaf.3, bf16[2,64,128]{2,1,0:T(8,128)(2,1)} %mid.3, bf16[64,128]{1,0:T(8,128)(2,1)} %root.1, bf16[256,128]{1,0:T(8,128)(2,1)} %leaf_panel.1, ...), custom_call_target="tpu_custom_call" | custom-call | tf_op jit(solution)/shard_map/pallas_call | solution.py:25
  9.7 5.9 %all-to-all-start = ((bf16[8,3,64,128]{3,2,1,0:T(8,128)(2,1)}), bf16[8,3,64,128]{3,2,1,0:T(8,128)(2,1)S(1)}, u32[]{:S(2)}, u32[]{:S(2)}) async-start(bf16[8,3,64,128]{3,2,1,0:T(8,128)(2,1)} %get-tuple-element.27), calls=%async_computation | async-start | bytes 786432 | tf_op jit(solution)/shard_map/all_to_all | solution.py:249
  15.6 6.2 %collective-permute-start = (bf16[3,128,128]{2,1,0:T(8,128)(2,1)}, bf16[3,128,128]{2,1,0:T(8,128)(2,1)S(1)}, u32[]{:S(2)}, u32[]{:S(2)}) collective-permute-start(bf16[3,128,128]{2,1,0:T(8,128)(2,1)} %get-tuple-element.28), channel_id=1, source_target_pairs={{0,0},{1,16},{2,32},{3,48},{4,64},{5,80},{6,96},{7,112},{8,17},{9,... | collective-permute-start | bytes 294920 | tf_op jit(solution)/shard_map/ppermute | solution.py:245
  21.8 10.3 %collective-permute-start.1 = (bf16[3,128,128]{2,1,0:T(8,128)(2,1)}, bf16[3,128,128]{2,1,0:T(8,128)(2,1)S(1)}, u32[]{:S(2)}, u32[]{:S(2)}) collective-permute-start(bf16[3,128,128]{2,1,0:T(8,128)(2,1)} %get-tuple-element.29), channel_id=1, source_target_pairs={{0,8},{1,24},{2,40},{3,56},{4,72},{5,88},{6,104},{7,120},{8,25},{9... | collective-permute-start | bytes 294920 | tf_op jit(solution)/shard_map/ppermute | solution.py:245
  32.2 1.9 %collective-permute-done.1.high = bf16[3,128,128]{2,1,0:T(8,128)(2,1)S(1)} collective-permute-done((bf16[3,128,128]{2,1,0:T(8,128)(2,1)}, bf16[3,128,128]{2,1,0:T(8,128)(2,1)S(1)}, u32[]{:S(2)}, u32[]{:S(2)}) %collective-permute-start.1) | collective-permute-done | bytes 98336 | tf_op jit(solution)/shard_map/ppermute | solution.py:245
  34.9 7.4 %all-to-all-start.1 = ((bf16[8,3,256,128]{3,2,1,0:T(8,128)(2,1)}), bf16[8,3,256,128]{3,2,1,0:T(8,128)(2,1)S(1)}, u32[]{:S(2)}, u32[]{:S(2)}) async-start(bf16[8,3,256,128]{3,2,1,0:T(8,128)(2,1)} %get-tuple-element.37), calls=%async_computation.1 | async-start | bytes 3145728 | tf_op jit(solution)/shard_map/all_to_all | solution.py:249
  42.4 4.3 %collective-permute-start.2 = (bf16[2,128,128]{2,1,0:T(8,128)(2,1)S(1)}, bf16[2,128,128]{2,1,0:T(8,128)(2,1)S(1)}, u32[]{:S(2)}, u32[]{:S(2)}) collective-permute-start(bf16[2,128,128]{2,1,0:T(8,128)(2,1)S(1)} %get-tuple-element.34), channel_id=1, source_target_pairs={{0,128},{128,0},{1,129},{129,1},{2,130},{130,2},{3,131},{131,3},{4... | collective-permute-start | bytes 196616 | tf_op jit(solution)/shard_map/ppermute | solution.py:235
  46.8 4.8 %collective-permute-start.3 = (bf16[128,128]{1,0:T(8,128)(2,1)S(1)}, bf16[128,128]{1,0:T(8,128)(2,1)S(1)}, u32[]{:S(2)}, u32[]{:S(2)}) collective-permute-start(bf16[128,128]{1,0:T(8,128)(2,1)S(1)} %get-tuple-element.35), channel_id=1, source_target_pairs={{0,256},{256,0},{1,257},{257,1},{2,258},{258,2},{3,259},{259,3},{4... | collective-permute-start | bytes 98312 | tf_op jit(solution)/shard_map/ppermute | solution.py:235
  51.5 2.4 %collective-permute-start.4 = (bf16[128,128]{1,0:T(8,128)(2,1)S(1)}, bf16[128,128]{1,0:T(8,128)(2,1)S(1)}, u32[]{:S(2)}, u32[]{:S(2)}) collective-permute-start(bf16[128,128]{1,0:T(8,128)(2,1)S(1)} %get-tuple-element.35), channel_id=1, source_target_pairs={{0,384},{128,256},{256,128},{384,0},{1,385},{129,257},{257,129},{3... | collective-permute-start | bytes 98312 | tf_op jit(solution)/shard_map/ppermute | solution.py:289
  53.9 13.3 %collective-permute-done.3.across = bf16[128,128]{1,0:T(8,128)(2,1)S(1)} collective-permute-done((bf16[128,128]{1,0:T(8,128)(2,1)S(1)}, bf16[128,128]{1,0:T(8,128)(2,1)S(1)}, u32[]{:S(2)}, u32[]{:S(2)}) %collective-permute-start.3) | collective-permute-done | bytes 32800 | tf_op jit(solution)/shard_map/ppermute | solution.py:235
  67.2 0.8 shard_map.167
  68.0 0.9 copy-done.2
  69.0 3.6 %collective-permute-start.5 = (bf16[8,3,256,128]{3,2,1,0:T(8,128)(2,1)S(1)}, bf16[8,3,256,128]{3,2,1,0:T(8,128)(2,1)}, u32[]{:S(2)}, u32[]{:S(2)}) collective-permute-start(bf16[8,3,256,128]{3,2,1,0:T(8,128)(2,1)S(1)} %all-to-all-done.1._.far_own.panels), channel_id=1, source_target_pairs={{0,8},{8,0},{1,9},{9,1},{2,10},{10,2},{3,11},{11,3},{4,12},{12,4},... | collective-permute-start | bytes 4718600 | tf_op jit(solution)/shard_map/ppermute | solution.py:235
  72.6 0.8 shard_map.168
  73.4 1.9 %collective-permute-start.6 = (f32[3,256,128]{2,1,0:T(8,128)}, f32[3,256,128]{2,1,0:T(8,128)S(1)}, u32[]{:S(2)}, u32[]{:S(2)}) collective-permute-start(f32[3,256,128]{2,1,0:T(8,128)} %shard_map.168), channel_id=1, source_target_pairs={{0,8},{8,0},{1,9},{9,1},{2,10},{10,2},{3,11},{11,3},{4,12},{12,4},... | collective-permute-start | bytes 1179656 | tf_op jit(solution)/shard_map/ppermute | solution.py:235
  75.3 4.8 %all-to-all-start.2 = ((bf16[8,3,128,128]{3,2,1,0:T(8,128)(2,1)}), bf16[8,3,128,128]{3,2,1,0:T(8,128)(2,1)S(1)}, u32[]{:S(2)}, u32[]{:S(2)}) async-start(bf16[8,3,128,128]{3,2,1,0:T(8,128)(2,1)} %copy-done.2), calls=%async_computation.2 | async-start | bytes 1572864 | tf_op jit(solution)/shard_map/all_to_all | solution.py:249
  80.1 2.8 %all-gather.5.cloned.1.call-done = bf16[32,64,1024]{2,1,0:T(8,128)(2,1)} async-done(((bf16[2,64,1024]{2,1,0:T(8,128)(2,1)}), bf16[32,64,1024]{2,1,0:T(8,128)(2,1)}) %all-gather.5.cloned.1.call-update) | async-done | bytes 4194320 | tf_op jit(solution)/shard_map/all_gather | solution.py:286
  82.9 2.2 %copy-done.10 = bf16[32,64,1024]{2,1,0:T(8,128)(2,1)S(1)} copy-done((bf16[32,64,1024]{2,1,0:T(8,128)(2,1)S(1)}, bf16[32,64,1024]{2,1,0:T(8,128)(2,1)}, u32[]{:S(2)}) %copy-start.10) | copy-done | bytes 4194328
  85.1 5.6 %shard_map.169 = (bf16[512,1024]{1,0:T(8,128)(2,1)}, bf16[256,128]{1,0:T(8,128)(2,1)S(1)}, bf16[256,128]{1,0:T(8,128)(2,1)S(1)}) custom-call(s32[4,16]{1,0:T(4,128)S(1)} %copy-done.5, s32[2,32]{1,0:T(2,128)S(1)} %copy-done.7, bf16[16,2,64,1024]{3,2,1,0:T(8,128)(2,1)S(1)} %bitcast.5, bf16[8,3,256,128]{3,2,1,0:T(8,128)(2,1)S(1)} %all-to-all-done.1._.far_own.panels, ...), custom_call_target="tpu_custom_call" | custom-call | flops 2147483648 | bytes 4194304 | tf_op jit(solution)/shard_map/pallas_call | solution.py:25
  92.0 2.3 %collective-permute-start.8 = (bf16[512,1024]{1,0:T(8,128)(2,1)}, bf16[512,1024]{1,0:T(8,128)(2,1)}, u32[]{:S(2)}, u32[]{:S(2)}) collective-permute-start(bf16[512,1024]{1,0:T(8,128)(2,1)} %get-tuple-element.46.turned), channel_id=1, source_target_pairs={{0,8},{8,0},{1,9},{9,1},{2,10},{10,2},{3,11},{11,3},{4,12},{12,4},... | collective-permute-start | bytes 3145736 | tf_op jit(solution)/shard_map/ppermute | solution.py:235
  94.3 9.5 %all-to-all-done.2.blocks = bf16[8,3,128,128]{3,2,1,0:T(8,128)(2,1)S(1)} async-done(((bf16[8,3,128,128]{3,2,1,0:T(8,128)(2,1)}), bf16[8,3,128,128]{3,2,1,0:T(8,128)(2,1)S(1)}, u32[]{:S(2)}, u32[]{:S(2)}) %all-to-all-start.2) | async-done | bytes 786464 | tf_op jit(solution)/shard_map/all_to_all | solution.py:249
  103.8 2.7 %shard_map.171 = bf16[32,2,3,8,128]{4,3,2,1,0:T(8,128)(2,1)S(1)} custom-call(s32[4,16]{1,0:T(4,128)S(1)} %copy-done.5, s32[2,32]{1,0:T(2,128)S(1)} %copy-done.7, bf16[512,1024]{1,0:T(8,128)(2,1)} %get-tuple-element.46.turned, bf16[512,1024]{1,0:T(8,128)(2,1)} %collective-permute-done.8.other_turned, bf16[8,3,128,128]{3,2,1,0:T(8,128)(2,1)S(1)} %all-to-all-done.2.blocks, ...), custom_call_target="tpu_custom_call" | custom-call | tf_op jit(solution)/shard_map/pallas_call | solution.py:25
  106.5 20.7 %all_to_all.25.pieces = bf16[32,2,3,8,128]{4,3,2,1,0:T(8,128)(2,1)S(1)} all-to-all(bf16[32,2,3,8,128]{4,3,2,1,0:T(8,128)(2,1)S(1)} %shard_map.171), channel_id=1, replica_groups=mesh['pair'=2,'half'=2,'z'=8,'core'=2,'ylo'=2,'x'=4] {'pair','half','z'}, dimensions={0} | all-to-all | bytes 786432 | tf_op jit(solution)/shard_map/all_to_all | solution.py:249
  127.2 2.2 %shard_map.172 = bf16[64,4,8,128]{3,2,1,0:T(8,128)(2,1)} custom-call(s32[4,16]{1,0:T(4,128)S(1)} %copy-done.6, s32[2,32]{1,0:T(2,128)S(1)} %copy-done.8, bf16[32,2,3,8,128]{4,3,2,1,0:T(8,128)(2,1)S(1)} %all_to_all.25.pieces), custom_call_target="tpu_custom_call" | custom-call | tf_op jit(solution)/shard_map/pallas_call | solution.py:25
  129.4 7.5 %all-to-all-start.4 = ((bf16[64,4,8,128]{3,2,1,0:T(8,128)(2,1)}), bf16[64,4,8,128]{3,2,1,0:T(8,128)(2,1)S(1)}, u32[]{:S(2)}, u32[]{:S(2)}) async-start(bf16[64,4,8,128]{3,2,1,0:T(8,128)(2,1)} %shard_map.172), calls=%async_computation.4 | async-start | bytes 1048576 | tf_op jit(solution)/shard_map/all_to_all | solution.py:249
  136.9 2.4 %collective-permute-start.7 = (bf16[256,128]{1,0:T(8,128)(2,1)S(1)}, bf16[256,128]{1,0:T(8,128)(2,1)S(1)}, u32[]{:S(2)}, u32[]{:S(2)}) collective-permute-start(bf16[256,128]{1,0:T(8,128)(2,1)S(1)} %copy-done.13), channel_id=1, source_target_pairs={{0,8},{8,0},{1,9},{9,1},{2,10},{10,2},{3,11},{11,3},{4,12},{12,4},... | collective-permute-start | bytes 196616 | tf_op jit(solution)/shard_map/ppermute | solution.py:235
  139.3 0.9 collective-permute-done.7
  140.8 2.2 %copy-done.9 = bf16[256,64,128]{2,1,0:T(8,128)(2,1)S(1)} copy-done((bf16[256,64,128]{2,1,0:T(8,128)(2,1)S(1)}, bf16[256,64,128]{2,1,0:T(8,128)(2,1)}, u32[]{:S(2)}) %copy-start.9) | copy-done | bytes 4194328
  143.0 1.2 copy-done.11
  144.3 4.4 %shard_map.170 = (f32[256,1024]{1,0:T(8,128)S(1)}, bf16[256,128]{1,0:T(8,128)(2,1)}) custom-call(s32[64]{0:T(128)S(1)} %copy-done.14, bf16[8,3,256,128]{3,2,1,0:T(8,128)(2,1)S(1)} %all-to-all-done.1._.far_own.panels, bf16[16,16,64,128]{3,2,1,0:T(8,128)(2,1)S(1)} %bitcast.4, f32[256,1024]{1,0:T(8,128)S(1)} %copy-done.11), custom_call_target="tpu_custom_call" | custom-call | flops 4294967296 | bytes 8388608 | tf_op jit(solution)/shard_map/pallas_call | solution.py:344
  148.7 7.6 %all-to-all-done.4 = bf16[64,4,8,128]{3,2,1,0:T(8,128)(2,1)S(1)} async-done(((bf16[64,4,8,128]{3,2,1,0:T(8,128)(2,1)}), bf16[64,4,8,128]{3,2,1,0:T(8,128)(2,1)S(1)}, u32[]{:S(2)}, u32[]{:S(2)}) %all-to-all-start.4) | async-done | bytes 524320 | tf_op jit(solution)/shard_map/all_to_all | solution.py:249
  156.3 1.7 %shard_map.173 = f32[256,1024]{1,0:T(8,128)} custom-call(f32[256,1024]{1,0:T(8,128)S(1)} %get-tuple-element.45.base, bf16[32,2,4,8,128]{4,3,2,1,0:T(8,128)(2,1)S(1)} %bitcast.3), custom_call_target="tpu_custom_call" | custom-call | tf_op jit(solution)/shard_map/pallas_call | solution.py:364
  (41 shorter events, 2.9 us)
Async XLA Ops:
  9.7 24.4 %all-to-all-start = ((bf16[8,3,64,128]{3,2,1,0:T(8,128)(2,1)}), bf16[8,3,64,128]{3,2,1,0:T(8,128)(2,1)S(1)}, u32[]{:S(2)}, u32[]{:S(2)}) async-start(bf16[8,3,64,128]{3,2,1,0:T(8,128)(2,1)} %get-tuple-element.27), calls=%async_computation | async-start | bytes 786432 | tf_op jit(solution)/shard_map/all_to_all | solution.py:249
  15.5 67.4 %all-gather.5.cloned.1.call-start = ((), (), s32[]{:S(2)}) async-start(), calls=%async_computation.5 | async-start | bytes 4456448 | tf_op jit(solution)/shard_map/all_gather | solution.py:286
  15.6 16.6 %collective-permute-start = (bf16[3,128,128]{2,1,0:T(8,128)(2,1)}, bf16[3,128,128]{2,1,0:T(8,128)(2,1)S(1)}, u32[]{:S(2)}, u32[]{:S(2)}) collective-permute-start(bf16[3,128,128]{2,1,0:T(8,128)(2,1)} %get-tuple-element.28), channel_id=1, source_target_pairs={{0,0},{1,16},{2,32},{3,48},{4,64},{5,80},{6,96},{7,112},{8,17},{9,... | collective-permute-start | bytes 294920 | tf_op jit(solution)/shard_map/ppermute | solution.py:245
  21.8 12.3 %collective-permute-start.1 = (bf16[3,128,128]{2,1,0:T(8,128)(2,1)}, bf16[3,128,128]{2,1,0:T(8,128)(2,1)S(1)}, u32[]{:S(2)}, u32[]{:S(2)}) collective-permute-start(bf16[3,128,128]{2,1,0:T(8,128)(2,1)} %get-tuple-element.29), channel_id=1, source_target_pairs={{0,8},{1,24},{2,40},{3,56},{4,72},{5,88},{6,104},{7,120},{8,25},{9... | collective-permute-start | bytes 294920 | tf_op jit(solution)/shard_map/ppermute | solution.py:245
  34.9 32.3 %all-to-all-start.1 = ((bf16[8,3,256,128]{3,2,1,0:T(8,128)(2,1)}), bf16[8,3,256,128]{3,2,1,0:T(8,128)(2,1)S(1)}, u32[]{:S(2)}, u32[]{:S(2)}) async-start(bf16[8,3,256,128]{3,2,1,0:T(8,128)(2,1)} %get-tuple-element.37), calls=%async_computation.1 | async-start | bytes 3145728 | tf_op jit(solution)/shard_map/all_to_all | solution.py:249
  42.3 30.3 %copy-start = (f32[256,512]{1,0:T(8,128)S(1)}, f32[256,512]{1,0:T(8,128)}, u32[]{:S(2)}) copy-start(f32[256,512]{1,0:T(8,128)} %mid.5) | copy-start | bytes 1572868
  42.3 30.3 %copy-start.1 = (f32[256,256]{1,0:T(8,128)S(1)}, f32[256,256]{1,0:T(8,128)}, u32[]{:S(2)}) copy-start(f32[256,256]{1,0:T(8,128)} %leaf.5) | copy-start | bytes 786436
  42.4 98.5 %all-gather.7.cloned.1.call-start = ((), (), s32[]{:S(2)}) async-start(), calls=%async_computation.6 | async-start | bytes 4456448 | tf_op jit(solution)/shard_map/all_gather | solution.py:298
  42.4 24.8 %collective-permute-start.2 = (bf16[2,128,128]{2,1,0:T(8,128)(2,1)S(1)}, bf16[2,128,128]{2,1,0:T(8,128)(2,1)S(1)}, u32[]{:S(2)}, u32[]{:S(2)}) collective-permute-start(bf16[2,128,128]{2,1,0:T(8,128)(2,1)S(1)} %get-tuple-element.34), channel_id=1, source_target_pairs={{0,128},{128,0},{1,129},{129,1},{2,130},{130,2},{3,131},{131,3},{4... | collective-permute-start | bytes 196616 | tf_op jit(solution)/shard_map/ppermute | solution.py:235
  46.8 20.4 %collective-permute-start.3 = (bf16[128,128]{1,0:T(8,128)(2,1)S(1)}, bf16[128,128]{1,0:T(8,128)(2,1)S(1)}, u32[]{:S(2)}, u32[]{:S(2)}) collective-permute-start(bf16[128,128]{1,0:T(8,128)(2,1)S(1)} %get-tuple-element.35), channel_id=1, source_target_pairs={{0,256},{256,0},{1,257},{257,1},{2,258},{258,2},{3,259},{259,3},{4... | collective-permute-start | bytes 98312 | tf_op jit(solution)/shard_map/ppermute | solution.py:235
  51.5 15.7 %collective-permute-start.4 = (bf16[128,128]{1,0:T(8,128)(2,1)S(1)}, bf16[128,128]{1,0:T(8,128)(2,1)S(1)}, u32[]{:S(2)}, u32[]{:S(2)}) collective-permute-start(bf16[128,128]{1,0:T(8,128)(2,1)S(1)} %get-tuple-element.35), channel_id=1, source_target_pairs={{0,384},{128,256},{256,128},{384,0},{1,385},{129,257},{257,129},{3... | collective-permute-start | bytes 98312 | tf_op jit(solution)/shard_map/ppermute | solution.py:289
  68.0 0.9 copy-start.2
  68.9 14.0 %copy-start.5 = (s32[4,16]{1,0:T(4,128)S(1)}, s32[4,16]{1,0:T(4,128)}, u32[]{:S(2)}) copy-start(s32[4,16]{1,0:T(4,128)} %leaf_fill.3) | copy-start | bytes 772
  68.9 14.0 %copy-start.7 = (s32[2,32]{1,0:T(2,128)S(1)}, s32[2,32]{1,0:T(2,128)}, u32[]{:S(2)}) copy-start(s32[2,32]{1,0:T(2,128)} %mid_fill.3) | copy-start | bytes 772
  69.0 11.2 %collective-permute-start.5 = (bf16[8,3,256,128]{3,2,1,0:T(8,128)(2,1)S(1)}, bf16[8,3,256,128]{3,2,1,0:T(8,128)(2,1)}, u32[]{:S(2)}, u32[]{:S(2)}) collective-permute-start(bf16[8,3,256,128]{3,2,1,0:T(8,128)(2,1)S(1)} %all-to-all-done.1._.far_own.panels), channel_id=1, source_target_pairs={{0,8},{8,0},{1,9},{9,1},{2,10},{10,2},{3,11},{11,3},{4,12},{12,4},... | collective-permute-start | bytes 4718600 | tf_op jit(solution)/shard_map/ppermute | solution.py:235
  73.4 6.7 %collective-permute-start.6 = (f32[3,256,128]{2,1,0:T(8,128)}, f32[3,256,128]{2,1,0:T(8,128)S(1)}, u32[]{:S(2)}, u32[]{:S(2)}) collective-permute-start(f32[3,256,128]{2,1,0:T(8,128)} %shard_map.168), channel_id=1, source_target_pairs={{0,8},{8,0},{1,9},{9,1},{2,10},{10,2},{3,11},{11,3},{4,12},{12,4},... | collective-permute-start | bytes 1179656 | tf_op jit(solution)/shard_map/ppermute | solution.py:235
  75.3 28.4 %all-to-all-start.2 = ((bf16[8,3,128,128]{3,2,1,0:T(8,128)(2,1)}), bf16[8,3,128,128]{3,2,1,0:T(8,128)(2,1)S(1)}, u32[]{:S(2)}, u32[]{:S(2)}) async-start(bf16[8,3,128,128]{3,2,1,0:T(8,128)(2,1)} %copy-done.2), calls=%async_computation.2 | async-start | bytes 1572864 | tf_op jit(solution)/shard_map/all_to_all | solution.py:249
  82.9 2.2 %copy-start.10 = (bf16[32,64,1024]{2,1,0:T(8,128)(2,1)S(1)}, bf16[32,64,1024]{2,1,0:T(8,128)(2,1)}, u32[]{:S(2)}) copy-start(bf16[32,64,1024]{2,1,0:T(8,128)(2,1)} %all-gather.5.cloned.1.call-done) | copy-start | bytes 12582916
  90.7 0.6 copy-start.3
  91.4 0.6 copy-start.12
  92.0 35.2 %copy-start.6 = (s32[4,16]{1,0:T(4,128)S(1)}, s32[4,16]{1,0:T(4,128)}, u32[]{:S(2)}) copy-start(s32[4,16]{1,0:T(4,128)} %leaf_map.1) | copy-start | bytes 772
  92.0 35.2 %copy-start.8 = (s32[2,32]{1,0:T(2,128)S(1)}, s32[2,32]{1,0:T(2,128)}, u32[]{:S(2)}) copy-start(s32[2,32]{1,0:T(2,128)} %mid_map.1) | copy-start | bytes 772
  92.0 11.8 %collective-permute-start.8 = (bf16[512,1024]{1,0:T(8,128)(2,1)}, bf16[512,1024]{1,0:T(8,128)(2,1)}, u32[]{:S(2)}, u32[]{:S(2)}) collective-permute-start(bf16[512,1024]{1,0:T(8,128)(2,1)} %get-tuple-element.46.turned), channel_id=1, source_target_pairs={{0,8},{8,0},{1,9},{9,1},{2,10},{10,2},{3,11},{11,3},{4,12},{12,4},... | collective-permute-start | bytes 3145736 | tf_op jit(solution)/shard_map/ppermute | solution.py:235
  106.5 30.4 %copy-start.13 = (bf16[256,128]{1,0:T(8,128)(2,1)S(1)}, bf16[256,128]{1,0:T(8,128)(2,1)}, u32[]{:S(2)}) copy-start(bf16[256,128]{1,0:T(8,128)(2,1)} %copy-done.12) | copy-start | bytes 196612
  106.5 33.7 %copy-start.4 = (bf16[256,128]{1,0:T(8,128)(2,1)S(1)}, bf16[256,128]{1,0:T(8,128)(2,1)}, u32[]{:S(2)}) copy-start(bf16[256,128]{1,0:T(8,128)(2,1)} %copy-done.3) | copy-start | bytes 196612
  106.5 34.4 %copy-start.14 = (s32[64]{0:T(128)S(1)}, s32[64]{0:T(128)}, u32[]{:S(2)}) copy-start(s32[64]{0:T(128)} %fill.1) | copy-start | bytes 772
  129.4 26.9 %all-to-all-start.4 = ((bf16[64,4,8,128]{3,2,1,0:T(8,128)(2,1)}), bf16[64,4,8,128]{3,2,1,0:T(8,128)(2,1)S(1)}, u32[]{:S(2)}, u32[]{:S(2)}) async-start(bf16[64,4,8,128]{3,2,1,0:T(8,128)(2,1)} %shard_map.172), calls=%async_computation.4 | async-start | bytes 1048576 | tf_op jit(solution)/shard_map/all_to_all | solution.py:249
  136.9 3.3 %collective-permute-start.7 = (bf16[256,128]{1,0:T(8,128)(2,1)S(1)}, bf16[256,128]{1,0:T(8,128)(2,1)S(1)}, u32[]{:S(2)}, u32[]{:S(2)}) collective-permute-start(bf16[256,128]{1,0:T(8,128)(2,1)S(1)} %copy-done.13), channel_id=1, source_target_pairs={{0,8},{8,0},{1,9},{9,1},{2,10},{10,2},{3,11},{11,3},{4,12},{12,4},... | collective-permute-start | bytes 196616 | tf_op jit(solution)/shard_map/ppermute | solution.py:235
  140.8 2.2 %copy-start.9 = (bf16[256,64,128]{2,1,0:T(8,128)(2,1)S(1)}, bf16[256,64,128]{2,1,0:T(8,128)(2,1)}, u32[]{:S(2)}) copy-start(bf16[256,64,128]{2,1,0:T(8,128)(2,1)} %all-gather.7.cloned.1.call-done) | copy-start | bytes 12582916
  143.0 1.2 copy-start.11
Sparse Core Ops, SparseCore 0:
  35.0 47.8 all-gather.4
  85.1 52.5 all-gather.6
